TPU v7x, 32 devices: a whole 2x2x4 slice. The times are simulated.
32 devices in a mesh: src: 8 (over y, x, core), freq: 4 (over z).
Axes of the slice: x: 2, y: 2, z: 4, core: 2. Of those that a mesh axis runs over, the one named last changes fastest.
Arguments:
- receivers: bfloat16 [4, 8, 2, 256, 512], P('freq', 'src'), may hold values from -6 to 6
- data: bfloat16 [4, 2, 4096, 1024], P('freq', None, None, 'src'), may hold values from -0.0625 to 0.0625
- block_of_slot: int32 [8], replicated, may hold values from 0 to 7, each once
- receiver_order: int32 [256], replicated, may hold values from 0 to 255, each once
Outputs:
- traces: bfloat16 [256, 1024, 256], P('freq', 'src')
Inputs may be any that keep to these rules, and one draw needn't show every extreme that they name: `block_of_slot`: each of the 8 bounce blocks is held in exactly one slot. `receiver_order`: each receiver appears in exactly one trace row.
All inputs are finite; a program needn't handle non-finite values.
Results may differ from a plain program's by a relative error of at most 0.0049.
Values may be sent and summed in bfloat16 or wider, within the bound.
No kernel may reach another device: no remote copies, remote signals or barrier semaphores. Data moves between devices by JAX's collectives and lax.ppermute only.
A program may use at most 64 MiB of HBM per device.

v0:
```python
import math

import jax
import jax.numpy as jnp
from jax import lax
from jax.sharding import PartitionSpec as P

NT = 256


def multiply(acc, piece, block, data):
    width = piece.shape[3]
    rows = lax.dynamic_slice_in_dim(data, block * width, width, 2)
    g_re, g_im = (piece[:, 0], piece[:, 1])
    d_re, d_im = (rows[:, 0], rows[:, 1])
    real = jnp.einsum("frk,fks->frs", g_re, d_re, preferred_element_type=jnp.float32) - jnp.einsum(
        "frk,fks->frs", g_im, d_im, preferred_element_type=jnp.float32
    )
    imag = jnp.einsum("frk,fks->frs", g_re, d_im, preferred_element_type=jnp.float32) + jnp.einsum(
        "frk,fks->frs", g_im, d_re, preferred_element_type=jnp.float32
    )
    return acc + jnp.stack([real, imag], 1)


def transform(moved):
    high = lax.Precision.HIGHEST
    count = moved.shape[0]
    spectra = moved.astype(jnp.float32)
    times = jnp.arange(NT, dtype=jnp.int32)
    bins = (2 * jnp.arange(count, dtype=jnp.int32) + 1) * (NT // (4 * count))
    phase = bins[:, None] * times[None, :] % NT
    angle = phase.astype(jnp.float32) * (2.0 * math.pi / NT)
    cosine = jnp.cos(angle)
    sine = jnp.sin(angle)
    value = jnp.einsum("frs,ft->rst", spectra[:, 0], cosine, precision=high) - jnp.einsum(
        "frs,ft->rst", spectra[:, 1], sine, precision=high
    )
    return (value * count ** (-0.5)).astype(jnp.bfloat16)


def body(receivers, data, block_of_slot, receiver_order):
    start = jnp.zeros((receivers.shape[0], 2, receivers.shape[3], data.shape[3]), jnp.float32)
    piece = lax.all_gather(receivers, "src", axis=1, tiled=True)

    def inner(index, acc):
        single = lax.dynamic_index_in_dim(piece, index, 1, keepdims=False)
        return multiply(acc, single, block_of_slot[index], data)

    acc = lax.fori_loop(0, piece.shape[1], inner, start)
    spectra = acc.astype(jnp.bfloat16)
    ordered = jnp.take(spectra, receiver_order, axis=2)
    return transform(lax.all_to_all(ordered, "freq", split_axis=2, concat_axis=0, tiled=True))


def solution(mesh):
    placed = (P("freq", "src", None, None, None), P("freq", None, None, "src"), P(), P())
    return jax.shard_map(
        body, mesh=mesh, in_specs=placed, out_specs=P("freq", "src", None), check_vma=False
    )
```

profile of v0, /device:TPU:0, one launch (start us, length us, event | category | flops | bytes accessed | tf_op | source)
XLA Modules:
  0.0 138.1 jit_solution(292602120018596496)
XLA Ops:
  8.6 40.0 %all-gather.2.cloned.1.call-done = bf16[1,8,2,256,512]{4,3,2,0,1:T(8,128)(2,1)} async-done(((bf16[1,1,2,256,512]{4,3,2,0,1:T(8,128)(2,1)}), bf16[1,8,2,256,512]{4,3,2,0,1:T(8,128)(2,1)}) %all-gather.2.cloned.1.call-update) | async-done | bytes 4194320 | tf_op jit(solution)/shard_map/all_gather | solution.py:43
  48.7 60.7 %while.14 = (s32[]{:T(128)}, f32[1,2,256,128]{3,2,1,0:T(8,128)S(1)}, bf16[1,8,2,256,512]{4,3,2,1,0:T(8,128)(2,1)}, s32[8]{0:T(128)}, bf16[1,2,4096,128]{3,2,1,0:...) while((s32[]{:T(128)}, f32[1,2,256,128]{3,2,1,0:T(8,128)S(1)}, ...), condition=%wide.region_1.2_spmd.clone, body=%wide.region_0.1_spmd.clone.sunk | while | flops 134479872 | bytes 4194521 | solution.py:49
  48.7 1.3 dynamic_slice.29
  52.8 1.1 fusion.34
  56.3 1.3 dynamic_slice.29
  60.4 1.1 fusion.34
  63.9 1.3 dynamic_slice.29
  68.0 1.1 fusion.34
  70.2 1.1 fusion.32
  71.4 1.3 dynamic_slice.29
  75.6 1.1 fusion.34
  79.0 1.3 dynamic_slice.29
  83.1 1.1 fusion.34
  85.4 1.1 fusion.32
  86.6 1.3 dynamic_slice.29
  90.7 1.1 fusion.34
  94.2 1.3 dynamic_slice.29
  98.3 1.1 fusion.34
  101.8 1.3 dynamic_slice.29
  105.9 1.1 fusion.34
  111.5 4.6 %all-to-all-start = ((bf16[1,2,256,128]{3,1,0,2:T(2,128)(2,1)}), bf16[1,2,256,128]{3,1,0,2:T(2,128)(2,1)S(1)}, u32[]{:S(2)}, u32[]{:S(2)}) async-start(bf16[1,2,256,128]{3,1,0,2:T(2,128)(2,1)} %fusion.8), calls=%async_computation | async-start | bytes 262144 | tf_op jit(solution)/shard_map/all_to_all | solution.py:52
  116.1 6.3 %all-to-all-done = bf16[1,2,256,128]{3,1,0,2:T(2,128)(2,1)S(1)} async-done(((bf16[1,2,256,128]{3,1,0,2:T(2,128)(2,1)}), bf16[1,2,256,128]{3,1,0,2:T(2,128)(2,1)S(1)}, u32[]{:S(2)}, u32[]{:S(2)}) %all-to-all-start) | async-done | bytes 131104 | tf_op jit(solution)/shard_map/all_to_all | solution.py:52
  122.5 3.5 %fusion.9 = f32[64,128,256]{2,1,0:T(8,128)S(1)} fusion(bf16[4,2,64,128]{3,0,2,1:T(4,128)(2,1)S(1)} %bitcast.79, s32[4]{0:T(128)S(1)} %add_multiply_fusion), kind=kOutput, calls=%fused_computation.24 | convolution fusion | flops 100677632 | bytes 8454656 | tf_op jit(solution)/shard_map/frs,ft->rst/dot_general | solution.py:35
  126.1 5.2 %multiply_convert_fusion = bf16[64,128,256]{2,1,0:T(8,128)(2,1)} fusion(f32[64,128,256]{2,1,0:T(8,128)S(1)} %fusion.9, bf16[4,2,64,128]{3,0,2,1:T(4,128)(2,1)S(1)} %bitcast.80, s32[4]{0:T(128)S(1)} %add_multiply_fusion), kind=kOutput, calls=%fused_computation.17 | convolution fusion | flops 106969088 | bytes 12648960 | tf_op jit(solution)/shard_map/frs,ft->rst/dot_general | solution.py:35
  (50 shorter events, 38.2 us)
Async XLA Ops:
  6.5 42.2 %all-gather.2.cloned.1.call-start = ((), (), s32[]{:S(2)}) async-start(), calls=%async_computation.1 | async-start | bytes 4718592 | tf_op jit(solution)/shard_map/all_gather | solution.py:43
  111.5 10.9 %all-to-all-start = ((bf16[1,2,256,128]{3,1,0,2:T(2,128)(2,1)}), bf16[1,2,256,128]{3,1,0,2:T(2,128)(2,1)S(1)}, u32[]{:S(2)}, u32[]{:S(2)}) async-start(bf16[1,2,256,128]{3,1,0,2:T(2,128)(2,1)} %fusion.8), calls=%async_computation | async-start | bytes 262144 | tf_op jit(solution)/shard_map/all_to_all | solution.py:52
Sparse Core Ops, SparseCore 0:
  9.2 39.4 all-gather.1
where the time goes:
time: 139 us; the launch traced here: 138 us
  waiting for transfers between devices  47.1 us (34%)
  matrix products  44.7 us (32%)
  local copies, waits for them, and re-layouts  20 us (14%)
  between operations  13.4 us (10%)
  loops' own time  5.36 us (4%)
  starting transfers between devices  4.6 us (3%)
  other arithmetic  2.99 us (2%)
    all_gather x1, waiting for transfers between devices, body(): piece = lax.all_gather(receivers, 'src', axis=1, tiled=True)  40 us
    dynamic_slice x8, local copies, waits for them, and re-layouts, inner(): return multiply(acc, single, block_of_slot[index], data)  10.2 us
    dot_general x8, matrix products, multiply(): jnp.einsum('frk,fks->frs', g_im, d_im, preferred_element_type=jnp.float32)  8.98 us
    dot_general x8, matrix products, multiply(): jnp.einsum('frk,fks->frs', g_im, d_re, preferred_element_type=jnp.float32)  8.98 us
    dot_general x8, matrix products, multiply(): jnp.einsum('frk,fks->frs', g_re, d_re, preferred_element_type=jnp.float32)  8.97 us
    dot_general x8, matrix products, multiply(): jnp.einsum('frk,fks->frs', g_re, d_im, preferred_element_type=jnp.float32)  8.97 us
    squeeze x8, local copies, waits for them, and re-layouts, inner(): single = lax.dynamic_index_in_dim(piece, index, 1, keepdims=False)  8.66 us
    all_to_all x1, waiting for transfers between devices, body(): lax.all_to_all(ordered, 'freq', split_axis=2, concat_axis=0, tiled=True)  6.33 us
  transfers between devices with their start and end apart: 2, of which 2 were waited for; matrix products, arithmetic and copies ran while one was open for 1% of the time, Pallas kernels for 0%

commit v1 on v0

v1 whole, which is shorter than its diff:
```python
import functools
import math

import jax
import jax.numpy as jnp
import numpy as np
from jax import lax
from jax.experimental import pallas as pl
from jax.experimental.pallas import tpu as pltpu
from jax.sharding import PartitionSpec as P

NT = 256
UNIT = 16
SHARES = (1, 1)
VMEM = pl.BlockSpec(memory_space=pltpu.VMEM)
SMEM = pl.BlockSpec(memory_space=pltpu.SMEM)
ANY = pl.BlockSpec(memory_space=pl.ANY)
PARAMS = pltpu.CompilerParams(vmem_limit_bytes=40 * 2**20)


def cuts_of(quarter):
    units = quarter // UNIT
    total = sum(SHARES)
    edges = [0]
    for i in range(len(SHARES)):
        edges.append(units * sum(SHARES[: i + 1]) // total * UNIT)
    return [(a, b - a) for a, b in zip(edges[:-1], edges[1:]) if b > a]


def order_rows(receivers, receiver_order, nf):
    _, _, two, rows, width = receivers.shape
    quarter = rows // nf
    cuts = cuts_of(quarter)

    def kernel(order_ref, g_ref, *refs):
        outs, hot = refs[:-1], refs[-1]
        z = lax.axis_index("freq")
        wanted = jnp.broadcast_to(order_ref[...], (rows, rows)).T
        lane = lax.broadcasted_iota(jnp.int32, (rows, rows), 1)
        hot[...] = jnp.where(wanted == lane, 1.0, 0.0).astype(jnp.bfloat16)
        for (off, count), out in zip(cuts, outs):
            for step in range(nf):
                at = pl.multiple_of(lax.rem(z + step, nf) * quarter + off, UNIT)
                pick = hot[pl.ds(at, count), :]
                for part in range(two):
                    out[part, step * count : (step + 1) * count, :] = jnp.dot(
                        pick, g_ref[0, 0, part], preferred_element_type=jnp.float32
                    ).astype(jnp.bfloat16)

    return pl.pallas_call(
        kernel,
        out_shape=[jax.ShapeDtypeStruct((two, nf * count, width), jnp.bfloat16) for _, count in cuts],
        in_specs=[VMEM, VMEM],
        out_specs=[VMEM] * len(cuts),
        scratch_shapes=[pltpu.VMEM((rows, rows), jnp.bfloat16)],
        compiler_params=PARAMS,
        name="order_rows",
    )(receiver_order.reshape(1, rows), receivers)


def pick_blocks(data, block_of_slot, width, ns):
    _, two, _, cols = data.shape
    chips = ns // 2

    def kernel(block_ref, data_ref, mine, theirs, sems):
        me = lax.axis_index("src")
        chip, core = me // 2, lax.rem(me, 2)
        copies = []
        for j in range(chips):
            for which, (out, side) in enumerate(((theirs, 1 - core), (mine, core))):
                block = block_ref[jnp.bitwise_xor(chip, j) * 2 + side]
                at = pl.multiple_of(block * width, width)
                copies.append(
                    pltpu.make_async_copy(data_ref.at[0, :, pl.ds(at, width), :], out.at[j], sems.at[which, j])
                )
        for copy in copies:
            copy.start()
        for copy in copies:
            copy.wait()

    shape = jax.ShapeDtypeStruct((chips, two, width, cols), jnp.bfloat16)
    return pl.pallas_call(
        kernel,
        out_shape=[shape, shape],
        in_specs=[SMEM, ANY],
        out_specs=[ANY, ANY],
        scratch_shapes=[pltpu.SemaphoreType.DMA((2, chips))],
        compiler_params=PARAMS,
        name="pick_blocks",
    )(block_of_slot, data)


def accumulate(pieces, mine, theirs, first, sums):
    arrays = []
    plan = []
    for piece in pieces:
        entry = []
        for array, plane in piece:
            if not any(array is other for other in arrays):
                arrays.append(array)
            at = next(i for i, other in enumerate(arrays) if other is array)
            entry.append((at, plane))
        plan.append(entry)
    n = len(arrays)
    chips, two, width, cols = mine.shape
    rows = arrays[0].shape[1]

    def kernel(*refs):
        given, (mine_ref, theirs_ref) = refs[:n], refs[n : n + 2]
        old, new = refs[n + 2 : -2], refs[-2:]
        for side, (d_ref, out) in enumerate(zip((mine_ref, theirs_ref), new)):
            total = old[side][...] if old else None
            for j, ((re_at, re_plane), (im_at, im_plane)) in enumerate(plan):
                d_re, d_im = d_ref[j, 0], d_ref[j, 1]
                for at, plane, rhs in (
                    (re_at, re_plane, (d_re, d_im)),
                    (im_at, im_plane, (-d_im, d_re)),
                ):
                    term = jnp.dot(
                        given[at][plane], jnp.concatenate(rhs, axis=1), preferred_element_type=jnp.float32
                    )
                    total = term if total is None else total + term
            out[...] = total

    count = len(pieces)
    spec = pl.BlockSpec((count, two, width, cols), lambda i: (first // count, 0, 0, 0), memory_space=pltpu.VMEM)
    shape = jax.ShapeDtypeStruct((rows, 2 * cols), jnp.float32)
    return pl.pallas_call(
        kernel,
        grid=(1,),
        out_shape=[shape, shape],
        in_specs=[VMEM] * n + [spec, spec] + [VMEM] * len(sums),
        out_specs=[VMEM, VMEM],
        compiler_params=PARAMS,
        cost_estimate=pl.CostEstimate(
            flops=2 * 2 * count * two * rows * width * 2 * cols,
            bytes_accessed=2 * (n * two * rows * width + 2 * count * two * width * cols),
            transcendentals=0,
        ),
        name="accumulate",
    )(*arrays, mine, theirs, *sums)


def finish(mine, other, nf):
    rows, both = mine.shape
    count, cols = rows // nf, both // 2

    def kernel(a, b, out):
        total = (a[...] + b[...]).astype(jnp.bfloat16)
        for step in range(nf):
            for part in range(2):
                out[step, part] = total[step * count : (step + 1) * count, part * cols : (part + 1) * cols]

    return pl.pallas_call(
        kernel,
        out_shape=jax.ShapeDtypeStruct((nf, 2, count, cols), jnp.bfloat16),
        in_specs=[VMEM, VMEM],
        out_specs=VMEM,
        compiler_params=PARAMS,
        name="finish",
    )(mine, other)


def table_of(nf):
    freqs = (np.arange(nf)[:, None] - np.arange(nf)[None, :]) % nf
    bins = (2 * freqs + 1) * (NT // (4 * nf))
    phase = bins[:, :, None] * np.arange(NT) % NT
    angle = phase * (2.0 * math.pi / NT)
    full = np.stack([np.cos(angle), -np.sin(angle)], 2) * nf**-0.5
    high = full.astype(jnp.bfloat16)
    low = (full - high.astype(np.float64)).astype(jnp.bfloat16)
    both = np.stack([high, low], 1)
    both = np.broadcast_to(both[:, :, :, :, None, :], (nf, 2, nf, 2, UNIT, NT))
    return np.ascontiguousarray(both).reshape(nf, 4 * nf * UNIT, NT)


def transform(table, own, others, off, quarter, out):
    nf, _, count, cols = own.shape
    groups = count // UNIT
    depth = table.shape[0]
    each = 4
    steps = UNIT // each

    def kernel(table_ref, own_ref, *refs):
        given = [own_ref.at[0], *refs[: nf - 1]]
        out_ref, held, sems = refs[-3:]
        lhs = []
        for g in range(groups):
            x = jnp.concatenate([ref[part, g * UNIT : (g + 1) * UNIT, :] for ref in given for part in range(2)], axis=0)
            x = x.T
            lhs.append(jnp.concatenate([x, x], axis=1))
        lhs = jnp.concatenate(lhs, axis=0)
        row = lax.rem(lax.broadcasted_iota(jnp.int32, (depth, NT), 0), UNIT)
        full = table_ref[...]
        copies = []
        for step in range(steps):
            for r in range(step * each, (step + 1) * each):
                rhs = jnp.where(row == r, full, jnp.zeros_like(full))
                res = jnp.dot(lhs, rhs, preferred_element_type=jnp.float32).astype(jnp.bfloat16)
                held[:, r] = res.reshape(groups, cols, NT)
            copy = pltpu.make_async_copy(
                held.at[:, pl.ds(step * each, each)],
                out_ref.at[pl.ds(off // UNIT, groups), pl.ds(step * each, each)],
                sems.at[step],
            )
            copy.start()
            copies.append(copy)
        for copy in copies:
            copy.wait()

    first = out is None
    return pl.pallas_call(
        kernel,
        grid=(1,),
        out_shape=jax.ShapeDtypeStruct((quarter // UNIT, UNIT, cols, NT), jnp.bfloat16),
        in_specs=[VMEM, pl.BlockSpec((1, 2, count, cols), lambda i: (0, 0, 0, 0), memory_space=pltpu.VMEM)]
        + [VMEM] * (nf - 1)
        + ([] if first else [ANY]),
        out_specs=ANY,
        scratch_shapes=[pltpu.VMEM((groups, UNIT, cols, NT), jnp.bfloat16), pltpu.SemaphoreType.DMA((steps,))],
        input_output_aliases={} if first else {nf + 1: 0},
        compiler_params=PARAMS,
        name="transform",
    )(table, own, *others, *([] if first else [out]))


def body(ns, nf, receivers, data, block_of_slot, receiver_order):
    rows, width = receivers.shape[3:]
    chips = ns // 2
    quarter = rows // nf
    cuts = cuts_of(quarter)

    def over(value, flip):
        return lax.ppermute(value, "src", [(i, i ^ flip) for i in range(ns)])

    z = lax.axis_index("freq")
    own = order_rows(receivers, receiver_order, nf)
    near = [(over(v, 2), over(v, 4)) for v in own]
    mine, send = pick_blocks(data, block_of_slot, width, ns)
    theirs = over(send, 1)
    table = lax.dynamic_index_in_dim(jnp.asarray(table_of(nf)), z, 0, keepdims=False)
    out = None
    for (off, count), v, (a, b) in zip(cuts, own, near):
        c = over(b[0:1], 2)
        d = over(a[1:2], 4)
        sums = accumulate([[(v, 0), (v, 1)], [(a, 0), (a, 1)], [(b, 0), (b, 1)]], mine, theirs, 0, ())
        sums = accumulate([[(c, 0), (d, 0)]], mine, theirs, 3, sums)
        total = finish(sums[0], over(sums[1], 1), nf)
        others = [
            lax.ppermute(total[s], "freq", [(i, (i + s) % nf) for i in range(nf)]) for s in range(1, nf)
        ]
        out = transform(table, total, others, off, quarter, out)
    return out.reshape(quarter, *out.shape[2:])


def solution(mesh):
    ns, nf = mesh.shape["src"], mesh.shape["freq"]
    placed = (P("freq", "src", None, None, None), P("freq", None, None, "src"), P(), P())
    return jax.shard_map(
        functools.partial(body, ns, nf), mesh=mesh, in_specs=placed, out_specs=P("freq", "src", None), check_vma=False
    )
```

time: 139 us -> 46.6 us (0.34)
  matrix products: 44.7 us -> 0 us
  waiting for transfers between devices: 47.1 us -> 12.1 us
  starting transfers between devices: 4.6 us -> 21 us
  local copies, waits for them, and re-layouts: 20 us -> 6.25 us
  between operations: 13.4 us -> 0.17 us
  Pallas kernels: 0 us -> 6.84 us
  loops' own time: 5.36 us -> 0 us
  other arithmetic: 2.99 us -> 0 us
    dot_general x34 -> x0, matrix products: 44.7 us -> none  [the longest x8 8.98 us: multiply(): jnp.einsum('frk,fks->frs', g_im, d_im, preferred_element_type=jnp.float32)]
    all_gather x1 -> x0, waiting for transfers between devices: 40 us -> none  [body(): piece = lax.all_gather(receivers, 'src', axis=1, tiled=True)]
    ppermute x0 -> x17, starting transfers between devices: none -> 21 us  [the longest x11 12.4 us: over(): return lax.ppermute(value, 'src', [(i, i ^ flip) for i in range(ns)])]
    ppermute x0 -> x17, waiting for transfers between devices: none -> 12.1 us  [the longest x11 9.14 us: over(): return lax.ppermute(value, 'src', [(i, i ^ flip) for i in range(ns)])]
    dynamic_slice x8 -> x0, local copies, waits for them, and re-layouts: 10.2 us -> none  [inner(): return multiply(acc, single, block_of_slot[index], data)]
    squeeze x8 -> x3, local copies, waits for them, and re-layouts: 8.66 us -> 0.92 us  [the longest x1 0.91 us: body(): lax.dynamic_index_in_dim(jnp.asarray(table_of(nf)), z, 0, keepdims=False)]
    pallas_call x0 -> x10, Pallas kernels: none -> 6.84 us  [the longest x2 3.34 us: transform(): pl.pallas_call(kernel, grid=(1,), out_shape=jax.ShapeDtypeStruct((quarter...]
    all_to_all x1 -> x0, waiting for transfers between devices: 6.33 us -> none  [body(): lax.all_to_all(ordered, 'freq', split_axis=2, concat_axis=0, tiled=True)]
  transfers between devices with their start and end apart: 2 -> 17, of which waited for: 2 -> 6; matrix products, arithmetic and copies ran while one was open for 1% -> 5% of each run, Pallas kernels for 0% -> 9%
where the time goes in v1:
time: 46.6 us; the launch traced here: 46.3 us
  starting transfers between devices  21 us (45%)
  waiting for transfers between devices  12.1 us (26%)
  Pallas kernels  6.84 us (15%)
  local copies, waits for them, and re-layouts  6.25 us (13%)
    ppermute x11, starting transfers between devices, over(): return lax.ppermute(value, 'src', [(i, i ^ flip) for i in range(ns)])  12.4 us
    ppermute x11, waiting for transfers between devices, over(): return lax.ppermute(value, 'src', [(i, i ^ flip) for i in range(ns)])  9.14 us
    ppermute x6, starting transfers between devices, body(): lax.ppermute(total[s], 'freq', [(i, (i + s) % nf) for i in range(nf)])  8.66 us
    unnamed x8, local copies, waits for them, and re-layouts  3.96 us
    pallas_call x2, Pallas kernels, transform(): pl.pallas_call(kernel, grid=(1,), out_shape=jax.ShapeDtypeStruct((quarter...  3.34 us
    ppermute x6, waiting for transfers between devices, body(): lax.ppermute(total[s], 'freq', [(i, (i + s) % nf) for i in range(nf)])  2.92 us
    pallas_call x4, Pallas kernels, accumulate(): pl.pallas_call(kernel, grid=(1,), out_shape=[shape, shape], in_specs=[VME...  1.79 us
  transfers between devices with their start and end apart: 17, of which 6 were waited for; matrix products, arithmetic and copies ran while one was open for 5% of the time, Pallas kernels for 9%

profile of v1, /device:TPU:0, one launch (start us, length us, event | category | flops | bytes accessed | tf_op | source)
XLA Modules:
  0.0 46.3 jit_solution(2968184791257845916)
XLA Ops:
  0.0 1.6 %copy-done = bf16[1,2,4096,128]{3,2,1,0:T(8,128)(2,1)S(1)} copy-done((bf16[1,2,4096,128]{3,2,1,0:T(8,128)(2,1)S(1)}, bf16[1,2,4096,128]{3,2,1,0:T(8,128)(2,1)}, u32[]{:S(2)}) %copy-start) | copy-done | bytes 2097176
  2.2 0.8 %pick_blocks.1 = (bf16[4,2,512,128]{3,2,1,0:T(8,128)(2,1)S(1)}, bf16[4,2,512,128]{3,2,1,0:T(8,128)(2,1)S(1)}) custom-call(s32[8]{0:T(128)S(1)} %copy-done.3, bf16[1,2,4096,128]{3,2,1,0:T(8,128)(2,1)S(1)} %copy-done), custom_call_target="tpu_custom_call" | custom-call | tf_op jit(solution)/shard_map/pick_blocks/pallas_call | solution.py:82
  3.6 1.0 %copy-done.1 = bf16[1,1,2,256,512]{4,3,2,1,0:T(8,128)(2,1)S(1)} copy-done((bf16[1,1,2,256,512]{4,3,2,1,0:T(8,128)(2,1)S(1)}, bf16[1,1,2,256,512]{4,3,2,1,0:T(8,128)(2,1)}, u32[]{:S(2)}) %copy-start.1) | copy-done | bytes 524312
  4.6 0.7 %copy-done.2 = s32[256]{0:T(256)S(1)} copy-done((s32[256]{0:T(256)S(1)}, s32[256]{0:T(256)}, u32[]{:S(2)}) %copy-start.2) | copy-done | bytes 1048
  5.3 0.9 %order_rows.1 = (bf16[2,128,512]{2,1,0:T(8,128)(2,1)S(1)}, bf16[2,128,512]{2,1,0:T(8,128)(2,1)S(1)}) custom-call(s32[1,256]{1,0:T(1,128)S(1)} %bitcast.16, bf16[1,1,2,256,512]{4,3,2,1,0:T(8,128)(2,1)S(1)} %copy-done.1), custom_call_target="tpu_custom_call" | custom-call | tf_op jit(solution)/shard_map/order_rows/pallas_call | solution.py:50
  6.2 2.6 %collective-permute-start.11 = (bf16[2,128,512]{2,1,0:T(8,128)(2,1)S(1)}, bf16[2,128,512]{2,1,0:T(8,128)(2,1)S(1)}, u32[]{:S(2)}, u32[]{:S(2)}) collective-permute-start(bf16[2,128,512]{2,1,0:T(8,128)(2,1)S(1)} %get-tuple-element.24.refs_0_), channel_id=1, source_target_pairs={{0,8},{4,12},{8,0},{12,4},{16,24},{20,28},{24,16},{28,20},{1,9},{5... | collective-permute-start | bytes 786440 | tf_op jit(solution)/shard_map/ppermute | solution.py:234
  8.7 1.5 %collective-permute-start.9 = (bf16[2,128,512]{2,1,0:T(8,128)(2,1)S(1)}, bf16[2,128,512]{2,1,0:T(8,128)(2,1)S(1)}, u32[]{:S(2)}, u32[]{:S(2)}) collective-permute-start(bf16[2,128,512]{2,1,0:T(8,128)(2,1)S(1)} %get-tuple-element.24.refs_0_), channel_id=1, source_target_pairs={{0,16},{4,20},{8,24},{12,28},{16,0},{20,4},{24,8},{28,12},{1,17},{... | collective-permute-start | bytes 786440 | tf_op jit(solution)/shard_map/ppermute | solution.py:234
  10.8 5.0 %collective-permute-done.11.refs_1_ = bf16[2,128,512]{2,1,0:T(8,128)(2,1)S(1)} collective-permute-done((bf16[2,128,512]{2,1,0:T(8,128)(2,1)S(1)}, bf16[2,128,512]{2,1,0:T(8,128)(2,1)S(1)}, u32[]{:S(2)}, u32[]{:S(2)}) %collective-permute-start.11) | collective-permute-done | bytes 262176 | tf_op jit(solution)/shard_map/ppermute | solution.py:234
  15.9 2.0 %collective-permute-start.12 = (bf16[1,128,512]{2,1,0:T(8,128)(2,1)S(1)}, bf16[1,128,512]{2,1,0:T(8,128)(2,1)S(1)}, u32[]{:S(2)}, u32[]{:S(2)}) collective-permute-start(bf16[1,128,512]{2,1,0:T(8,128)(2,1)S(1)} %slice.46), channel_id=1, source_target_pairs={{0,16},{4,20},{8,24},{12,28},{16,0},{20,4},{24,8},{28,12},{1,17},{... | collective-permute-start | bytes 393224 | tf_op jit(solution)/shard_map/ppermute | solution.py:234
  18.0 1.6 %collective-permute-start.10 = (bf16[1,128,512]{2,1,0:T(8,128)(2,1)S(1)}, bf16[1,128,512]{2,1,0:T(8,128)(2,1)S(1)}, u32[]{:S(2)}, u32[]{:S(2)}) collective-permute-start(bf16[1,128,512]{2,1,0:T(8,128)(2,1)S(1)} %slice.45), channel_id=1, source_target_pairs={{0,8},{4,12},{8,0},{12,4},{16,24},{20,28},{24,16},{28,20},{1,9},{5... | collective-permute-start | bytes 393224 | tf_op jit(solution)/shard_map/ppermute | solution.py:234
  19.5 2.0 %collective-permute-done.2.refs_1_ = bf16[2,128,512]{2,1,0:T(8,128)(2,1)S(1)} collective-permute-done((bf16[2,128,512]{2,1,0:T(8,128)(2,1)S(1)}, bf16[2,128,512]{2,1,0:T(8,128)(2,1)S(1)}, u32[]{:S(2)}, u32[]{:S(2)}) %collective-permute-start.2) | collective-permute-done | bytes 262176 | tf_op jit(solution)/shard_map/ppermute | solution.py:234
  21.5 0.7 %slice.41 = bf16[1,128,512]{2,1,0:T(8,128)(2,1)} slice(bf16[2,128,512]{2,1,0:T(8,128)(2,1)S(1)} %collective-permute-done.2.refs_1_), slice={[1:2], [0:128], [0:512]} | slice | bytes 262144 | tf_op jit(solution)/shard_map/slice | solution.py:245
  22.2 2.0 %collective-permute-start.3 = (bf16[1,128,512]{2,1,0:T(8,128)(2,1)}, bf16[1,128,512]{2,1,0:T(8,128)(2,1)S(1)}, u32[]{:S(2)}, u32[]{:S(2)}) collective-permute-start(bf16[1,128,512]{2,1,0:T(8,128)(2,1)} %slice.41), channel_id=1, source_target_pairs={{0,16},{4,20},{8,24},{12,28},{16,0},{20,4},{24,8},{28,12},{1,17},{... | collective-permute-start | bytes 393224 | tf_op jit(solution)/shard_map/ppermute | solution.py:234
  24.8 1.5 %collective-permute-start.1 = (bf16[1,128,512]{2,1,0:T(8,128)(2,1)}, bf16[1,128,512]{2,1,0:T(8,128)(2,1)S(1)}, u32[]{:S(2)}, u32[]{:S(2)}) collective-permute-start(bf16[1,128,512]{2,1,0:T(8,128)(2,1)} %slice.40), channel_id=1, source_target_pairs={{0,8},{4,12},{8,0},{12,4},{16,24},{20,28},{24,16},{28,20},{1,9},{5... | collective-permute-start | bytes 393224 | tf_op jit(solution)/shard_map/ppermute | solution.py:234
  28.4 1.6 %collective-permute-done.1.refs_0_ = bf16[1,128,512]{2,1,0:T(8,128)(2,1)S(1)} collective-permute-done((bf16[1,128,512]{2,1,0:T(8,128)(2,1)}, bf16[1,128,512]{2,1,0:T(8,128)(2,1)S(1)}, u32[]{:S(2)}, u32[]{:S(2)}) %collective-permute-start.1) | collective-permute-done | bytes 131104 | tf_op jit(solution)/shard_map/ppermute | solution.py:234
  30.4 3.7 %collective-permute-start.16 = (bf16[2,32,128]{2,1,0:T(8,128)(2,1)S(1)}, bf16[2,32,128]{2,1,0:T(8,128)(2,1)S(1)}, u32[]{:S(2)}, u32[]{:S(2)}) collective-permute-start(bf16[2,32,128]{2,1,0:T(8,128)(2,1)S(1)} %get-tuple-element.29), channel_id=1, source_target_pairs={{0,3},{1,0},{2,1},{3,2},{4,7},{5,4},{6,5},{7,6},{8,11},{9,8},{10,9... | collective-permute-start | bytes 49160 | tf_op jit(solution)/shard_map/ppermute | solution.py:250
  34.1 1.0 %collective-permute-start.14 = (bf16[2,32,128]{2,1,0:T(8,128)(2,1)S(1)}, bf16[2,32,128]{2,1,0:T(8,128)(2,1)S(1)}, u32[]{:S(2)}, u32[]{:S(2)}) collective-permute-start(bf16[2,32,128]{2,1,0:T(8,128)(2,1)S(1)} %get-tuple-element.31), channel_id=1, source_target_pairs={{0,1},{1,2},{2,3},{3,0},{4,5},{5,6},{6,7},{7,4},{8,9},{9,10},{10,1... | collective-permute-start | bytes 49160 | tf_op jit(solution)/shard_map/ppermute | solution.py:250
  35.1 2.9 %collective-permute-start.8 = (bf16[2,32,128]{2,1,0:T(8,128)(2,1)S(1)}, bf16[2,32,128]{2,1,0:T(8,128)(2,1)S(1)}, u32[]{:S(2)}, u32[]{:S(2)}) collective-permute-start(bf16[2,32,128]{2,1,0:T(8,128)(2,1)S(1)} %get-tuple-element.32), channel_id=1, source_target_pairs={{0,3},{1,0},{2,1},{3,2},{4,7},{5,4},{6,5},{7,6},{8,11},{9,8},{10,9... | collective-permute-start | bytes 49160 | tf_op jit(solution)/shard_map/ppermute | solution.py:250
  38.0 1.1 %collective-permute-start.7 = (bf16[2,32,128]{2,1,0:T(8,128)(2,1)S(1)}, bf16[2,32,128]{2,1,0:T(8,128)(2,1)S(1)}, u32[]{:S(2)}, u32[]{:S(2)}) collective-permute-start(bf16[2,32,128]{2,1,0:T(8,128)(2,1)S(1)} %get-tuple-element.33), channel_id=1, source_target_pairs={{0,2},{1,3},{2,0},{3,1},{4,6},{5,7},{6,4},{7,5},{8,10},{9,11},{10,... | collective-permute-start | bytes 49160 | tf_op jit(solution)/shard_map/ppermute | solution.py:250
  39.1 0.9 %dynamic-slice_bitcast_fusion.table_ref = bf16[256,256]{1,0:T(8,128)(2,1)S(1)} fusion(bf16[4,256,256]{2,1,0:T(8,128)(2,1)} %constant.12.clone, s32[]{:T(128)S(6)} %select_n.4), kind=kLoop, calls=%fused_computation | loop fusion | bytes 262148 | tf_op jit(solution)/shard_map/jit(dynamic_index_in_dim)/squeeze | solution.py:241
  40.1 1.7 %transform.2.refs_3_ = bf16[4,16,128,256]{3,2,1,0:T(8,128)(2,1)} custom-call(bf16[256,256]{1,0:T(8,128)(2,1)S(1)} %dynamic-slice_bitcast_fusion.table_ref, bf16[4,2,32,128]{3,2,1,0:T(8,128)(2,1)S(1)} %finish.3.own_ref, bf16[2,32,128]{2,1,0:T(8,128)(2,1)S(1)} %collective-permute-done.14.refs_0_, bf16[2,32,128]{2,1,0:T(8,128)(2,1)S(1)} %collective-permute-done.15.refs_1_, ...), custom_call_target="tpu_custom_call" | custom-call | tf_op jit(solution)/shard_map/transform/pallas_call | solution.py:212
  41.8 0.9 %collective-permute-done.7.refs_1_ = bf16[2,32,128]{2,1,0:T(8,128)(2,1)S(1)} collective-permute-done((bf16[2,32,128]{2,1,0:T(8,128)(2,1)S(1)}, bf16[2,32,128]{2,1,0:T(8,128)(2,1)S(1)}, u32[]{:S(2)}, u32[]{:S(2)}) %collective-permute-start.7) | collective-permute-done | bytes 16416 | tf_op jit(solution)/shard_map/ppermute | solution.py:250
  42.7 2.0 %collective-permute-done.6.refs_0_ = bf16[2,32,128]{2,1,0:T(8,128)(2,1)S(1)} collective-permute-done((bf16[2,32,128]{2,1,0:T(8,128)(2,1)S(1)}, bf16[2,32,128]{2,1,0:T(8,128)(2,1)S(1)}, u32[]{:S(2)}, u32[]{:S(2)}) %collective-permute-start.6) | collective-permute-done | bytes 16416 | tf_op jit(solution)/shard_map/ppermute | solution.py:250
  44.7 1.7 %transform.3 = bf16[4,16,128,256]{3,2,1,0:T(8,128)(2,1)} custom-call(bf16[256,256]{1,0:T(8,128)(2,1)S(1)} %dynamic-slice_bitcast_fusion.table_ref, bf16[4,2,32,128]{3,2,1,0:T(8,128)(2,1)S(1)} %finish.2.own_ref, bf16[2,32,128]{2,1,0:T(8,128)(2,1)S(1)} %collective-permute-done.6.refs_0_, ...), custom_call_target="tpu_custom_call", output_to_operand_aliasing={{}: (5, {})} | custom-call | tf_op jit(solution)/shard_map/transform/pallas_call | solution.py:212
  (35 shorter events, 4.9 us)
Async XLA Ops:
  0.0 1.6 %copy-start = (bf16[1,2,4096,128]{3,2,1,0:T(8,128)(2,1)S(1)}, bf16[1,2,4096,128]{3,2,1,0:T(8,128)(2,1)}, u32[]{:S(2)}) copy-start(bf16[1,2,4096,128]{3,2,1,0:T(8,128)(2,1)} %data_ref.1) | copy-start | bytes 6291460
  1.6 0.7 %copy-start.3 = (s32[8]{0:T(128)S(1)}, s32[8]{0:T(128)}, u32[]{:S(2)}) copy-start(s32[8]{0:T(128)} %block_ref.1) | copy-start | bytes 100
  3.1 23.3 %collective-permute-start.4 = (bf16[4,2,512,128]{3,2,1,0:T(8,128)(2,1)S(1)}, bf16[4,2,512,128]{3,2,1,0:T(8,128)(2,1)S(1)}, u32[]{:S(2)}, u32[]{:S(2)}) collective-permute-start(bf16[4,2,512,128]{3,2,1,0:T(8,128)(2,1)S(1)} %get-tuple-element.19), channel_id=1, source_target_pairs={{0,4},{4,0},{8,12},{12,8},{16,20},{20,16},{24,28},{28,24},{1,5},{5... | collective-permute-start | bytes 3145736 | tf_op jit(solution)/shard_map/ppermute | solution.py:234
  3.6 1.0 %copy-start.1 = (bf16[1,1,2,256,512]{4,3,2,1,0:T(8,128)(2,1)S(1)}, bf16[1,1,2,256,512]{4,3,2,1,0:T(8,128)(2,1)}, u32[]{:S(2)}) copy-start(bf16[1,1,2,256,512]{4,3,2,1,0:T(8,128)(2,1)} %g_ref.1) | copy-start | bytes 1572868
  4.6 0.7 %copy-start.2 = (s32[256]{0:T(256)S(1)}, s32[256]{0:T(256)}, u32[]{:S(2)}) copy-start(s32[256]{0:T(256)} %param.8) | copy-start | bytes 3076
  6.2 9.7 %collective-permute-start.11 = (bf16[2,128,512]{2,1,0:T(8,128)(2,1)S(1)}, bf16[2,128,512]{2,1,0:T(8,128)(2,1)S(1)}, u32[]{:S(2)}, u32[]{:S(2)}) collective-permute-start(bf16[2,128,512]{2,1,0:T(8,128)(2,1)S(1)} %get-tuple-element.24.refs_0_), channel_id=1, source_target_pairs={{0,8},{4,12},{8,0},{12,4},{16,24},{20,28},{24,16},{28,20},{1,9},{5... | collective-permute-start | bytes 786440 | tf_op jit(solution)/shard_map/ppermute | solution.py:234
  8.7 9.2 %collective-permute-start.9 = (bf16[2,128,512]{2,1,0:T(8,128)(2,1)S(1)}, bf16[2,128,512]{2,1,0:T(8,128)(2,1)S(1)}, u32[]{:S(2)}, u32[]{:S(2)}) collective-permute-start(bf16[2,128,512]{2,1,0:T(8,128)(2,1)S(1)} %get-tuple-element.24.refs_0_), channel_id=1, source_target_pairs={{0,16},{4,20},{8,24},{12,28},{16,0},{20,4},{24,8},{28,12},{1,17},{... | collective-permute-start | bytes 786440 | tf_op jit(solution)/shard_map/ppermute | solution.py:234
  10.3 11.3 %collective-permute-start.2 = (bf16[2,128,512]{2,1,0:T(8,128)(2,1)S(1)}, bf16[2,128,512]{2,1,0:T(8,128)(2,1)S(1)}, u32[]{:S(2)}, u32[]{:S(2)}) collective-permute-start(bf16[2,128,512]{2,1,0:T(8,128)(2,1)S(1)} %get-tuple-element.17.refs_0_), channel_id=1, source_target_pairs={{0,8},{4,12},{8,0},{12,4},{16,24},{20,28},{24,16},{28,20},{1,9},{5... | collective-permute-start | bytes 786440 | tf_op jit(solution)/shard_map/ppermute | solution.py:234
  10.8 13.4 %collective-permute-start = (bf16[2,128,512]{2,1,0:T(8,128)(2,1)S(1)}, bf16[2,128,512]{2,1,0:T(8,128)(2,1)S(1)}, u32[]{:S(2)}, u32[]{:S(2)}) collective-permute-start(bf16[2,128,512]{2,1,0:T(8,128)(2,1)S(1)} %get-tuple-element.17.refs_0_), channel_id=1, source_target_pairs={{0,16},{4,20},{8,24},{12,28},{16,0},{20,4},{24,8},{28,12},{1,17},{... | collective-permute-start | bytes 786440 | tf_op jit(solution)/shard_map/ppermute | solution.py:234
  15.9 11.0 %collective-permute-start.12 = (bf16[1,128,512]{2,1,0:T(8,128)(2,1)S(1)}, bf16[1,128,512]{2,1,0:T(8,128)(2,1)S(1)}, u32[]{:S(2)}, u32[]{:S(2)}) collective-permute-start(bf16[1,128,512]{2,1,0:T(8,128)(2,1)S(1)} %slice.46), channel_id=1, source_target_pairs={{0,16},{4,20},{8,24},{12,28},{16,0},{20,4},{24,8},{28,12},{1,17},{... | collective-permute-start | bytes 393224 | tf_op jit(solution)/shard_map/ppermute | solution.py:234
  18.0 9.0 %collective-permute-start.10 = (bf16[1,128,512]{2,1,0:T(8,128)(2,1)S(1)}, bf16[1,128,512]{2,1,0:T(8,128)(2,1)S(1)}, u32[]{:S(2)}, u32[]{:S(2)}) collective-permute-start(bf16[1,128,512]{2,1,0:T(8,128)(2,1)S(1)} %slice.45), channel_id=1, source_target_pairs={{0,8},{4,12},{8,0},{12,4},{16,24},{20,28},{24,16},{28,20},{1,9},{5... | collective-permute-start | bytes 393224 | tf_op jit(solution)/shard_map/ppermute | solution.py:234
  22.2 6.2 %collective-permute-start.3 = (bf16[1,128,512]{2,1,0:T(8,128)(2,1)}, bf16[1,128,512]{2,1,0:T(8,128)(2,1)S(1)}, u32[]{:S(2)}, u32[]{:S(2)}) collective-permute-start(bf16[1,128,512]{2,1,0:T(8,128)(2,1)} %slice.41), channel_id=1, source_target_pairs={{0,16},{4,20},{8,24},{12,28},{16,0},{20,4},{24,8},{28,12},{1,17},{... | collective-permute-start | bytes 393224 | tf_op jit(solution)/shard_map/ppermute | solution.py:234
  24.8 5.2 %collective-permute-start.1 = (bf16[1,128,512]{2,1,0:T(8,128)(2,1)}, bf16[1,128,512]{2,1,0:T(8,128)(2,1)S(1)}, u32[]{:S(2)}, u32[]{:S(2)}) collective-permute-start(bf16[1,128,512]{2,1,0:T(8,128)(2,1)} %slice.40), channel_id=1, source_target_pairs={{0,8},{4,12},{8,0},{12,4},{16,24},{20,28},{24,16},{28,20},{1,9},{5... | collective-permute-start | bytes 393224 | tf_op jit(solution)/shard_map/ppermute | solution.py:234
  27.2 3.2 %collective-permute-start.13 = (f32[128,256]{1,0:T(8,128)S(1)}, f32[128,256]{1,0:T(8,128)S(1)}, u32[]{:S(2)}, u32[]{:S(2)}) collective-permute-start(f32[128,256]{1,0:T(8,128)S(1)} %get-tuple-element.28), channel_id=1, source_target_pairs={{0,4},{4,0},{8,12},{12,8},{16,20},{20,16},{24,28},{28,24},{1,5},{5... | collective-permute-start | bytes 393224 | tf_op jit(solution)/shard_map/ppermute | solution.py:234
  30.3 4.8 %collective-permute-start.5 = (f32[128,256]{1,0:T(8,128)S(1)}, f32[128,256]{1,0:T(8,128)S(1)}, u32[]{:S(2)}, u32[]{:S(2)}) collective-permute-start(f32[128,256]{1,0:T(8,128)S(1)} %get-tuple-element.23), channel_id=1, source_target_pairs={{0,4},{4,0},{8,12},{12,8},{16,20},{20,16},{24,28},{28,24},{1,5},{5... | collective-permute-start | bytes 393224 | tf_op jit(solution)/shard_map/ppermute | solution.py:234
  30.4 8.7 %collective-permute-start.16 = (bf16[2,32,128]{2,1,0:T(8,128)(2,1)S(1)}, bf16[2,32,128]{2,1,0:T(8,128)(2,1)S(1)}, u32[]{:S(2)}, u32[]{:S(2)}) collective-permute-start(bf16[2,32,128]{2,1,0:T(8,128)(2,1)S(1)} %get-tuple-element.29), channel_id=1, source_target_pairs={{0,3},{1,0},{2,1},{3,2},{4,7},{5,4},{6,5},{7,6},{8,11},{9,8},{10,9... | collective-permute-start | bytes 49160 | tf_op jit(solution)/shard_map/ppermute | solution.py:250
  34.1 6.0 %collective-permute-start.15 = (bf16[2,32,128]{2,1,0:T(8,128)(2,1)S(1)}, bf16[2,32,128]{2,1,0:T(8,128)(2,1)S(1)}, u32[]{:S(2)}, u32[]{:S(2)}) collective-permute-start(bf16[2,32,128]{2,1,0:T(8,128)(2,1)S(1)} %get-tuple-element.30), channel_id=1, source_target_pairs={{0,2},{1,3},{2,0},{3,1},{4,6},{5,7},{6,4},{7,5},{8,10},{9,11},{10,... | collective-permute-start | bytes 49160 | tf_op jit(solution)/shard_map/ppermute | solution.py:250
  34.1 6.0 %collective-permute-start.14 = (bf16[2,32,128]{2,1,0:T(8,128)(2,1)S(1)}, bf16[2,32,128]{2,1,0:T(8,128)(2,1)S(1)}, u32[]{:S(2)}, u32[]{:S(2)}) collective-permute-start(bf16[2,32,128]{2,1,0:T(8,128)(2,1)S(1)} %get-tuple-element.31), channel_id=1, source_target_pairs={{0,1},{1,2},{2,3},{3,0},{4,5},{5,6},{6,7},{7,4},{8,9},{9,10},{10,1... | collective-permute-start | bytes 49160 | tf_op jit(solution)/shard_map/ppermute | solution.py:250
  35.1 6.6 %collective-permute-start.8 = (bf16[2,32,128]{2,1,0:T(8,128)(2,1)S(1)}, bf16[2,32,128]{2,1,0:T(8,128)(2,1)S(1)}, u32[]{:S(2)}, u32[]{:S(2)}) collective-permute-start(bf16[2,32,128]{2,1,0:T(8,128)(2,1)S(1)} %get-tuple-element.32), channel_id=1, source_target_pairs={{0,3},{1,0},{2,1},{3,2},{4,7},{5,4},{6,5},{7,6},{8,11},{9,8},{10,9... | collective-permute-start | bytes 49160 | tf_op jit(solution)/shard_map/ppermute | solution.py:250
  38.0 4.6 %collective-permute-start.7 = (bf16[2,32,128]{2,1,0:T(8,128)(2,1)S(1)}, bf16[2,32,128]{2,1,0:T(8,128)(2,1)S(1)}, u32[]{:S(2)}, u32[]{:S(2)}) collective-permute-start(bf16[2,32,128]{2,1,0:T(8,128)(2,1)S(1)} %get-tuple-element.33), channel_id=1, source_target_pairs={{0,2},{1,3},{2,0},{3,1},{4,6},{5,7},{6,4},{7,5},{8,10},{9,11},{10,... | collective-permute-start | bytes 49160 | tf_op jit(solution)/shard_map/ppermute | solution.py:250
  39.1 5.5 %collective-permute-start.6 = (bf16[2,32,128]{2,1,0:T(8,128)(2,1)S(1)}, bf16[2,32,128]{2,1,0:T(8,128)(2,1)S(1)}, u32[]{:S(2)}, u32[]{:S(2)}) collective-permute-start(bf16[2,32,128]{2,1,0:T(8,128)(2,1)S(1)} %get-tuple-element.34), channel_id=1, source_target_pairs={{0,1},{1,2},{2,3},{3,0},{4,5},{5,6},{6,7},{7,4},{8,9},{9,10},{10,1... | collective-permute-start | bytes 49160 | tf_op jit(solution)/shard_map/ppermute | solution.py:250

commit v2 on v1

v2 whole, which is shorter than its diff:
```python
import functools
import math

import jax
import jax.numpy as jnp
import numpy as np
from jax import lax
from jax.experimental import pallas as pl
from jax.experimental.pallas import tpu as pltpu
from jax.sharding import PartitionSpec as P

NT = 256
UNIT = 16
VMEM = pl.BlockSpec(memory_space=pltpu.VMEM)
ANY = pl.BlockSpec(memory_space=pl.ANY)
PARAMS = pltpu.CompilerParams(vmem_limit_bytes=16 * 2**20)


def order_rows(receivers, receiver_order, nf):
    _, _, two, rows, width = receivers.shape
    quarter = rows // nf
    count = quarter // 2
    far = (nf - 1) * count

    def kernel(order_ref, g_ref, keep_far, keep_near, give_far, give_near, order, g, hot, sems):
        copies = [
            pltpu.make_async_copy(order_ref, order, sems.at[0]),
            pltpu.make_async_copy(g_ref.at[0, 0], g, sems.at[1]),
        ]
        for copy in copies:
            copy.start()
        core = lax.rem(lax.axis_index("src"), 2)
        z = lax.axis_index("freq")
        copies[0].wait()
        wanted = jnp.broadcast_to(order[...], (rows, rows)).T
        lane = lax.broadcasted_iota(jnp.int32, (rows, rows), 1)
        hot[...] = jnp.where(wanted == lane, 1.0, 0.0).astype(jnp.bfloat16)
        copies[1].wait()
        for half, out_far, out_near in ((core, keep_far, keep_near), (1 - core, give_far, give_near)):
            picks = []
            for step in range(1, nf + 1):
                at = pl.multiple_of(lax.rem(z + step, nf) * quarter + half * count, UNIT)
                picks.append(hot[pl.ds(at, count), :])
            pick = jnp.concatenate(picks, axis=0)
            for part in range(two):
                found = jnp.dot(pick, g[part], preferred_element_type=jnp.float32).astype(jnp.bfloat16)
                out_far[part] = found[:far]
                out_near[part] = found[far:]

    shapes = [jax.ShapeDtypeStruct((two, n, width), jnp.bfloat16) for n in (far, count)]
    return pl.pallas_call(
        kernel,
        out_shape=shapes * 2,
        in_specs=[ANY, ANY],
        out_specs=[VMEM] * 4,
        scratch_shapes=[
            pltpu.VMEM((1, rows), jnp.int32),
            pltpu.VMEM((two, rows, width), jnp.bfloat16),
            pltpu.VMEM((rows, rows), jnp.bfloat16),
            pltpu.SemaphoreType.DMA((2,)),
        ],
        compiler_params=pltpu.CompilerParams(vmem_limit_bytes=PRELUDE),
        name="order_rows",
    )(receiver_order.reshape(1, rows), receivers)


PRELUDE = 60 * 2**20


def pick_blocks(block_of_slot, data, theirs, tables, width, ns):
    chips = ns // 2
    two, _, cols = data.shape[1:]

    def kernel(block_ref, data_ref, theirs_ref, tables_ref, out, table, block, sems, more):
        me = lax.axis_index("src")
        chip, core = me // 2, lax.rem(me, 2)
        copy = pltpu.make_async_copy(block_ref, block, more.at[0])
        copy.start()
        last = pltpu.make_async_copy(tables_ref.at[lax.axis_index("freq")], table, more.at[1])
        last.start()
        copy.wait()
        copies = []
        for j in range(chips):
            for other in range(2):
                slot = jnp.bitwise_xor(chip, j) * 2 + (1 - core if other else core)
                at = pl.multiple_of(block[slot] * width, width)
                for side, ref in enumerate((data_ref, theirs_ref)):
                    copies.append(
                        pltpu.make_async_copy(
                            ref.at[0, :, pl.ds(at, width), :], out.at[2 * j + other, side], sems.at[2 * j + other, side]
                        )
                    )
        for copy in copies:
            copy.start()
        for copy in copies:
            copy.wait()
        last.wait()

    return pl.pallas_call(
        kernel,
        out_shape=[
            jax.ShapeDtypeStruct((ns, 2, two, width, cols), jnp.bfloat16),
            jax.ShapeDtypeStruct(tables.shape[1:], jnp.bfloat16),
        ],
        in_specs=[ANY] * 4,
        out_specs=[VMEM, VMEM],
        scratch_shapes=[
            pltpu.SMEM((ns,), jnp.int32),
            pltpu.SemaphoreType.DMA((ns, 2)),
            pltpu.SemaphoreType.DMA((2,)),
        ],
        compiler_params=PARAMS,
        name="pick_blocks",
    )(block_of_slot, data, theirs, tables)


def accumulate(pieces, blocks, old, steps):
    arrays = []
    plan = []
    for j, other, array, plane in pieces:
        if not any(array is held for held in arrays):
            arrays.append(array)
        plan.append((2 * j + other, next(i for i, held in enumerate(arrays) if held is array), plane))
    n = len(arrays)
    _, rows, width = arrays[0].shape
    two, _, cols = blocks.shape[2:]

    def kernel(*refs):
        given, block_ref, before, out = refs[:n], refs[n], refs[n + 1 : -1], refs[-1]
        total = before[0][...] if before else None
        for which, at, plane in plan:
            sides = [(block_ref[which, side, 0], block_ref[which, side, 1]) for side in range(2)]
            straight = jnp.concatenate([x for re, im in sides for x in (re, im)], axis=1)
            crossed = jnp.concatenate([x for re, im in sides for x in (-im, re)], axis=1)
            for part, rhs in ((0, straight), (1, crossed)):
                term = jnp.dot(given[at][plane + part], rhs, preferred_element_type=jnp.float32)
                total = term if total is None else total + term
        if not steps:
            out[...] = total
            return
        size = rows // steps
        total = total.astype(jnp.bfloat16)
        for step in range(steps):
            for side in range(2):
                for part in range(two):
                    at = (side * two + part) * cols
                    out[step, side, part] = total[step * size : (step + 1) * size, at : at + cols]

    shape = (
        jax.ShapeDtypeStruct((steps, 2, two, rows // steps, cols), jnp.bfloat16)
        if steps
        else jax.ShapeDtypeStruct((rows, 4 * cols), jnp.float32)
    )
    return pl.pallas_call(
        kernel,
        out_shape=shape,
        in_specs=[VMEM] * (n + 1 + (old is not None)),
        out_specs=VMEM,
        compiler_params=PARAMS,
        cost_estimate=pl.CostEstimate(
            flops=2 * len(plan) * two * rows * width * 4 * cols,
            bytes_accessed=2 * len(plan) * (two * rows * width + 2 * two * width * cols),
            transcendentals=0,
        ),
        name="accumulate",
    )(*arrays, blocks, *(() if old is None else (old,)))


def tables_of(nf):
    freqs = (np.arange(nf)[:, None] - np.arange(nf)[None, :]) % nf
    bins = (2 * freqs + 1) * (NT // (4 * nf))
    phase = bins[:, :, None] * np.arange(NT) % NT
    angle = phase * (2.0 * math.pi / NT)
    full = np.stack([np.cos(angle), -np.sin(angle)], 2) * nf**-0.5
    high = full.astype(jnp.bfloat16)
    low = (full - high.astype(np.float64)).astype(jnp.bfloat16)
    both = np.stack([high, low], 1)
    both = np.broadcast_to(both[:, :, :, :, None, :], (nf, 2, nf, 2, UNIT, NT))
    return np.ascontiguousarray(both).reshape(nf, 4 * nf * UNIT, NT)


def transform(table, spectra, side, other, quarter, out):
    nf = len(spectra)
    count, cols = spectra[0].shape[-2:]
    groups = count // UNIT
    depth = table.shape[0]
    each = 4
    steps = UNIT // each
    first = out is None

    def kernel(table_ref, *refs):
        given = refs[:nf]
        out_ref, held, sems = refs[-3:]
        core = lax.rem(lax.axis_index("src"), 2)
        half = 1 - core if other else core
        lhs = []
        for g in range(groups):
            rows = pl.ds(g * UNIT, UNIT)
            x = jnp.concatenate(
                [ref[part, rows, :] if side is None else ref[side, part, rows, :] for ref in given for part in range(2)],
                axis=0,
            )
            x = x.T
            lhs.append(jnp.concatenate([x, x], axis=1))
        lhs = jnp.concatenate(lhs, axis=0)
        row = lax.rem(lax.broadcasted_iota(jnp.int32, (depth, NT), 0), UNIT)
        full = table_ref[...]
        copies = []
        for step in range(steps):
            for r in range(step * each, (step + 1) * each):
                rhs = jnp.where(row == r, full, jnp.zeros_like(full))
                res = jnp.dot(lhs, rhs, preferred_element_type=jnp.float32).astype(jnp.bfloat16)
                held[:, r] = res.reshape(groups, cols, NT)
            copy = pltpu.make_async_copy(
                held.at[:, pl.ds(step * each, each)],
                out_ref.at[pl.ds(half * groups, groups), pl.ds(step * each, each)],
                sems.at[step],
            )
            copy.start()
            copies.append(copy)
        for copy in copies:
            copy.wait()

    return pl.pallas_call(
        kernel,
        out_shape=jax.ShapeDtypeStruct((quarter // UNIT, UNIT, cols, NT), jnp.bfloat16),
        in_specs=[VMEM] * (1 + nf) + ([] if first else [ANY]),
        out_specs=ANY,
        scratch_shapes=[pltpu.VMEM((groups, UNIT, cols, NT), jnp.bfloat16), pltpu.SemaphoreType.DMA((steps,))],
        input_output_aliases={} if first else {nf + 1: 0},
        compiler_params=PARAMS,
        name="transform",
    )(table, *spectra, *([] if first else [out]))


def body(ns, nf, receivers, data, block_of_slot, receiver_order):
    rows, width = receivers.shape[3:]
    chips = ns // 2
    quarter = rows // nf

    def over(value, flip):
        return lax.ppermute(value, "src", [(i, i ^ flip) for i in range(ns)])

    keep, keep_near, give, give_near = order_rows(receivers, receiver_order, nf)
    taken, taken_near = over(give, 1), over(give_near, 1)
    b_keep = over(keep, 4)
    a_taken = over(taken, 2)
    a_keep = over(keep, 2)
    b_taken = over(taken, 4)
    theirs = over(data, 1)
    early = [(0, 0, keep, 0), (0, 1, taken, 0), (2, 0, b_keep, 0), (1, 1, a_taken, 0), (1, 0, a_keep, 0), (2, 1, b_taken, 0)]
    late = [(3, 0, over(b_keep, 2), 0), (3, 1, over(a_taken, 4), 0)]
    near = jnp.concatenate([keep_near, taken_near], axis=0)
    far = 4
    while far < chips:
        late += [(far + j, other, over(array, 2 * far), 0) for j, other, array, _ in early + late]
        far *= 2
    nears = [near] + [over(near, 2 * j) for j in range(1, chips)]
    blocks, table = pick_blocks(block_of_slot, data, theirs, jnp.asarray(tables_of(nf)), width, ns)
    sums = accumulate(early, blocks, None, 0)
    sums = accumulate(late, blocks, sums, nf - 1)
    got = [
        lax.ppermute(sums[s - 1], "freq", [(i, (i + s) % nf) for i in range(nf)]) for s in range(1, nf)
    ]
    own = accumulate([(j, other, array, 2 * other) for j, array in enumerate(nears) for other in range(2)], blocks, None, 1)
    got = [own[0]] + got
    crossed = over(jnp.stack([x[1] for x in got]), 1)
    out = transform(table, got, 0, False, quarter, None)
    out = transform(table, [crossed[s] for s in range(nf)], None, True, quarter, out)
    return out.reshape(quarter, *out.shape[2:])


def solution(mesh):
    ns, nf = mesh.shape["src"], mesh.shape["freq"]
    placed = (P("freq", "src", None, None, None), P("freq", None, None, "src"), P(), P())
    return jax.shard_map(
        functools.partial(body, ns, nf), mesh=mesh, in_specs=placed, out_specs=P("freq", "src", None), check_vma=False
    )
```

time: 46.6 us -> 38.4 us (0.82)
  waiting for transfers between devices: 12.1 us -> 4.63 us
  Pallas kernels: 6.84 us -> 9.64 us
  local copies, waits for them, and re-layouts: 6.25 us -> 4.18 us
  starting transfers between devices: 21 us -> 19.4 us
    ppermute x11 -> x13, waiting for transfers between devices: 9.14 us -> 2.23 us  [over(): return lax.ppermute(value, 'src', [(i, i ^ flip) for i in range(ns)])]
    ppermute x6 -> x3, starting transfers between devices: 8.66 us -> 4.67 us  [body(): lax.ppermute(sums[s - 1], 'freq', [(i, (i + s) % nf) for i in range(nf)])]
    pallas_call x10 -> x7, Pallas kernels: 6.84 us -> 9.64 us  [the longest x2 3.35 us: transform(): pl.pallas_call(kernel, out_shape=jax.ShapeDtypeStruct((quarter // UNIT, U...]
    ppermute x11 -> x13, starting transfers between devices: 12.4 us -> 14.7 us  [over(): return lax.ppermute(value, 'src', [(i, i ^ flip) for i in range(ns)])]
    slice x4, local copies, waits for them, and re-layouts: 1.36 us -> 0.02 us  [body(): crossed = over(jnp.stack([x[1] for x in got]), 1)]
    squeeze x3 -> x2, local copies, waits for them, and re-layouts: 0.92 us -> 0.02 us  [the longest x1 0.01 us: body(): sums[s - 1]]
    ppermute x6 -> x3, waiting for transfers between devices: 2.92 us -> 2.4 us  [body(): lax.ppermute(sums[s - 1], 'freq', [(i, (i + s) % nf) for i in range(nf)])]
    unnamed x8 -> x9, local copies, waits for them, and re-layouts: 3.96 us -> 4.14 us
  transfers between devices with their start and end apart: 17 -> 16, of which waited for: 6 -> 4; matrix products, arithmetic and copies ran while one was open for 5% -> 2% of each run, Pallas kernels for 9% -> 21%
where the time goes in v2:
time: 38.4 us; the launch traced here: 38 us
  starting transfers between devices  19.4 us (51%)
  Pallas kernels  9.64 us (25%)
  waiting for transfers between devices  4.63 us (12%)
  local copies, waits for them, and re-layouts  4.18 us (11%)
    ppermute x13, starting transfers between devices, over(): return lax.ppermute(value, 'src', [(i, i ^ flip) for i in range(ns)])  14.7 us
    ppermute x3, starting transfers between devices, body(): lax.ppermute(sums[s - 1], 'freq', [(i, (i + s) % nf) for i in range(nf)])  4.67 us
    unnamed x9, local copies, waits for them, and re-layouts  4.14 us
    pallas_call x2, Pallas kernels, transform(): pl.pallas_call(kernel, out_shape=jax.ShapeDtypeStruct((quarter // UNIT, U...  3.35 us
    pallas_call x3, Pallas kernels, accumulate(): pl.pallas_call(kernel, out_shape=shape, in_specs=[VMEM] * (n + 1 + (old i...  3.18 us
    ppermute x3, waiting for transfers between devices, body(): lax.ppermute(sums[s - 1], 'freq', [(i, (i + s) % nf) for i in range(nf)])  2.4 us
    ppermute x13, waiting for transfers between devices, over(): return lax.ppermute(value, 'src', [(i, i ^ flip) for i in range(ns)])  2.23 us
    pallas_call x1, Pallas kernels, order_rows(): pl.pallas_call(kernel, out_shape=shapes * 2, in_specs=[ANY, ANY], out_spe...  2.07 us
  transfers between devices with their start and end apart: 16, of which 4 were waited for; matrix products, arithmetic and copies ran while one was open for 2% of the time, Pallas kernels for 21%

profile of v2, /device:TPU:0, one launch (start us, length us, event | category | flops | bytes accessed | tf_op | source)
XLA Modules:
  0.0 38.0 jit_solution(13992689889168141808)
XLA Ops:
  0.5 2.1 %order_rows.1 = (bf16[2,96,512]{2,1,0:T(8,128)(2,1)}, bf16[2,32,512]{2,1,0:T(8,128)(2,1)}, bf16[2,96,512]{2,1,0:T(8,128)(2,1)}, bf16[2,32,512]{2,1,0:T(8,128)(2,1)}) custom-call(s32[1,256]{1,0:T(1,128)} %bitcast.20, bf16[1,1,2,256,512]{4,3,2,1,0:T(8,128)(2,1)} %g_ref.1), custom_call_target="tpu_custom_call" | custom-call | tf_op jit(solution)/shard_map/order_rows/pallas_call | solution.py:51
  2.7 3.0 %collective-permute-start.5 = (bf16[2,96,512]{2,1,0:T(8,128)(2,1)}, bf16[2,96,512]{2,1,0:T(8,128)(2,1)S(1)}, u32[]{:S(2)}, u32[]{:S(2)}) collective-permute-start(bf16[2,96,512]{2,1,0:T(8,128)(2,1)} %get-tuple-element.15.refs_0_), channel_id=1, source_target_pairs={{0,16},{4,20},{8,24},{12,28},{16,0},{20,4},{24,8},{28,12},{1,17},{... | collective-permute-start | bytes 589832 | tf_op jit(solution)/shard_map/ppermute | solution.py:242
  5.6 2.0 %collective-permute-start.8 = (bf16[2,96,512]{2,1,0:T(8,128)(2,1)S(1)}, bf16[2,96,512]{2,1,0:T(8,128)(2,1)S(1)}, u32[]{:S(2)}, u32[]{:S(2)}) collective-permute-start(bf16[2,96,512]{2,1,0:T(8,128)(2,1)S(1)} %collective-permute-done.7.refs_1_), channel_id=1, source_target_pairs={{0,8},{4,12},{8,0},{12,4},{16,24},{20,28},{24,16},{28,20},{1,9},{5... | collective-permute-start | bytes 589832 | tf_op jit(solution)/shard_map/ppermute | solution.py:242
  7.7 1.3 %collective-permute-done.1 = bf16[2,32,512]{2,1,0:T(8,128)(2,1)S(1)} collective-permute-done((bf16[2,32,512]{2,1,0:T(8,128)(2,1)}, bf16[2,32,512]{2,1,0:T(8,128)(2,1)S(1)}, u32[]{:S(2)}, u32[]{:S(2)}) %collective-permute-start.1) | collective-permute-done | bytes 65568 | tf_op jit(solution)/shard_map/ppermute | solution.py:242
  9.1 1.5 %collective-permute-start.11 = (bf16[2,96,512]{2,1,0:T(8,128)(2,1)S(1)}, bf16[2,96,512]{2,1,0:T(8,128)(2,1)S(1)}, u32[]{:S(2)}, u32[]{:S(2)}) collective-permute-start(bf16[2,96,512]{2,1,0:T(8,128)(2,1)S(1)} %collective-permute-done.7.refs_1_), channel_id=1, source_target_pairs={{0,16},{4,20},{8,24},{12,28},{16,0},{20,4},{24,8},{28,12},{1,17},{... | collective-permute-start | bytes 589832 | tf_op jit(solution)/shard_map/ppermute | solution.py:242
  11.0 1.9 %collective-permute-start.6 = (bf16[2,96,512]{2,1,0:T(8,128)(2,1)S(1)}, bf16[2,96,512]{2,1,0:T(8,128)(2,1)S(1)}, u32[]{:S(2)}, u32[]{:S(2)}) collective-permute-start(bf16[2,96,512]{2,1,0:T(8,128)(2,1)S(1)} %collective-permute-done.5.refs_2_), channel_id=1, source_target_pairs={{0,8},{4,12},{8,0},{12,4},{16,24},{20,28},{24,16},{28,20},{1,9},{5... | collective-permute-start | bytes 589832 | tf_op jit(solution)/shard_map/ppermute | solution.py:242
  13.4 2.0 %collective-permute-start.9 = (bf16[2,96,512]{2,1,0:T(8,128)(2,1)S(1)}, bf16[2,96,512]{2,1,0:T(8,128)(2,1)S(1)}, u32[]{:S(2)}, u32[]{:S(2)}) collective-permute-start(bf16[2,96,512]{2,1,0:T(8,128)(2,1)S(1)} %collective-permute-done.8.refs_3_), channel_id=1, source_target_pairs={{0,16},{4,20},{8,24},{12,28},{16,0},{20,4},{24,8},{28,12},{1,17},{... | collective-permute-start | bytes 589832 | tf_op jit(solution)/shard_map/ppermute | solution.py:242
  15.4 0.8 %constant_dynamic-update-slice_fusion.1 = bf16[4,32,512]{2,1,0:T(8,128)(2,1)S(1)} fusion(bf16[2,32,512]{2,1,0:T(8,128)(2,1)} %get-tuple-element.12), kind=kLoop, calls=%fused_computation.10 | loop fusion | bytes 131072
  16.2 1.5 %collective-permute-start.4 = (bf16[4,32,512]{2,1,0:T(8,128)(2,1)S(1)}, bf16[4,32,512]{2,1,0:T(8,128)(2,1)S(1)}, u32[]{:S(2)}, u32[]{:S(2)}) collective-permute-start(bf16[4,32,512]{2,1,0:T(8,128)(2,1)S(1)} %constant_dynamic-update-slice_fusion.refs_0_), channel_id=1, source_target_pairs={{0,24},{4,28},{8,16},{12,20},{16,8},{20,12},{24,0},{28,4},{1,25},{... | collective-permute-start | bytes 393224 | tf_op jit(solution)/shard_map/ppermute | solution.py:242
  17.7 1.6 %copy-done = bf16[1,2,4096,128]{3,2,1,0:T(8,128)(2,1)S(1)} copy-done((bf16[1,2,4096,128]{3,2,1,0:T(8,128)(2,1)S(1)}, bf16[1,2,4096,128]{3,2,1,0:T(8,128)(2,1)}, u32[]{:S(2)}) %copy-start) | copy-done | bytes 2097176
  19.3 1.0 %copy-done.1 = bf16[4,256,256]{2,1,0:T(8,128)(2,1)S(1)} copy-done((bf16[4,256,256]{2,1,0:T(8,128)(2,1)S(1)}, bf16[4,256,256]{2,1,0:T(8,128)(2,1)}, u32[]{:S(2)}) %copy-start.1) | copy-done | bytes 524312
  20.4 0.7 %copy-done.3 = s32[8]{0:T(128)S(1)} copy-done((s32[8]{0:T(128)S(1)}, s32[8]{0:T(128)}, u32[]{:S(2)}) %copy-start.3) | copy-done | bytes 56
  21.0 1.0 %pick_blocks.1 = (bf16[8,2,2,512,128]{4,3,2,1,0:T(8,128)(2,1)S(1)}, bf16[256,256]{1,0:T(8,128)(2,1)S(1)}) custom-call(s32[8]{0:T(128)S(1)} %copy-done.3, bf16[1,2,4096,128]{3,2,1,0:T(8,128)(2,1)S(1)} %copy-done, bf16[1,2,4096,128]{3,2,1,0:T(8,128)(2,1)S(1)} %collective-permute-done.theirs_ref, bf16[4,256,256]{2,1,0:T(8,128)(2,1)S(1)} %copy-done.1), custom_call_target="tpu_custom_call" | custom-call | tf_op jit(solution)/shard_map/pick_blocks/pallas_call | solution.py:99
  22.1 1.6 %collective-permute-start.3 = (bf16[4,32,512]{2,1,0:T(8,128)(2,1)S(1)}, bf16[4,32,512]{2,1,0:T(8,128)(2,1)S(1)}, u32[]{:S(2)}, u32[]{:S(2)}) collective-permute-start(bf16[4,32,512]{2,1,0:T(8,128)(2,1)S(1)} %constant_dynamic-update-slice_fusion.refs_0_), channel_id=1, source_target_pairs={{0,16},{4,20},{8,24},{12,28},{16,0},{20,4},{24,8},{28,12},{1,17},{... | collective-permute-start | bytes 393224 | tf_op jit(solution)/shard_map/ppermute | solution.py:242
  23.7 0.5 %collective-permute-start.2 = (bf16[4,32,512]{2,1,0:T(8,128)(2,1)S(1)}, bf16[4,32,512]{2,1,0:T(8,128)(2,1)S(1)}, u32[]{:S(2)}, u32[]{:S(2)}) collective-permute-start(bf16[4,32,512]{2,1,0:T(8,128)(2,1)S(1)} %constant_dynamic-update-slice_fusion.refs_0_), channel_id=1, source_target_pairs={{0,8},{4,12},{8,0},{12,4},{16,24},{20,28},{24,16},{28,20},{1,9},{5... | collective-permute-start | bytes 393224 | tf_op jit(solution)/shard_map/ppermute | solution.py:242
  24.2 1.1 %accumulate.4.refs_3_ = f32[96,512]{1,0:T(8,128)S(1)} custom-call(bf16[2,96,512]{2,1,0:T(8,128)(2,1)S(1)} %copy-done.2, bf16[2,96,512]{2,1,0:T(8,128)(2,1)S(1)} %collective-permute-done.7.refs_1_, bf16[2,96,512]{2,1,0:T(8,128)(2,1)S(1)} %collective-permute-done.5.refs_2_, bf16[2,96,512]{2,1,0:T(8,128)(2,1)S(1)} %collective-permute-done.8.refs_3_, ...), custom_call_target="tpu_custom_call" | custom-call | flops 603979776 | bytes 4325376 | tf_op jit(solution)/shard_map/accumulate/pallas_call | solution.py:154
  25.4 0.5 %accumulate.5 = bf16[3,2,2,32,128]{4,3,2,1,0:T(8,128)(2,1)S(1)} custom-call(bf16[2,96,512]{2,1,0:T(8,128)(2,1)S(1)} %collective-permute-done.6.refs_0_, bf16[2,96,512]{2,1,0:T(8,128)(2,1)S(1)} %collective-permute-done.9.refs_1_, bf16[8,2,2,512,128]{4,3,2,1,0:T(8,128)(2,1)S(1)} %get-tuple-element.14.refs_4_.refs_6_.refs_2_, f32[96,512]{1,0:T(8,128)S(1)} %accumulate.4.refs_3_), custom_call_target="tpu_custom_call" | custom-call | flops 201326592 | bytes 1441792 | tf_op jit(solution)/shard_map/accumulate/pallas_call | solution.py:154
  25.9 1.6 %collective-permute-start.12 = (bf16[2,2,32,128]{3,2,1,0:T(8,128)(2,1)S(1)}, bf16[2,2,32,128]{3,2,1,0:T(8,128)(2,1)S(1)}, u32[]{:S(2)}, u32[]{:S(2)}) collective-permute-start(bf16[2,2,32,128]{3,2,1,0:T(8,128)(2,1)S(1)} %get-tuple-element.17), channel_id=1, source_target_pairs={{0,1},{1,2},{2,3},{3,0},{4,5},{5,6},{6,7},{7,4},{8,9},{9,10},{10,1... | collective-permute-start | bytes 98312 | tf_op jit(solution)/shard_map/ppermute | solution.py:263
  27.5 2.2 %collective-permute-start.14 = (bf16[2,2,32,128]{3,2,1,0:T(8,128)(2,1)S(1)}, bf16[2,2,32,128]{3,2,1,0:T(8,128)(2,1)S(1)}, u32[]{:S(2)}, u32[]{:S(2)}) collective-permute-start(bf16[2,2,32,128]{3,2,1,0:T(8,128)(2,1)S(1)} %get-tuple-element.18), channel_id=1, source_target_pairs={{0,3},{1,0},{2,1},{3,2},{4,7},{5,4},{6,5},{7,6},{8,11},{9,8},{10,9... | collective-permute-start | bytes 98312 | tf_op jit(solution)/shard_map/ppermute | solution.py:263
  29.8 0.8 %collective-permute-start.13 = (bf16[2,2,32,128]{3,2,1,0:T(8,128)(2,1)S(1)}, bf16[2,2,32,128]{3,2,1,0:T(8,128)(2,1)S(1)}, u32[]{:S(2)}, u32[]{:S(2)}) collective-permute-start(bf16[2,2,32,128]{3,2,1,0:T(8,128)(2,1)S(1)} %get-tuple-element.19), channel_id=1, source_target_pairs={{0,2},{1,3},{2,0},{3,1},{4,6},{5,7},{6,4},{7,5},{8,10},{9,11},{10,... | collective-permute-start | bytes 98312 | tf_op jit(solution)/shard_map/ppermute | solution.py:263
  30.6 1.6 %accumulate.3 = bf16[1,2,2,32,128]{4,3,2,1,0:T(8,128)(2,1)S(1)} custom-call(bf16[4,32,512]{2,1,0:T(8,128)(2,1)S(1)} %constant_dynamic-update-slice_fusion.refs_0_, bf16[4,32,512]{2,1,0:T(8,128)(2,1)S(1)} %collective-permute-done.2.refs_1_, bf16[4,32,512]{2,1,0:T(8,128)(2,1)S(1)} %collective-permute-done.3.refs_2_, ...), custom_call_target="tpu_custom_call" | custom-call | flops 268435456 | bytes 4718592 | tf_op jit(solution)/shard_map/accumulate/pallas_call | solution.py:154
  32.2 2.4 %collective-permute-done.13.refs_2_ = bf16[2,2,32,128]{3,2,1,0:T(8,128)(2,1)S(1)} collective-permute-done((bf16[2,2,32,128]{3,2,1,0:T(8,128)(2,1)S(1)}, bf16[2,2,32,128]{3,2,1,0:T(8,128)(2,1)S(1)}, u32[]{:S(2)}, u32[]{:S(2)}) %collective-permute-start.13) | collective-permute-done | bytes 32800 | tf_op jit(solution)/shard_map/ppermute | solution.py:263
  34.7 1.7 %transform.2.refs_4_ = bf16[4,16,128,256]{3,2,1,0:T(8,128)(2,1)} custom-call(bf16[256,256]{1,0:T(8,128)(2,1)S(1)} %get-tuple-element.11.table_ref, bf16[2,2,32,128]{3,2,1,0:T(8,128)(2,1)S(1)} %bitcast.19, bf16[2,2,32,128]{3,2,1,0:T(8,128)(2,1)S(1)} %collective-permute-done.12.refs_1_, bf16[2,2,32,128]{3,2,1,0:T(8,128)(2,1)S(1)} %collective-permute-done.13.refs_2_, ...), custom_call_target="tpu_custom_call" | custom-call | tf_op jit(solution)/shard_map/transform/pallas_call | solution.py:224
  36.4 1.7 %transform.3 = bf16[4,16,128,256]{3,2,1,0:T(8,128)(2,1)} custom-call(bf16[256,256]{1,0:T(8,128)(2,1)S(1)} %get-tuple-element.11.table_ref, bf16[2,32,128]{2,1,0:T(8,128)(2,1)S(1)} %get-tuple-element.23.refs_0_, bf16[2,32,128]{2,1,0:T(8,128)(2,1)S(1)} %get-tuple-element.22.refs_1_, ...), custom_call_target="tpu_custom_call", output_to_operand_aliasing={{}: (5, {})} | custom-call | tf_op jit(solution)/shard_map/transform/pallas_call | solution.py:224
  (32 shorter events, 1.8 us)
Async XLA Ops:
  0.0 16.2 %collective-permute-start = (bf16[1,2,4096,128]{3,2,1,0:T(8,128)(2,1)}, bf16[1,2,4096,128]{3,2,1,0:T(8,128)(2,1)S(1)}, u32[]{:S(2)}, u32[]{:S(2)}) collective-permute-start(bf16[1,2,4096,128]{3,2,1,0:T(8,128)(2,1)} %data_ref.1), channel_id=1, source_target_pairs={{0,4},{4,0},{8,12},{12,8},{16,20},{20,16},{24,28},{28,24},{1,5},{5... | collective-permute-start | bytes 6291464 | tf_op jit(solution)/shard_map/ppermute | solution.py:242
  2.5 21.7 %copy-start.2 = (bf16[2,96,512]{2,1,0:T(8,128)(2,1)S(1)}, bf16[2,96,512]{2,1,0:T(8,128)(2,1)}, u32[]{:S(2)}) copy-start(bf16[2,96,512]{2,1,0:T(8,128)(2,1)} %get-tuple-element.15.refs_0_) | copy-start | bytes 589828
  2.5 3.1 %collective-permute-start.7 = (bf16[2,96,512]{2,1,0:T(8,128)(2,1)}, bf16[2,96,512]{2,1,0:T(8,128)(2,1)S(1)}, u32[]{:S(2)}, u32[]{:S(2)}) collective-permute-start(bf16[2,96,512]{2,1,0:T(8,128)(2,1)} %get-tuple-element.16), channel_id=1, source_target_pairs={{0,4},{4,0},{8,12},{12,8},{16,20},{20,16},{24,28},{28,24},{1,5},{5... | collective-permute-start | bytes 589832 | tf_op jit(solution)/shard_map/ppermute | solution.py:242
  2.7 8.3 %collective-permute-start.5 = (bf16[2,96,512]{2,1,0:T(8,128)(2,1)}, bf16[2,96,512]{2,1,0:T(8,128)(2,1)S(1)}, u32[]{:S(2)}, u32[]{:S(2)}) collective-permute-start(bf16[2,96,512]{2,1,0:T(8,128)(2,1)} %get-tuple-element.15.refs_0_), channel_id=1, source_target_pairs={{0,16},{4,20},{8,24},{12,28},{16,0},{20,4},{24,8},{28,12},{1,17},{... | collective-permute-start | bytes 589832 | tf_op jit(solution)/shard_map/ppermute | solution.py:242
  5.6 7.7 %collective-permute-start.8 = (bf16[2,96,512]{2,1,0:T(8,128)(2,1)S(1)}, bf16[2,96,512]{2,1,0:T(8,128)(2,1)S(1)}, u32[]{:S(2)}, u32[]{:S(2)}) collective-permute-start(bf16[2,96,512]{2,1,0:T(8,128)(2,1)S(1)} %collective-permute-done.7.refs_1_), channel_id=1, source_target_pairs={{0,8},{4,12},{8,0},{12,4},{16,24},{20,28},{24,16},{28,20},{1,9},{5... | collective-permute-start | bytes 589832 | tf_op jit(solution)/shard_map/ppermute | solution.py:242
  7.6 1.5 %collective-permute-start.1 = (bf16[2,32,512]{2,1,0:T(8,128)(2,1)}, bf16[2,32,512]{2,1,0:T(8,128)(2,1)S(1)}, u32[]{:S(2)}, u32[]{:S(2)}) collective-permute-start(bf16[2,32,512]{2,1,0:T(8,128)(2,1)} %get-tuple-element.13), channel_id=1, source_target_pairs={{0,4},{4,0},{8,12},{12,8},{16,20},{20,16},{24,28},{28,24},{1,5},{5... | collective-permute-start | bytes 196616 | tf_op jit(solution)/shard_map/ppermute | solution.py:242
  7.6 14.5 %collective-permute-start.10 = (bf16[2,96,512]{2,1,0:T(8,128)(2,1)}, bf16[2,96,512]{2,1,0:T(8,128)(2,1)S(1)}, u32[]{:S(2)}, u32[]{:S(2)}) collective-permute-start(bf16[2,96,512]{2,1,0:T(8,128)(2,1)} %get-tuple-element.15.refs_0_), channel_id=1, source_target_pairs={{0,8},{4,12},{8,0},{12,4},{16,24},{20,28},{24,16},{28,20},{1,9},{5... | collective-permute-start | bytes 589832 | tf_op jit(solution)/shard_map/ppermute | solution.py:242
  9.1 14.6 %collective-permute-start.11 = (bf16[2,96,512]{2,1,0:T(8,128)(2,1)S(1)}, bf16[2,96,512]{2,1,0:T(8,128)(2,1)S(1)}, u32[]{:S(2)}, u32[]{:S(2)}) collective-permute-start(bf16[2,96,512]{2,1,0:T(8,128)(2,1)S(1)} %collective-permute-done.7.refs_1_), channel_id=1, source_target_pairs={{0,16},{4,20},{8,24},{12,28},{16,0},{20,4},{24,8},{28,12},{1,17},{... | collective-permute-start | bytes 589832 | tf_op jit(solution)/shard_map/ppermute | solution.py:242
  11.0 14.4 %collective-permute-start.6 = (bf16[2,96,512]{2,1,0:T(8,128)(2,1)S(1)}, bf16[2,96,512]{2,1,0:T(8,128)(2,1)S(1)}, u32[]{:S(2)}, u32[]{:S(2)}) collective-permute-start(bf16[2,96,512]{2,1,0:T(8,128)(2,1)S(1)} %collective-permute-done.5.refs_2_), channel_id=1, source_target_pairs={{0,8},{4,12},{8,0},{12,4},{16,24},{20,28},{24,16},{28,20},{1,9},{5... | collective-permute-start | bytes 589832 | tf_op jit(solution)/shard_map/ppermute | solution.py:242
  13.4 12.0 %collective-permute-start.9 = (bf16[2,96,512]{2,1,0:T(8,128)(2,1)S(1)}, bf16[2,96,512]{2,1,0:T(8,128)(2,1)S(1)}, u32[]{:S(2)}, u32[]{:S(2)}) collective-permute-start(bf16[2,96,512]{2,1,0:T(8,128)(2,1)S(1)} %collective-permute-done.8.refs_3_), channel_id=1, source_target_pairs={{0,16},{4,20},{8,24},{12,28},{16,0},{20,4},{24,8},{28,12},{1,17},{... | collective-permute-start | bytes 589832 | tf_op jit(solution)/shard_map/ppermute | solution.py:242
  16.2 13.5 %collective-permute-start.4 = (bf16[4,32,512]{2,1,0:T(8,128)(2,1)S(1)}, bf16[4,32,512]{2,1,0:T(8,128)(2,1)S(1)}, u32[]{:S(2)}, u32[]{:S(2)}) collective-permute-start(bf16[4,32,512]{2,1,0:T(8,128)(2,1)S(1)} %constant_dynamic-update-slice_fusion.refs_0_), channel_id=1, source_target_pairs={{0,24},{4,28},{8,16},{12,20},{16,8},{20,12},{24,0},{28,4},{1,25},{... | collective-permute-start | bytes 393224 | tf_op jit(solution)/shard_map/ppermute | solution.py:242
  17.7 1.6 %copy-start = (bf16[1,2,4096,128]{3,2,1,0:T(8,128)(2,1)S(1)}, bf16[1,2,4096,128]{3,2,1,0:T(8,128)(2,1)}, u32[]{:S(2)}) copy-start(bf16[1,2,4096,128]{3,2,1,0:T(8,128)(2,1)} %data_ref.1) | copy-start | bytes 6291460
  19.3 1.0 %copy-start.1 = (bf16[4,256,256]{2,1,0:T(8,128)(2,1)S(1)}, bf16[4,256,256]{2,1,0:T(8,128)(2,1)}, u32[]{:S(2)}) copy-start(bf16[4,256,256]{2,1,0:T(8,128)(2,1)} %constant.2.clone.tables_ref) | copy-start | bytes 1572868
  20.4 0.7 %copy-start.3 = (s32[8]{0:T(128)S(1)}, s32[8]{0:T(128)}, u32[]{:S(2)}) copy-start(s32[8]{0:T(128)} %block_ref.1) | copy-start | bytes 100
  22.1 8.5 %collective-permute-start.3 = (bf16[4,32,512]{2,1,0:T(8,128)(2,1)S(1)}, bf16[4,32,512]{2,1,0:T(8,128)(2,1)S(1)}, u32[]{:S(2)}, u32[]{:S(2)}) collective-permute-start(bf16[4,32,512]{2,1,0:T(8,128)(2,1)S(1)} %constant_dynamic-update-slice_fusion.refs_0_), channel_id=1, source_target_pairs={{0,16},{4,20},{8,24},{12,28},{16,0},{20,4},{24,8},{28,12},{1,17},{... | collective-permute-start | bytes 393224 | tf_op jit(solution)/shard_map/ppermute | solution.py:242
  23.7 6.9 %collective-permute-start.2 = (bf16[4,32,512]{2,1,0:T(8,128)(2,1)S(1)}, bf16[4,32,512]{2,1,0:T(8,128)(2,1)S(1)}, u32[]{:S(2)}, u32[]{:S(2)}) collective-permute-start(bf16[4,32,512]{2,1,0:T(8,128)(2,1)S(1)} %constant_dynamic-update-slice_fusion.refs_0_), channel_id=1, source_target_pairs={{0,8},{4,12},{8,0},{12,4},{16,24},{20,28},{24,16},{28,20},{1,9},{5... | collective-permute-start | bytes 393224 | tf_op jit(solution)/shard_map/ppermute | solution.py:242
  25.9 6.3 %collective-permute-start.12 = (bf16[2,2,32,128]{3,2,1,0:T(8,128)(2,1)S(1)}, bf16[2,2,32,128]{3,2,1,0:T(8,128)(2,1)S(1)}, u32[]{:S(2)}, u32[]{:S(2)}) collective-permute-start(bf16[2,2,32,128]{3,2,1,0:T(8,128)(2,1)S(1)} %get-tuple-element.17), channel_id=1, source_target_pairs={{0,1},{1,2},{2,3},{3,0},{4,5},{5,6},{6,7},{7,4},{8,9},{9,10},{10,1... | collective-permute-start | bytes 98312 | tf_op jit(solution)/shard_map/ppermute | solution.py:263
  27.5 4.6 %collective-permute-start.14 = (bf16[2,2,32,128]{3,2,1,0:T(8,128)(2,1)S(1)}, bf16[2,2,32,128]{3,2,1,0:T(8,128)(2,1)S(1)}, u32[]{:S(2)}, u32[]{:S(2)}) collective-permute-start(bf16[2,2,32,128]{3,2,1,0:T(8,128)(2,1)S(1)} %get-tuple-element.18), channel_id=1, source_target_pairs={{0,3},{1,0},{2,1},{3,2},{4,7},{5,4},{6,5},{7,6},{8,11},{9,8},{10,9... | collective-permute-start | bytes 98312 | tf_op jit(solution)/shard_map/ppermute | solution.py:263
  29.8 4.8 %collective-permute-start.13 = (bf16[2,2,32,128]{3,2,1,0:T(8,128)(2,1)S(1)}, bf16[2,2,32,128]{3,2,1,0:T(8,128)(2,1)S(1)}, u32[]{:S(2)}, u32[]{:S(2)}) collective-permute-start(bf16[2,2,32,128]{3,2,1,0:T(8,128)(2,1)S(1)} %get-tuple-element.19), channel_id=1, source_target_pairs={{0,2},{1,3},{2,0},{3,1},{4,6},{5,7},{6,4},{7,5},{8,10},{9,11},{10,... | collective-permute-start | bytes 98312 | tf_op jit(solution)/shard_map/ppermute | solution.py:263
  34.6 1.8 %collective-permute-start.15 = (bf16[4,2,32,128]{3,2,1,0:T(8,128)(2,1)S(1)}, bf16[4,2,32,128]{3,2,1,0:T(8,128)(2,1)S(1)}, u32[]{:S(2)}, u32[]{:S(2)}) collective-permute-start(bf16[4,2,32,128]{3,2,1,0:T(8,128)(2,1)S(1)} %pad_maximum_fusion), channel_id=1, source_target_pairs={{0,4},{4,0},{8,12},{12,8},{16,20},{20,16},{24,28},{28,24},{1,5},{5... | collective-permute-start | bytes 196616 | tf_op jit(solution)/shard_map/ppermute | solution.py:242

commit v3 on v2

v3 whole, which is shorter than its diff:
```python
import functools
import math

import jax
import jax.numpy as jnp
import numpy as np
from jax import lax
from jax.experimental import pallas as pl
from jax.experimental.pallas import tpu as pltpu
from jax.sharding import PartitionSpec as P

NT = 256
UNIT = 16
VMEM = pl.BlockSpec(memory_space=pltpu.VMEM)
ANY = pl.BlockSpec(memory_space=pl.ANY)
PARAMS = pltpu.CompilerParams(vmem_limit_bytes=16 * 2**20)


def flip_of(step, nf):
    return (nf - step) % nf


def order_rows(receivers, receiver_order, nf):
    _, _, two, rows, width = receivers.shape
    quarter = rows // nf
    count = quarter // 2

    def kernel(order_ref, g_ref, keep, give, order, g, hot, sems):
        copies = [
            pltpu.make_async_copy(order_ref, order, sems.at[0]),
            pltpu.make_async_copy(g_ref.at[0, 0], g, sems.at[1]),
        ]
        for copy in copies:
            copy.start()
        core = lax.rem(lax.axis_index("src"), 2)
        z = lax.axis_index("freq")
        copies[0].wait()
        wanted = jnp.broadcast_to(order[...], (rows, rows)).T
        lane = lax.broadcasted_iota(jnp.int32, (rows, rows), 1)
        hot[...] = jnp.where(wanted == lane, 1.0, 0.0).astype(jnp.bfloat16)
        copies[1].wait()
        for half, out in ((core, keep), (1 - core, give)):
            picks = []
            for step in [*range(1, nf), 0]:
                at = pl.multiple_of(jnp.bitwise_xor(z, flip_of(step, nf)) * quarter + half * count, UNIT)
                picks.append(hot[pl.ds(at, count), :])
            pick = jnp.concatenate(picks, axis=0)
            for part in range(two):
                out[part] = jnp.dot(pick, g[part], preferred_element_type=jnp.float32).astype(jnp.bfloat16)

    shape = jax.ShapeDtypeStruct((two, rows // 2, width), jnp.bfloat16)
    return pl.pallas_call(
        kernel,
        out_shape=[shape, shape],
        in_specs=[ANY, ANY],
        out_specs=[VMEM, VMEM],
        scratch_shapes=[
            pltpu.VMEM((1, rows), jnp.int32),
            pltpu.VMEM((two, rows, width), jnp.bfloat16),
            pltpu.VMEM((rows, rows), jnp.bfloat16),
            pltpu.SemaphoreType.DMA((2,)),
        ],
        compiler_params=PARAMS,
        name="order_rows",
    )(receiver_order, receivers)


def last_rows(arrays, lo):
    n = len(arrays)
    planes, rows, width = arrays[0].shape

    def kernel(*refs):
        for i, ref in enumerate(refs[:n]):
            refs[n][i * planes : (i + 1) * planes] = ref[:, lo:, :]

    return pl.pallas_call(
        kernel,
        out_shape=jax.ShapeDtypeStruct((n * planes, rows - lo, width), jnp.bfloat16),
        in_specs=[VMEM] * n,
        out_specs=VMEM,
        compiler_params=PARAMS,
        name="last_rows",
    )(*arrays)


def products(total, piece, plane, rows, sides):
    straight = jnp.concatenate([x for re, im in sides for x in (re, im)], axis=1)
    crossed = jnp.concatenate([x for re, im in sides for x in (-im, re)], axis=1)
    for part, rhs in ((0, straight), (1, crossed)):
        term = jnp.dot(piece[plane + part, rows, :], rhs, preferred_element_type=jnp.float32)
        total = term if total is None else total + term
    return total


def cost_of(count, rows, width, cols):
    return pl.CostEstimate(
        flops=16 * count * rows * width * cols,
        bytes_accessed=4 * count * (rows * width + 2 * width * cols),
        transcendentals=0,
    )


def accumulate_first(pieces, block_of_slot, data, theirs, tables, ns):
    n = len(pieces)
    two, rows, width = pieces[0][2].shape
    cols = data.shape[3]

    def kernel(block_ref, data_ref, theirs_ref, tables_ref, *refs):
        given, (out, blocks, table, block, sems, more) = refs[:n], refs[n:]
        me = lax.axis_index("src")
        chip, core = me // 2, lax.rem(me, 2)
        first = pltpu.make_async_copy(block_ref, block, more.at[0])
        first.start()
        last = pltpu.make_async_copy(tables_ref.at[lax.axis_index("freq")], table, more.at[1])
        last.start()
        first.wait()
        order = [2 * j + other for j, other, _ in pieces]
        order += [i for i in range(ns) if i not in order]
        copies = {}
        for i in order:
            slot = jnp.bitwise_xor(chip, i // 2) * 2 + (1 - core if i % 2 else core)
            at = pl.multiple_of(block[slot] * width, width)
            for side, ref in enumerate((data_ref, theirs_ref)):
                copies[i, side] = pltpu.make_async_copy(
                    ref.at[0, :, pl.ds(at, width), :], blocks.at[i, side], sems.at[i, side]
                )
                copies[i, side].start()
        total = None
        for i, piece in zip(order, given):
            for side in range(2):
                copies[i, side].wait()
            total = products(total, piece, 0, slice(None), [(blocks[i, side, 0], blocks[i, side, 1]) for side in range(2)])
        out[...] = total
        for i in order[n:]:
            for side in range(2):
                copies[i, side].wait()
        last.wait()

    return pl.pallas_call(
        kernel,
        out_shape=[
            jax.ShapeDtypeStruct((rows, 4 * cols), jnp.float32),
            jax.ShapeDtypeStruct((ns, 2, two, width, cols), jnp.bfloat16),
            jax.ShapeDtypeStruct(tables.shape[1:], jnp.bfloat16),
        ],
        in_specs=[ANY] * 4 + [VMEM] * n,
        out_specs=[VMEM] * 3,
        scratch_shapes=[
            pltpu.SMEM((ns,), jnp.int32),
            pltpu.SemaphoreType.DMA((ns, 2)),
            pltpu.SemaphoreType.DMA((2,)),
        ],
        compiler_params=PARAMS,
        cost_estimate=cost_of(n, rows, width, cols),
        name="accumulate_first",
    )(block_of_slot, data, theirs, tables, *(piece[2] for piece in pieces))


def accumulate(pieces, blocks, old, rows, steps):
    arrays = []
    plan = []
    for j, other, array, plane, lo in pieces:
        if not any(array is held for held in arrays):
            arrays.append(array)
        plan.append((2 * j + other, next(i for i, held in enumerate(arrays) if held is array), plane, lo))
    n = len(arrays)
    width = arrays[0].shape[2]
    two, _, cols = blocks.shape[2:]
    before, at = old

    def kernel(*refs):
        given, (block_ref, old_ref, out) = refs[:n], refs[n:]
        total = old_ref[at : at + rows, :]
        for i, which, plane, lo in plan:
            sides = [(block_ref[i, side, 0], block_ref[i, side, 1]) for side in range(2)]
            total = products(total, given[which], plane, slice(lo, lo + rows), sides)
        if not steps:
            out[...] = total
            return
        size = rows // steps
        total = total.astype(jnp.bfloat16)
        for step in range(steps):
            for side in range(2):
                for part in range(two):
                    lane = (side * two + part) * cols
                    out[step, side, part] = total[step * size : (step + 1) * size, lane : lane + cols]

    return pl.pallas_call(
        kernel,
        out_shape=jax.ShapeDtypeStruct((steps, 2, two, rows // steps, cols), jnp.bfloat16)
        if steps
        else jax.ShapeDtypeStruct((rows, 4 * cols), jnp.float32),
        in_specs=[VMEM] * (n + 2),
        out_specs=VMEM,
        compiler_params=PARAMS,
        cost_estimate=cost_of(len(plan), rows, width, cols),
        name="accumulate",
    )(*arrays, blocks, before)


def tables_of(nf):
    freqs = np.arange(nf)[:, None] ^ np.array([flip_of(step, nf) for step in range(nf)])[None, :]
    bins = (2 * freqs + 1) * (NT // (4 * nf))
    phase = bins[:, :, None] * np.arange(NT) % NT
    angle = phase * (2.0 * math.pi / NT)
    full = np.stack([np.cos(angle), -np.sin(angle)], 2) * nf**-0.5
    high = full.astype(jnp.bfloat16)
    low = (full - high.astype(np.float64)).astype(jnp.bfloat16)
    both = np.stack([high, low], 1)
    both = np.broadcast_to(both[:, :, :, :, None, :], (nf, 2, nf, 2, UNIT, NT))
    return np.ascontiguousarray(both).reshape(nf, 4 * nf * UNIT, NT)


def transform(table, spectra, side, other, quarter, out):
    nf = len(spectra)
    count, cols = spectra[0].shape[-2:]
    groups = count // UNIT
    depth = table.shape[0]
    each = 4
    steps = UNIT // each
    first = out is None

    def kernel(table_ref, *refs):
        given = refs[:nf]
        out_ref, held, sems = refs[-3:]
        core = lax.rem(lax.axis_index("src"), 2)
        half = 1 - core if other else core
        lhs = []
        for g in range(groups):
            rows = pl.ds(g * UNIT, UNIT)
            x = jnp.concatenate(
                [ref[part, rows, :] if side is None else ref[side, part, rows, :] for ref in given for part in range(2)],
                axis=0,
            )
            x = x.T
            lhs.append(jnp.concatenate([x, x], axis=1))
        lhs = jnp.concatenate(lhs, axis=0)
        row = lax.rem(lax.broadcasted_iota(jnp.int32, (depth, NT), 0), UNIT)
        full = table_ref[...]
        copies = []
        for step in range(steps):
            for r in range(step * each, (step + 1) * each):
                rhs = jnp.where(row == r, full, jnp.zeros_like(full))
                res = jnp.dot(lhs, rhs, preferred_element_type=jnp.float32).astype(jnp.bfloat16)
                held[:, r] = res.reshape(groups, cols, NT)
            copy = pltpu.make_async_copy(
                held.at[:, pl.ds(step * each, each)],
                out_ref.at[pl.ds(half * groups, groups), pl.ds(step * each, each)],
                sems.at[step],
            )
            copy.start()
            copies.append(copy)
        for copy in copies:
            copy.wait()

    return pl.pallas_call(
        kernel,
        out_shape=jax.ShapeDtypeStruct((quarter // UNIT, UNIT, cols, NT), jnp.bfloat16),
        in_specs=[VMEM] * (1 + nf) + ([] if first else [ANY]),
        out_specs=ANY,
        scratch_shapes=[pltpu.VMEM((groups, UNIT, cols, NT), jnp.bfloat16), pltpu.SemaphoreType.DMA((steps,))],
        input_output_aliases={} if first else {nf + 1: 0},
        compiler_params=PARAMS,
        name="transform",
    )(table, *spectra, *([] if first else [out]))


def body(ns, nf, receivers, data, block_of_slot, receiver_order):
    rows, width = receivers.shape[3:]
    chips = ns // 2
    quarter = rows // nf

    def over(value, flip):
        return lax.ppermute(value, "src", [(i, i ^ flip) for i in range(ns)])

    def in_hbm(value):
        return pltpu.with_memory_space_constraint(value, pltpu.HBM)

    half = rows // 2
    size = half // nf
    lo = half - size
    theirs = over(data, 1)
    keep, give = order_rows(in_hbm(receivers), in_hbm(receiver_order.reshape(1, rows)), nf)
    taken = over(give, 1)
    b_keep = over(keep, 4)
    a_taken = over(taken, 2)
    a_keep = over(keep, 2)
    b_taken = over(taken, 4)
    first = [(0, 0, keep), (0, 1, taken), (2, 0, b_keep), (1, 1, a_taken)]
    c_keep, c_taken = over(b_keep[:, :lo], 2), over(a_taken[:, :lo], 4)
    sums, blocks, table = accumulate_first(
        first, in_hbm(block_of_slot), in_hbm(data), theirs, in_hbm(jnp.asarray(tables_of(nf))), ns
    )
    a_keep, sums = lax.optimization_barrier((a_keep, sums))
    c_near = over(last_rows([a_keep, a_taken], lo), 4)
    second = [(1, 0, a_keep, 0, 0), (2, 1, b_taken, 0, 0)]
    slots = [(*piece[:2], (piece[2], 0, 0), (piece[2], 0, lo)) for piece in first + second]
    slots += [(3, 0, (c_keep, 0, 0), (c_near, 0, 0)), (3, 1, (c_taken, 0, 0), (c_near, 2, 0))]
    while len(slots) < ns:
        step = len(slots) // 2
        moved = {id(entry[0]): over(entry[0], 2 * step) for slot in slots for entry in slot[2:]}
        slots += [
            (step + j, other, *((moved[id(array)], plane, at) for array, plane, at in entries))
            for j, other, *entries in slots
        ]
    far = [(j, other, *entry) for j, other, entry, _ in slots[6:]]
    near = [(j, other, *entry) for j, other, _, entry in slots[6:]]
    sums = accumulate(second, blocks, (sums, 0), half, 0)
    ready = accumulate(far, blocks, (sums, 0), lo, nf - 1)
    got = [lax.ppermute(ready[s - 1], "freq", [(i, i ^ flip_of(s, nf)) for i in range(nf)]) for s in range(1, nf)]
    own = accumulate(near, blocks, (sums, lo), size, 1)
    got = [own[0]] + got
    crossed = over(jnp.stack([x[1] for x in got]), 1)
    out = transform(table, got, 0, False, quarter, None)
    out = transform(table, [crossed[s] for s in range(nf)], None, True, quarter, out)
    return out.reshape(quarter, *out.shape[2:])


def solution(mesh):
    ns, nf = mesh.shape["src"], mesh.shape["freq"]
    placed = (P("freq", "src", None, None, None), P("freq", None, None, "src"), P(), P())
    return jax.shard_map(
        functools.partial(body, ns, nf), mesh=mesh, in_specs=placed, out_specs=P("freq", "src", None), check_vma=False
    )
```

time: 38.4 us -> 37.3 us (0.971)
  waiting for transfers between devices: 4.63 us -> 8.93 us
  local copies, waits for them, and re-layouts: 4.18 us -> 0.05 us
  Pallas kernels: 9.64 us -> 8.82 us
    unnamed x9 -> x0, local copies, waits for them, and re-layouts: 4.14 us -> none
    ppermute x13 -> x10, waiting for transfers between devices: 2.23 us -> 4.76 us  [over(): return lax.ppermute(value, 'src', [(i, i ^ flip) for i in range(ns)])]
    ppermute x3, waiting for transfers between devices: 2.4 us -> 4.17 us  [body(): lax.ppermute(ready[s - 1], 'freq', [(i, i ^ flip_of(s, nf)) for i in rang...]
    pallas_call x5 -> x6, Pallas kernels: 6.3 us -> 5.48 us  [the longest x1 2.72 us: accumulate_first(): pl.pallas_call(kernel, out_shape=[jax.ShapeDtypeStruct((rows, 4 * cols),...]
    ppermute x13 -> x10, starting transfers between devices: 14.7 us -> 14.6 us  [over(): return lax.ppermute(value, 'src', [(i, i ^ flip) for i in range(ns)])]
  transfers between devices with their start and end apart: 16 -> 13, of which waited for: 4 -> 6; matrix products, arithmetic and copies ran while one was open for 2% -> 0% of each run, Pallas kernels for 21% -> 18%
where the time goes in v3:
time: 37.3 us; the launch traced here: 37.1 us
  starting transfers between devices  19.2 us (51%)
  waiting for transfers between devices  8.93 us (24%)
  Pallas kernels  8.82 us (24%)
    ppermute x10, starting transfers between devices, over(): return lax.ppermute(value, 'src', [(i, i ^ flip) for i in range(ns)])  14.6 us
    ppermute x10, waiting for transfers between devices, over(): return lax.ppermute(value, 'src', [(i, i ^ flip) for i in range(ns)])  4.76 us
    ppermute x3, starting transfers between devices, body(): lax.ppermute(ready[s - 1], 'freq', [(i, i ^ flip_of(s, nf)) for i in rang...  4.56 us
    ppermute x3, waiting for transfers between devices, body(): lax.ppermute(ready[s - 1], 'freq', [(i, i ^ flip_of(s, nf)) for i in rang...  4.17 us
    pallas_call x2, Pallas kernels, transform(): pl.pallas_call(kernel, out_shape=jax.ShapeDtypeStruct((quarter // UNIT, U...  3.34 us
    pallas_call x1, Pallas kernels, accumulate_first(): pl.pallas_call(kernel, out_shape=[jax.ShapeDtypeStruct((rows, 4 * cols),...  2.72 us
    pallas_call x1, Pallas kernels, order_rows(): pl.pallas_call(kernel, out_shape=[shape, shape], in_specs=[ANY, ANY], out...  1.38 us
    pallas_call x3, Pallas kernels, accumulate(): pl.pallas_call(kernel, out_shape=jax.ShapeDtypeStruct((steps, 2, two, row...  1.37 us
  transfers between devices with their start and end apart: 13, of which 6 were waited for; matrix products, arithmetic and copies ran while one was open for 0% of the time, Pallas kernels for 18%

profile of v3, /device:TPU:0, one launch (start us, length us, event | category | flops | bytes accessed | tf_op | source)
XLA Modules:
  0.0 37.1 jit_solution(11773730773075609207)
XLA Ops:
  0.0 0.5 %collective-permute-start = (bf16[1,2,4096,128]{3,2,1,0:T(8,128)(2,1)}, bf16[1,2,4096,128]{3,2,1,0:T(8,128)(2,1)S(1)}, u32[]{:S(2)}, u32[]{:S(2)}) collective-permute-start(bf16[1,2,4096,128]{3,2,1,0:T(8,128)(2,1)} %data_ref.1), channel_id=1, source_target_pairs={{0,4},{4,0},{8,12},{12,8},{16,20},{20,16},{24,28},{28,24},{1,5},{5... | collective-permute-start | bytes 6291464 | tf_op jit(solution)/shard_map/ppermute | solution.py:274
  0.5 1.4 %order_rows.1 = (bf16[2,128,512]{2,1,0:T(8,128)(2,1)S(1)}, bf16[2,128,512]{2,1,0:T(8,128)(2,1)S(1)}) custom-call(s32[1,256]{1,0:T(1,128)} %bitcast.20, bf16[1,1,2,256,512]{4,3,2,1,0:T(8,128)(2,1)} %g_ref.1), custom_call_target="tpu_custom_call" | custom-call | tf_op jit(solution)/shard_map/order_rows/pallas_call | solution.py:52
  1.8 0.1 collective-permute-start.1
  2.0 3.0 %collective-permute-start.2 = (bf16[2,128,512]{2,1,0:T(8,128)(2,1)S(1)}, bf16[2,128,512]{2,1,0:T(8,128)(2,1)S(1)}, u32[]{:S(2)}, u32[]{:S(2)}) collective-permute-start(bf16[2,128,512]{2,1,0:T(8,128)(2,1)S(1)} %get-tuple-element.12.refs_0_), channel_id=1, source_target_pairs={{0,16},{4,20},{8,24},{12,28},{16,0},{20,4},{24,8},{28,12},{1,17},{... | collective-permute-start | bytes 786440 | tf_op jit(solution)/shard_map/ppermute | solution.py:274
  4.9 2.5 %collective-permute-start.3 = (bf16[2,128,512]{2,1,0:T(8,128)(2,1)S(1)}, bf16[2,128,512]{2,1,0:T(8,128)(2,1)S(1)}, u32[]{:S(2)}, u32[]{:S(2)}) collective-permute-start(bf16[2,128,512]{2,1,0:T(8,128)(2,1)S(1)} %collective-permute-done.1.refs_1_), channel_id=1, source_target_pairs={{0,8},{4,12},{8,0},{12,4},{16,24},{20,28},{24,16},{28,20},{1,9},{5... | collective-permute-start | bytes 786440 | tf_op jit(solution)/shard_map/ppermute | solution.py:274
  7.5 2.0 %collective-permute-start.6 = (bf16[2,128,512]{2,1,0:T(8,128)(2,1)S(1)}, bf16[2,128,512]{2,1,0:T(8,128)(2,1)S(1)}, u32[]{:S(2)}, u32[]{:S(2)}) collective-permute-start(bf16[2,128,512]{2,1,0:T(8,128)(2,1)S(1)} %collective-permute-done.1.refs_1_), channel_id=1, source_target_pairs={{0,16},{4,20},{8,24},{12,28},{16,0},{20,4},{24,8},{28,12},{1,17},{... | collective-permute-start | bytes 786440 | tf_op jit(solution)/shard_map/ppermute | solution.py:274
  9.5 2.5 %collective-permute-done.2.refs_2_ = bf16[2,128,512]{2,1,0:T(8,128)(2,1)S(1)} collective-permute-done((bf16[2,128,512]{2,1,0:T(8,128)(2,1)S(1)}, bf16[2,128,512]{2,1,0:T(8,128)(2,1)S(1)}, u32[]{:S(2)}, u32[]{:S(2)}) %collective-permute-start.2) | collective-permute-done | bytes 262176 | tf_op jit(solution)/shard_map/ppermute | solution.py:274
  12.1 2.1 %collective-permute-start.7 = (bf16[2,96,512]{2,1,0:T(8,128)(2,1)S(1)}, bf16[2,96,512]{2,1,0:T(8,128)(2,1)S(1)}, u32[]{:S(2)}, u32[]{:S(2)}) collective-permute-start(bf16[2,96,512]{2,1,0:T(8,128)(2,1)S(1)} %slice.57), channel_id=1, source_target_pairs={{0,8},{4,12},{8,0},{12,4},{16,24},{20,28},{24,16},{28,20},{1,9},{5... | collective-permute-start | bytes 589832 | tf_op jit(solution)/shard_map/ppermute | solution.py:274
  14.2 0.4 %collective-permute-done.3.refs_3_.refs_1_ = bf16[2,128,512]{2,1,0:T(8,128)(2,1)S(1)} collective-permute-done((bf16[2,128,512]{2,1,0:T(8,128)(2,1)S(1)}, bf16[2,128,512]{2,1,0:T(8,128)(2,1)S(1)}, u32[]{:S(2)}, u32[]{:S(2)}) %collective-permute-start.3) | collective-permute-done | bytes 262176 | tf_op jit(solution)/shard_map/ppermute | solution.py:274
  14.6 2.2 %collective-permute-start.8 = (bf16[2,96,512]{2,1,0:T(8,128)(2,1)S(1)}, bf16[2,96,512]{2,1,0:T(8,128)(2,1)S(1)}, u32[]{:S(2)}, u32[]{:S(2)}) collective-permute-start(bf16[2,96,512]{2,1,0:T(8,128)(2,1)S(1)} %slice.58), channel_id=1, source_target_pairs={{0,16},{4,20},{8,24},{12,28},{16,0},{20,4},{24,8},{28,12},{1,17},{... | collective-permute-start | bytes 589832 | tf_op jit(solution)/shard_map/ppermute | solution.py:274
  16.7 2.7 %accumulate_first.1 = (f32[128,512]{1,0:T(8,128)S(1)}, bf16[8,2,2,512,128]{4,3,2,1,0:T(8,128)(2,1)S(1)}, bf16[256,256]{1,0:T(8,128)(2,1)S(1)}) custom-call(s32[8]{0:T(128)} %block_ref.1, bf16[1,2,4096,128]{3,2,1,0:T(8,128)(2,1)} %data_ref.1, bf16[1,2,4096,128]{3,2,1,0:T(8,128)(2,1)S(1)} %collective-permute-done.theirs_ref, ...), custom_call_target="tpu_custom_call" | custom-call | flops 536870912 | bytes 3145728 | tf_op jit(solution)/shard_map/accumulate_first/pallas_call | solution.py:139
  19.5 0.7 %collective-permute-done.4.refs_0_ = bf16[2,128,512]{2,1,0:T(8,128)(2,1)S(1)} collective-permute-done((bf16[2,128,512]{2,1,0:T(8,128)(2,1)S(1)}, bf16[2,128,512]{2,1,0:T(8,128)(2,1)S(1)}, u32[]{:S(2)}, u32[]{:S(2)}) %collective-permute-start.4) | collective-permute-done | bytes 262176 | tf_op jit(solution)/shard_map/ppermute | solution.py:274
  20.2 2.2 %collective-permute-start.5 = (bf16[4,32,512]{2,1,0:T(8,128)(2,1)S(1)}, bf16[4,32,512]{2,1,0:T(8,128)(2,1)S(1)}, u32[]{:S(2)}, u32[]{:S(2)}) collective-permute-start(bf16[4,32,512]{2,1,0:T(8,128)(2,1)S(1)} %last_rows.1), channel_id=1, source_target_pairs={{0,16},{4,20},{8,24},{12,28},{16,0},{20,4},{24,8},{28,12},{1,17},{... | collective-permute-start | bytes 393224 | tf_op jit(solution)/shard_map/ppermute | solution.py:274
  22.4 0.4 %accumulate.3.refs_2_.refs_3_ = f32[128,512]{1,0:T(8,128)S(1)} custom-call(bf16[2,128,512]{2,1,0:T(8,128)(2,1)S(1)} %collective-permute-done.4.refs_0_, bf16[2,128,512]{2,1,0:T(8,128)(2,1)S(1)} %collective-permute-done.6.refs_1_, bf16[8,2,2,512,128]{4,3,2,1,0:T(8,128)(2,1)S(1)} %get-tuple-element.17.refs_2_.refs_1_, f32[128,512]{1,0:T(8,128)S(1)} %get-tuple-element.18.refs_3_), custom_call_target="tpu_custom_call" | custom-call | flops 268435456 | bytes 1572864 | tf_op jit(solution)/shard_map/accumulate/pallas_call | solution.py:188
  22.8 1.1 %collective-permute-done.7.refs_0_ = bf16[2,96,512]{2,1,0:T(8,128)(2,1)S(1)} collective-permute-done((bf16[2,96,512]{2,1,0:T(8,128)(2,1)S(1)}, bf16[2,96,512]{2,1,0:T(8,128)(2,1)S(1)}, u32[]{:S(2)}, u32[]{:S(2)}) %collective-permute-start.7) | collective-permute-done | bytes 196640 | tf_op jit(solution)/shard_map/ppermute | solution.py:274
  23.9 0.5 %accumulate.5 = bf16[3,2,2,32,128]{4,3,2,1,0:T(8,128)(2,1)S(1)} custom-call(bf16[2,96,512]{2,1,0:T(8,128)(2,1)S(1)} %collective-permute-done.7.refs_0_, bf16[2,96,512]{2,1,0:T(8,128)(2,1)S(1)} %collective-permute-done.8.refs_1_, bf16[8,2,2,512,128]{4,3,2,1,0:T(8,128)(2,1)S(1)} %get-tuple-element.17.refs_2_.refs_1_, f32[128,512]{1,0:T(8,128)S(1)} %accumulate.3.refs_2_.refs_3_), custom_call_target="tpu_custom_call" | custom-call | flops 201326592 | bytes 1441792 | tf_op jit(solution)/shard_map/accumulate/pallas_call | solution.py:188
  24.4 3.9 %collective-permute-start.9 = (bf16[2,2,32,128]{3,2,1,0:T(8,128)(2,1)S(1)}, bf16[2,2,32,128]{3,2,1,0:T(8,128)(2,1)S(1)}, u32[]{:S(2)}, u32[]{:S(2)}) collective-permute-start(bf16[2,2,32,128]{3,2,1,0:T(8,128)(2,1)S(1)} %get-tuple-element.19), channel_id=1, source_target_pairs={{0,3},{1,2},{2,1},{3,0},{4,7},{5,6},{6,5},{7,4},{8,11},{9,10},{10,... | collective-permute-start | bytes 98312 | tf_op jit(solution)/shard_map/ppermute | solution.py:310
  28.3 0.6 %collective-permute-start.11 = (bf16[2,2,32,128]{3,2,1,0:T(8,128)(2,1)S(1)}, bf16[2,2,32,128]{3,2,1,0:T(8,128)(2,1)S(1)}, u32[]{:S(2)}, u32[]{:S(2)}) collective-permute-start(bf16[2,2,32,128]{3,2,1,0:T(8,128)(2,1)S(1)} %get-tuple-element.20), channel_id=1, source_target_pairs={{0,1},{1,0},{2,3},{3,2},{4,5},{5,4},{6,7},{7,6},{8,9},{9,8},{10,11... | collective-permute-start | bytes 98312 | tf_op jit(solution)/shard_map/ppermute | solution.py:310
  29.0 1.6 %collective-permute-done.9.refs_1_ = bf16[2,2,32,128]{3,2,1,0:T(8,128)(2,1)S(1)} collective-permute-done((bf16[2,2,32,128]{3,2,1,0:T(8,128)(2,1)S(1)}, bf16[2,2,32,128]{3,2,1,0:T(8,128)(2,1)S(1)}, u32[]{:S(2)}, u32[]{:S(2)}) %collective-permute-start.9) | collective-permute-done | bytes 32800 | tf_op jit(solution)/shard_map/ppermute | solution.py:310
  30.6 2.5 %collective-permute-done.10.refs_2_ = bf16[2,2,32,128]{3,2,1,0:T(8,128)(2,1)S(1)} collective-permute-done((bf16[2,2,32,128]{3,2,1,0:T(8,128)(2,1)S(1)}, bf16[2,2,32,128]{3,2,1,0:T(8,128)(2,1)S(1)}, u32[]{:S(2)}, u32[]{:S(2)}) %collective-permute-start.10) | collective-permute-done | bytes 32800 | tf_op jit(solution)/shard_map/ppermute | solution.py:310
  33.2 0.4 %accumulate.4 = bf16[1,2,2,32,128]{4,3,2,1,0:T(8,128)(2,1)S(1)} custom-call(bf16[4,32,512]{2,1,0:T(8,128)(2,1)S(1)} %collective-permute-done.5.refs_0_, bf16[8,2,2,512,128]{4,3,2,1,0:T(8,128)(2,1)S(1)} %get-tuple-element.17.refs_2_.refs_1_, f32[128,512]{1,0:T(8,128)S(1)} %accumulate.3.refs_2_.refs_3_), custom_call_target="tpu_custom_call" | custom-call | flops 67108864 | bytes 1179648 | tf_op jit(solution)/shard_map/accumulate/pallas_call | solution.py:188
  33.7 0.1 collective-permute-start.12
  33.7 1.7 %transform.2.refs_4_ = bf16[4,16,128,256]{3,2,1,0:T(8,128)(2,1)} custom-call(bf16[256,256]{1,0:T(8,128)(2,1)S(1)} %get-tuple-element.14.table_ref, bf16[2,2,32,128]{3,2,1,0:T(8,128)(2,1)S(1)} %bitcast.19, bf16[2,2,32,128]{3,2,1,0:T(8,128)(2,1)S(1)} %collective-permute-done.9.refs_1_, bf16[2,2,32,128]{3,2,1,0:T(8,128)(2,1)S(1)} %collective-permute-done.10.refs_2_, ...), custom_call_target="tpu_custom_call" | custom-call | tf_op jit(solution)/shard_map/transform/pallas_call | solution.py:256
  35.4 1.7 %transform.3 = bf16[4,16,128,256]{3,2,1,0:T(8,128)(2,1)} custom-call(bf16[256,256]{1,0:T(8,128)(2,1)S(1)} %get-tuple-element.14.table_ref, bf16[2,32,128]{2,1,0:T(8,128)(2,1)S(1)} %get-tuple-element.25.refs_0_, bf16[2,32,128]{2,1,0:T(8,128)(2,1)S(1)} %get-tuple-element.24.refs_1_, ...), custom_call_target="tpu_custom_call", output_to_operand_aliasing={{}: (5, {})} | custom-call | tf_op jit(solution)/shard_map/transform/pallas_call | solution.py:256
  (19 shorter events, 0.1 us)
Async XLA Ops:
  0.0 16.7 %collective-permute-start = (bf16[1,2,4096,128]{3,2,1,0:T(8,128)(2,1)}, bf16[1,2,4096,128]{3,2,1,0:T(8,128)(2,1)S(1)}, u32[]{:S(2)}, u32[]{:S(2)}) collective-permute-start(bf16[1,2,4096,128]{3,2,1,0:T(8,128)(2,1)} %data_ref.1), channel_id=1, source_target_pairs={{0,4},{4,0},{8,12},{12,8},{16,20},{20,16},{24,28},{28,24},{1,5},{5... | collective-permute-start | bytes 6291464 | tf_op jit(solution)/shard_map/ppermute | solution.py:274
  1.8 3.1 %collective-permute-start.1 = (bf16[2,128,512]{2,1,0:T(8,128)(2,1)S(1)}, bf16[2,128,512]{2,1,0:T(8,128)(2,1)S(1)}, u32[]{:S(2)}, u32[]{:S(2)}) collective-permute-start(bf16[2,128,512]{2,1,0:T(8,128)(2,1)S(1)} %get-tuple-element.13), channel_id=1, source_target_pairs={{0,4},{4,0},{8,12},{12,8},{16,20},{20,16},{24,28},{28,24},{1,5},{5... | collective-permute-start | bytes 786440 | tf_op jit(solution)/shard_map/ppermute | solution.py:274
  2.0 10.1 %collective-permute-start.2 = (bf16[2,128,512]{2,1,0:T(8,128)(2,1)S(1)}, bf16[2,128,512]{2,1,0:T(8,128)(2,1)S(1)}, u32[]{:S(2)}, u32[]{:S(2)}) collective-permute-start(bf16[2,128,512]{2,1,0:T(8,128)(2,1)S(1)} %get-tuple-element.12.refs_0_), channel_id=1, source_target_pairs={{0,16},{4,20},{8,24},{12,28},{16,0},{20,4},{24,8},{28,12},{1,17},{... | collective-permute-start | bytes 786440 | tf_op jit(solution)/shard_map/ppermute | solution.py:274
  4.9 9.6 %collective-permute-start.3 = (bf16[2,128,512]{2,1,0:T(8,128)(2,1)S(1)}, bf16[2,128,512]{2,1,0:T(8,128)(2,1)S(1)}, u32[]{:S(2)}, u32[]{:S(2)}) collective-permute-start(bf16[2,128,512]{2,1,0:T(8,128)(2,1)S(1)} %collective-permute-done.1.refs_1_), channel_id=1, source_target_pairs={{0,8},{4,12},{8,0},{12,4},{16,24},{20,28},{24,16},{28,20},{1,9},{5... | collective-permute-start | bytes 786440 | tf_op jit(solution)/shard_map/ppermute | solution.py:274
  7.5 12.7 %collective-permute-start.4 = (bf16[2,128,512]{2,1,0:T(8,128)(2,1)S(1)}, bf16[2,128,512]{2,1,0:T(8,128)(2,1)S(1)}, u32[]{:S(2)}, u32[]{:S(2)}) collective-permute-start(bf16[2,128,512]{2,1,0:T(8,128)(2,1)S(1)} %get-tuple-element.12.refs_0_), channel_id=1, source_target_pairs={{0,8},{4,12},{8,0},{12,4},{16,24},{20,28},{24,16},{28,20},{1,9},{5... | collective-permute-start | bytes 786440 | tf_op jit(solution)/shard_map/ppermute | solution.py:274
  7.5 14.8 %collective-permute-start.6 = (bf16[2,128,512]{2,1,0:T(8,128)(2,1)S(1)}, bf16[2,128,512]{2,1,0:T(8,128)(2,1)S(1)}, u32[]{:S(2)}, u32[]{:S(2)}) collective-permute-start(bf16[2,128,512]{2,1,0:T(8,128)(2,1)S(1)} %collective-permute-done.1.refs_1_), channel_id=1, source_target_pairs={{0,16},{4,20},{8,24},{12,28},{16,0},{20,4},{24,8},{28,12},{1,17},{... | collective-permute-start | bytes 786440 | tf_op jit(solution)/shard_map/ppermute | solution.py:274
  12.1 11.9 %collective-permute-start.7 = (bf16[2,96,512]{2,1,0:T(8,128)(2,1)S(1)}, bf16[2,96,512]{2,1,0:T(8,128)(2,1)S(1)}, u32[]{:S(2)}, u32[]{:S(2)}) collective-permute-start(bf16[2,96,512]{2,1,0:T(8,128)(2,1)S(1)} %slice.57), channel_id=1, source_target_pairs={{0,8},{4,12},{8,0},{12,4},{16,24},{20,28},{24,16},{28,20},{1,9},{5... | collective-permute-start | bytes 589832 | tf_op jit(solution)/shard_map/ppermute | solution.py:274
  14.6 9.3 %collective-permute-start.8 = (bf16[2,96,512]{2,1,0:T(8,128)(2,1)S(1)}, bf16[2,96,512]{2,1,0:T(8,128)(2,1)S(1)}, u32[]{:S(2)}, u32[]{:S(2)}) collective-permute-start(bf16[2,96,512]{2,1,0:T(8,128)(2,1)S(1)} %slice.58), channel_id=1, source_target_pairs={{0,16},{4,20},{8,24},{12,28},{16,0},{20,4},{24,8},{28,12},{1,17},{... | collective-permute-start | bytes 589832 | tf_op jit(solution)/shard_map/ppermute | solution.py:274
  20.2 13.0 %collective-permute-start.5 = (bf16[4,32,512]{2,1,0:T(8,128)(2,1)S(1)}, bf16[4,32,512]{2,1,0:T(8,128)(2,1)S(1)}, u32[]{:S(2)}, u32[]{:S(2)}) collective-permute-start(bf16[4,32,512]{2,1,0:T(8,128)(2,1)S(1)} %last_rows.1), channel_id=1, source_target_pairs={{0,16},{4,20},{8,24},{12,28},{16,0},{20,4},{24,8},{28,12},{1,17},{... | collective-permute-start | bytes 393224 | tf_op jit(solution)/shard_map/ppermute | solution.py:274
  24.4 6.2 %collective-permute-start.9 = (bf16[2,2,32,128]{3,2,1,0:T(8,128)(2,1)S(1)}, bf16[2,2,32,128]{3,2,1,0:T(8,128)(2,1)S(1)}, u32[]{:S(2)}, u32[]{:S(2)}) collective-permute-start(bf16[2,2,32,128]{3,2,1,0:T(8,128)(2,1)S(1)} %get-tuple-element.19), channel_id=1, source_target_pairs={{0,3},{1,2},{2,1},{3,0},{4,7},{5,6},{6,5},{7,4},{8,11},{9,10},{10,... | collective-permute-start | bytes 98312 | tf_op jit(solution)/shard_map/ppermute | solution.py:310
  28.3 4.8 %collective-permute-start.10 = (bf16[2,2,32,128]{3,2,1,0:T(8,128)(2,1)S(1)}, bf16[2,2,32,128]{3,2,1,0:T(8,128)(2,1)S(1)}, u32[]{:S(2)}, u32[]{:S(2)}) collective-permute-start(bf16[2,2,32,128]{3,2,1,0:T(8,128)(2,1)S(1)} %get-tuple-element.21), channel_id=1, source_target_pairs={{0,2},{1,3},{2,0},{3,1},{4,6},{5,7},{6,4},{7,5},{8,10},{9,11},{10,... | collective-permute-start | bytes 98312 | tf_op jit(solution)/shard_map/ppermute | solution.py:310
  28.3 4.8 %collective-permute-start.11 = (bf16[2,2,32,128]{3,2,1,0:T(8,128)(2,1)S(1)}, bf16[2,2,32,128]{3,2,1,0:T(8,128)(2,1)S(1)}, u32[]{:S(2)}, u32[]{:S(2)}) collective-permute-start(bf16[2,2,32,128]{3,2,1,0:T(8,128)(2,1)S(1)} %get-tuple-element.20), channel_id=1, source_target_pairs={{0,1},{1,0},{2,3},{3,2},{4,5},{5,4},{6,7},{7,6},{8,9},{9,8},{10,11... | collective-permute-start | bytes 98312 | tf_op jit(solution)/shard_map/ppermute | solution.py:310
  33.7 1.8 %collective-permute-start.12 = (bf16[4,2,32,128]{3,2,1,0:T(8,128)(2,1)S(1)}, bf16[4,2,32,128]{3,2,1,0:T(8,128)(2,1)S(1)}, u32[]{:S(2)}, u32[]{:S(2)}) collective-permute-start(bf16[4,2,32,128]{3,2,1,0:T(8,128)(2,1)S(1)} %pad_maximum_fusion), channel_id=1, source_target_pairs={{0,4},{4,0},{8,12},{12,8},{16,20},{20,16},{24,28},{28,24},{1,5},{5... | collective-permute-start | bytes 196616 | tf_op jit(solution)/shard_map/ppermute | solution.py:274

commit v4 on v3

--- a/solution.py
+++ b/solution.py
@@ -16,8 +16,8 @@
 PARAMS = pltpu.CompilerParams(vmem_limit_bytes=16 * 2**20)
 
 
-def flip_of(step, nf):
-    return (nf - step) % nf
+def shifts_of(nf):
+    return (nf - 1, *range(1, nf - 1))
 
 
 def order_rows(receivers, receiver_order, nf):
@@ -41,8 +41,8 @@
         copies[1].wait()
         for half, out in ((core, keep), (1 - core, give)):
             picks = []
-            for step in [*range(1, nf), 0]:
-                at = pl.multiple_of(jnp.bitwise_xor(z, flip_of(step, nf)) * quarter + half * count, UNIT)
+            for shift in (*shifts_of(nf), 0):
+                at = pl.multiple_of(lax.rem(z + shift, nf) * quarter + half * count, UNIT)
                 picks.append(hot[pl.ds(at, count), :])
             pick = jnp.concatenate(picks, axis=0)
             for part in range(two):
@@ -100,9 +100,9 @@
     )
 
 
-def accumulate_first(pieces, block_of_slot, data, theirs, tables, ns):
-    n = len(pieces)
-    two, rows, width = pieces[0][2].shape
+def accumulate_first(pieces, slots, block_of_slot, data, theirs, tables):
+    n, ns = len(pieces), len(slots)
+    two, rows, width = pieces[0].shape
     cols = data.shape[3]
 
     def kernel(block_ref, data_ref, theirs_ref, tables_ref, *refs):
@@ -114,26 +114,27 @@
         last = pltpu.make_async_copy(tables_ref.at[lax.axis_index("freq")], table, more.at[1])
         last.start()
         first.wait()
-        order = [2 * j + other for j, other, _ in pieces]
-        order += [i for i in range(ns) if i not in order]
-        copies = {}
-        for i in order:
-            slot = jnp.bitwise_xor(chip, i // 2) * 2 + (1 - core if i % 2 else core)
+        copies = []
+        for i, (even, odd, other) in enumerate(slots):
+            slot = jnp.bitwise_xor(chip, jnp.where(core == 0, even, odd)) * 2 + (1 - core if other else core)
             at = pl.multiple_of(block[slot] * width, width)
-            for side, ref in enumerate((data_ref, theirs_ref)):
-                copies[i, side] = pltpu.make_async_copy(
-                    ref.at[0, :, pl.ds(at, width), :], blocks.at[i, side], sems.at[i, side]
-                )
-                copies[i, side].start()
+            copies.append(
+                [
+                    pltpu.make_async_copy(ref.at[0, :, pl.ds(at, width), :], blocks.at[i, side], sems.at[i, side])
+                    for side, ref in enumerate((data_ref, theirs_ref))
+                ]
+            )
+            for copy in copies[-1]:
+                copy.start()
         total = None
-        for i, piece in zip(order, given):
-            for side in range(2):
-                copies[i, side].wait()
+        for i, piece in enumerate(given):
+            for copy in copies[i]:
+                copy.wait()
             total = products(total, piece, 0, slice(None), [(blocks[i, side, 0], blocks[i, side, 1]) for side in range(2)])
         out[...] = total
-        for i in order[n:]:
-            for side in range(2):
-                copies[i, side].wait()
+        for pair in copies[n:]:
+            for copy in pair:
+                copy.wait()
         last.wait()
 
     return pl.pallas_call(
@@ -153,20 +154,21 @@
         compiler_params=PARAMS,
         cost_estimate=cost_of(n, rows, width, cols),
         name="accumulate_first",
-    )(block_of_slot, data, theirs, tables, *(piece[2] for piece in pieces))
-
-
-def accumulate(pieces, blocks, old, rows, steps):
+    )(block_of_slot, data, theirs, tables, *pieces)
+
+
+def accumulate(pieces, blocks, old, rows, steps=0):
     arrays = []
     plan = []
-    for j, other, array, plane, lo in pieces:
+    for slot, array, plane, lo in pieces:
         if not any(array is held for held in arrays):
             arrays.append(array)
-        plan.append((2 * j + other, next(i for i, held in enumerate(arrays) if held is array), plane, lo))
+        plan.append((slot, next(i for i, held in enumerate(arrays) if held is array), plane, lo))
     n = len(arrays)
     width = arrays[0].shape[2]
     two, _, cols = blocks.shape[2:]
     before, at = old
+    size = rows // steps if steps else rows
 
     def kernel(*refs):
         given, (block_ref, old_ref, out) = refs[:n], refs[n:]
@@ -177,7 +179,6 @@
         if not steps:
             out[...] = total
             return
-        size = rows // steps
         total = total.astype(jnp.bfloat16)
         for step in range(steps):
             for side in range(2):
@@ -187,7 +188,7 @@
 
     return pl.pallas_call(
         kernel,
-        out_shape=jax.ShapeDtypeStruct((steps, 2, two, rows // steps, cols), jnp.bfloat16)
+        out_shape=jax.ShapeDtypeStruct((steps, 2, two, size, cols), jnp.bfloat16)
         if steps
         else jax.ShapeDtypeStruct((rows, 4 * cols), jnp.float32),
         in_specs=[VMEM] * (n + 2),
@@ -199,7 +200,7 @@
 
 
 def tables_of(nf):
-    freqs = np.arange(nf)[:, None] ^ np.array([flip_of(step, nf) for step in range(nf)])[None, :]
+    freqs = (np.arange(nf)[:, None] - np.array([0, *shifts_of(nf)])[None, :]) % nf
     bins = (2 * freqs + 1) * (NT // (4 * nf))
     phase = bins[:, :, None] * np.arange(NT) % NT
     angle = phase * (2.0 * math.pi / NT)
@@ -211,27 +212,41 @@
     return np.ascontiguousarray(both).reshape(nf, 4 * nf * UNIT, NT)
 
 
-def transform(table, spectra, side, other, quarter, out):
-    nf = len(spectra)
-    count, cols = spectra[0].shape[-2:]
+def settle(spectra):
+    n = len(spectra)
+
+    def kernel(*refs):
+        for side, out in enumerate(refs[n:]):
+            for i, ref in enumerate(refs[:n]):
+                out[i] = ref[side]
+
+    shape = jax.ShapeDtypeStruct((n, *spectra[0].shape[1:]), jnp.bfloat16)
+    return pl.pallas_call(
+        kernel,
+        out_shape=[shape, shape],
+        in_specs=[VMEM] * n,
+        out_specs=[VMEM, VMEM],
+        compiler_params=PARAMS,
+        name="settle",
+    )(*spectra)
+
+
+def transform(table, spectra, other, quarter, out):
+    nf, _, count, cols = spectra.shape
     groups = count // UNIT
     depth = table.shape[0]
     each = 4
     steps = UNIT // each
     first = out is None
 
-    def kernel(table_ref, *refs):
-        given = refs[:nf]
+    def kernel(table_ref, given, *refs):
         out_ref, held, sems = refs[-3:]
         core = lax.rem(lax.axis_index("src"), 2)
         half = 1 - core if other else core
         lhs = []
         for g in range(groups):
             rows = pl.ds(g * UNIT, UNIT)
-            x = jnp.concatenate(
-                [ref[part, rows, :] if side is None else ref[side, part, rows, :] for ref in given for part in range(2)],
-                axis=0,
-            )
+            x = jnp.concatenate([given[i, part, rows, :] for i in range(nf) for part in range(2)], axis=0)
             x = x.T
             lhs.append(jnp.concatenate([x, x], axis=1))
         lhs = jnp.concatenate(lhs, axis=0)
@@ -256,13 +271,13 @@
     return pl.pallas_call(
         kernel,
         out_shape=jax.ShapeDtypeStruct((quarter // UNIT, UNIT, cols, NT), jnp.bfloat16),
-        in_specs=[VMEM] * (1 + nf) + ([] if first else [ANY]),
+        in_specs=[VMEM] * 2 + ([] if first else [ANY]),
         out_specs=ANY,
         scratch_shapes=[pltpu.VMEM((groups, UNIT, cols, NT), jnp.bfloat16), pltpu.SemaphoreType.DMA((steps,))],
-        input_output_aliases={} if first else {nf + 1: 0},
+        input_output_aliases={} if first else {2: 0},
         compiler_params=PARAMS,
         name="transform",
-    )(table, *spectra, *([] if first else [out]))
+    )(table, spectra, *([] if first else [out]))
 
 
 def body(ns, nf, receivers, data, block_of_slot, receiver_order):
@@ -270,8 +285,9 @@
     chips = ns // 2
     quarter = rows // nf
 
-    def over(value, flip):
-        return lax.ppermute(value, "src", [(i, i ^ flip) for i in range(ns)])
+    def over(value, even, odd=None):
+        flips = (even, even if odd is None else odd)
+        return lax.ppermute(value, "src", [(i, i ^ flips[i % 2]) for i in range(ns)])
 
     def in_hbm(value):
         return pltpu.with_memory_space_constraint(value, pltpu.HBM)
@@ -279,40 +295,41 @@
     half = rows // 2
     size = half // nf
     lo = half - size
+    keep, give = order_rows(in_hbm(receivers), in_hbm(receiver_order.reshape(1, rows)), nf)
     theirs = over(data, 1)
-    keep, give = order_rows(in_hbm(receivers), in_hbm(receiver_order.reshape(1, rows)), nf)
     taken = over(give, 1)
-    b_keep = over(keep, 4)
-    a_taken = over(taken, 2)
-    a_keep = over(keep, 2)
-    b_taken = over(taken, 4)
-    first = [(0, 0, keep), (0, 1, taken), (2, 0, b_keep), (1, 1, a_taken)]
-    c_keep, c_taken = over(b_keep[:, :lo], 2), over(a_taken[:, :lo], 4)
-    sums, blocks, table = accumulate_first(
-        first, in_hbm(block_of_slot), in_hbm(data), theirs, in_hbm(jnp.asarray(tables_of(nf))), ns
-    )
-    a_keep, sums = lax.optimization_barrier((a_keep, sums))
-    c_near = over(last_rows([a_keep, a_taken], lo), 4)
-    second = [(1, 0, a_keep, 0, 0), (2, 1, b_taken, 0, 0)]
-    slots = [(*piece[:2], (piece[2], 0, 0), (piece[2], 0, lo)) for piece in first + second]
-    slots += [(3, 0, (c_keep, 0, 0), (c_near, 0, 0)), (3, 1, (c_taken, 0, 0), (c_near, 2, 0))]
+    y_then_x, x_then_y = (4, 2), (2, 4)
+    pairs = [(keep, taken)]
+    pairs += [tuple(over(value, *flips) for value in pairs[0]) for flips in (y_then_x, x_then_y)]
+    relays = [over(value[:, :lo], *x_then_y) for value in pairs[1]]
+    slots = [(even, odd, other) for even, odd in ((0, 0), (2, 1), (1, 2), (3, 3)) for other in range(2)]
+    whole = [value for pair in pairs for value in pair]
     while len(slots) < ns:
         step = len(slots) // 2
-        moved = {id(entry[0]): over(entry[0], 2 * step) for slot in slots for entry in slot[2:]}
-        slots += [
-            (step + j, other, *((moved[id(array)], plane, at) for array, plane, at in entries))
-            for j, other, *entries in slots
-        ]
-    far = [(j, other, *entry) for j, other, entry, _ in slots[6:]]
-    near = [(j, other, *entry) for j, other, _, entry in slots[6:]]
-    sums = accumulate(second, blocks, (sums, 0), half, 0)
-    ready = accumulate(far, blocks, (sums, 0), lo, nf - 1)
-    got = [lax.ppermute(ready[s - 1], "freq", [(i, i ^ flip_of(s, nf)) for i in range(nf)]) for s in range(1, nf)]
-    own = accumulate(near, blocks, (sums, lo), size, 1)
-    got = [own[0]] + got
-    crossed = over(jnp.stack([x[1] for x in got]), 1)
-    out = transform(table, got, 0, False, quarter, None)
-    out = transform(table, [crossed[s] for s in range(nf)], None, True, quarter, out)
+        slots += [(step + even, step + odd, other) for even, odd, other in slots]
+    sums, blocks, table = accumulate_first(
+        whole[:4], slots, in_hbm(block_of_slot), in_hbm(data), theirs, in_hbm(jnp.asarray(tables_of(nf)))
+    )
+    tied = lax.optimization_barrier((*pairs[1], sums, relays[0]))
+    sums = tied[2]
+    c_near = over(last_rows(tied[:2], lo), *x_then_y)
+    places = [((array, 0, 0), (array, 0, lo)) for array in whole]
+    places += [((array, 0, 0), (c_near, 2 * other, 0)) for other, array in enumerate(relays)]
+    while len(places) < ns:
+        step = len(places) // 2
+        moved = {id(entry[0]): over(entry[0], 2 * step) for place in places for entry in place}
+        places += [tuple((moved[id(array)], plane, at) for array, plane, at in place) for place in places]
+    sums = accumulate([(i, *places[i][0]) for i in (4, 5)], blocks, (sums, 0), half)
+    ready = accumulate([(i, *places[i][0]) for i in range(6, ns)], blocks, (sums, 0), lo, nf - 1)
+    own = accumulate([(i, *places[i][1]) for i in range(6, ns)], blocks, (sums, lo), size, 1)
+    got = [
+        lax.ppermute(ready[step], "freq", [(i, (i + shift) % nf) for i in range(nf)])
+        for step, shift in enumerate(shifts_of(nf))
+    ]
+    mine, other = settle([own[0], *got])
+    crossed = over(other, 1)
+    out = transform(table, mine, False, quarter, None)
+    out = transform(table, crossed, True, quarter, out)
     return out.reshape(quarter, *out.shape[2:])
 
 

time: 37.3 us -> 33.8 us (0.906)
  waiting for transfers between devices: 8.93 us -> 4.16 us
  starting transfers between devices: 19.2 us -> 20.5 us
    ppermute x13, waiting for transfers between devices: 8.93 us -> 4.16 us  [the longest x3 2.1 us: body(): lax.ppermute(ready[step], 'freq', [(i, (i + shift) % nf) for i in range(n...]
    ppermute x13, starting transfers between devices: 19.2 us -> 20.5 us  [the longest x10 15 us: over(): lax.ppermute(value, 'src', [(i, i ^ flips[i % 2]) for i in range(ns)])]
    pallas_call x3 -> x4, Pallas kernels: 1.37 us -> 1.38 us  [the longest x3 1.37 us: accumulate(): pl.pallas_call(kernel, out_shape=jax.ShapeDtypeStruct((steps, 2, two, siz...]
  transfers between devices with their start and end apart: 13 -> 13, of which waited for: 6 -> 4; matrix products, arithmetic and copies ran while one was open for 0% -> 0% of each run, Pallas kernels for 18% -> 21%
where the time goes in v4:
time: 33.8 us; the launch traced here: 33.6 us
  starting transfers between devices  20.5 us (61%)
  Pallas kernels  8.83 us (26%)
  waiting for transfers between devices  4.16 us (12%)
    ppermute x10, starting transfers between devices, over(): lax.ppermute(value, 'src', [(i, i ^ flips[i % 2]) for i in range(ns)])  15 us
    ppermute x3, starting transfers between devices, body(): lax.ppermute(ready[step], 'freq', [(i, (i + shift) % nf) for i in range(n...  5.5 us
    pallas_call x2, Pallas kernels, transform(): pl.pallas_call(kernel, out_shape=jax.ShapeDtypeStruct((quarter // UNIT, U...  3.34 us
    pallas_call x1, Pallas kernels, accumulate_first(): pl.pallas_call(kernel, out_shape=[jax.ShapeDtypeStruct((rows, 4 * cols),...  2.72 us
    ppermute x3, waiting for transfers between devices, body(): lax.ppermute(ready[step], 'freq', [(i, (i + shift) % nf) for i in range(n...  2.1 us
    ppermute x10, waiting for transfers between devices, over(): lax.ppermute(value, 'src', [(i, i ^ flips[i % 2]) for i in range(ns)])  2.07 us
    pallas_call x1, Pallas kernels, order_rows(): pl.pallas_call(kernel, out_shape=[shape, shape], in_specs=[ANY, ANY], out...  1.38 us
    pallas_call x3, Pallas kernels, accumulate(): pl.pallas_call(kernel, out_shape=jax.ShapeDtypeStruct((steps, 2, two, siz...  1.37 us
  transfers between devices with their start and end apart: 13, of which 4 were waited for; matrix products, arithmetic and copies ran while one was open for 0% of the time, Pallas kernels for 21%

profile of v4, /device:TPU:0, one launch (start us, length us, event | category | flops | bytes accessed | tf_op | source)
XLA Modules:
  0.0 33.6 jit_solution(8407202939919336214)
XLA Ops:
  0.0 0.5 %collective-permute-start = (bf16[1,2,4096,128]{3,2,1,0:T(8,128)(2,1)}, bf16[1,2,4096,128]{3,2,1,0:T(8,128)(2,1)S(1)}, u32[]{:S(2)}, u32[]{:S(2)}) collective-permute-start(bf16[1,2,4096,128]{3,2,1,0:T(8,128)(2,1)} %data_ref.1), channel_id=1, source_target_pairs={{0,4},{4,0},{8,12},{12,8},{16,20},{20,16},{24,28},{28,24},{1,5},{5... | collective-permute-start | bytes 6291464 | tf_op jit(solution)/shard_map/ppermute | solution.py:290
  0.5 1.4 %order_rows.1 = (bf16[2,128,512]{2,1,0:T(8,128)(2,1)S(1)}, bf16[2,128,512]{2,1,0:T(8,128)(2,1)S(1)}) custom-call(s32[1,256]{1,0:T(1,128)} %bitcast.10, bf16[1,1,2,256,512]{4,3,2,1,0:T(8,128)(2,1)} %g_ref.1), custom_call_target="tpu_custom_call" | custom-call | tf_op jit(solution)/shard_map/order_rows/pallas_call | solution.py:52
  1.8 0.1 collective-permute-start.1
  2.0 3.0 %collective-permute-start.2 = (bf16[2,128,512]{2,1,0:T(8,128)(2,1)S(1)}, bf16[2,128,512]{2,1,0:T(8,128)(2,1)S(1)}, u32[]{:S(2)}, u32[]{:S(2)}) collective-permute-start(bf16[2,128,512]{2,1,0:T(8,128)(2,1)S(1)} %get-tuple-element.15.refs_0_), channel_id=1, source_target_pairs={{0,16},{4,12},{8,24},{12,4},{16,0},{20,28},{24,8},{28,20},{1,17},{... | collective-permute-start | bytes 786440 | tf_op jit(solution)/shard_map/ppermute | solution.py:290
  4.9 2.6 %collective-permute-start.3 = (bf16[2,128,512]{2,1,0:T(8,128)(2,1)S(1)}, bf16[2,128,512]{2,1,0:T(8,128)(2,1)S(1)}, u32[]{:S(2)}, u32[]{:S(2)}) collective-permute-start(bf16[2,128,512]{2,1,0:T(8,128)(2,1)S(1)} %collective-permute-done.1.refs_1_), channel_id=1, source_target_pairs={{0,16},{4,12},{8,24},{12,4},{16,0},{20,28},{24,8},{28,20},{1,17},{... | collective-permute-start | bytes 786440 | tf_op jit(solution)/shard_map/ppermute | solution.py:290
  7.5 1.5 %collective-permute-start.6 = (bf16[2,128,512]{2,1,0:T(8,128)(2,1)S(1)}, bf16[2,128,512]{2,1,0:T(8,128)(2,1)S(1)}, u32[]{:S(2)}, u32[]{:S(2)}) collective-permute-start(bf16[2,128,512]{2,1,0:T(8,128)(2,1)S(1)} %get-tuple-element.15.refs_0_), channel_id=1, source_target_pairs={{0,8},{4,20},{8,0},{12,28},{16,24},{20,4},{24,16},{28,12},{1,9},{5... | collective-permute-start | bytes 786440 | tf_op jit(solution)/shard_map/ppermute | solution.py:290
  9.0 0.5 %collective-permute-start.7 = (bf16[2,128,512]{2,1,0:T(8,128)(2,1)S(1)}, bf16[2,128,512]{2,1,0:T(8,128)(2,1)S(1)}, u32[]{:S(2)}, u32[]{:S(2)}) collective-permute-start(bf16[2,128,512]{2,1,0:T(8,128)(2,1)S(1)} %collective-permute-done.1.refs_1_), channel_id=1, source_target_pairs={{0,8},{4,20},{8,0},{12,28},{16,24},{20,4},{24,16},{28,12},{1,9},{5... | collective-permute-start | bytes 786440 | tf_op jit(solution)/shard_map/ppermute | solution.py:290
  9.6 2.8 %collective-permute-start.4 = (bf16[2,96,512]{2,1,0:T(8,128)(2,1)S(1)}, bf16[2,96,512]{2,1,0:T(8,128)(2,1)S(1)}, u32[]{:S(2)}, u32[]{:S(2)}) collective-permute-start(bf16[2,96,512]{2,1,0:T(8,128)(2,1)S(1)} %slice.20), channel_id=1, source_target_pairs={{0,8},{4,20},{8,0},{12,28},{16,24},{20,4},{24,16},{28,12},{1,9},{5... | collective-permute-start | bytes 589832 | tf_op jit(solution)/shard_map/ppermute | solution.py:290
  12.3 1.9 %collective-permute-done.3.refs_3_.refs_1_ = bf16[2,128,512]{2,1,0:T(8,128)(2,1)S(1)} collective-permute-done((bf16[2,128,512]{2,1,0:T(8,128)(2,1)S(1)}, bf16[2,128,512]{2,1,0:T(8,128)(2,1)S(1)}, u32[]{:S(2)}, u32[]{:S(2)}) %collective-permute-start.3) | collective-permute-done | bytes 262176 | tf_op jit(solution)/shard_map/ppermute | solution.py:290
  14.3 3.7 %collective-permute-start.8 = (bf16[2,96,512]{2,1,0:T(8,128)(2,1)S(1)}, bf16[2,96,512]{2,1,0:T(8,128)(2,1)S(1)}, u32[]{:S(2)}, u32[]{:S(2)}) collective-permute-start(bf16[2,96,512]{2,1,0:T(8,128)(2,1)S(1)} %slice.21), channel_id=1, source_target_pairs={{0,8},{4,20},{8,0},{12,28},{16,24},{20,4},{24,16},{28,12},{1,9},{5... | collective-permute-start | bytes 589832 | tf_op jit(solution)/shard_map/ppermute | solution.py:290
  18.0 2.7 %accumulate_first.1 = (f32[128,512]{1,0:T(8,128)S(1)}, bf16[8,2,2,512,128]{4,3,2,1,0:T(8,128)(2,1)S(1)}, bf16[256,256]{1,0:T(8,128)(2,1)S(1)}) custom-call(s32[8]{0:T(128)} %block_ref.1, bf16[1,2,4096,128]{3,2,1,0:T(8,128)(2,1)} %data_ref.1, bf16[1,2,4096,128]{3,2,1,0:T(8,128)(2,1)S(1)} %collective-permute-done.theirs_ref, ...), custom_call_target="tpu_custom_call" | custom-call | flops 536870912 | bytes 3145728 | tf_op jit(solution)/shard_map/accumulate_first/pallas_call | solution.py:140
  20.7 0.3 collective-permute-start.5
  21.0 0.4 %accumulate.3.refs_2_.refs_3_ = f32[128,512]{1,0:T(8,128)S(1)} custom-call(bf16[2,128,512]{2,1,0:T(8,128)(2,1)S(1)} %collective-permute-done.6.refs_0_, bf16[2,128,512]{2,1,0:T(8,128)(2,1)S(1)} %collective-permute-done.7.refs_1_, bf16[8,2,2,512,128]{4,3,2,1,0:T(8,128)(2,1)S(1)} %get-tuple-element.21.refs_2_.refs_1_, f32[128,512]{1,0:T(8,128)S(1)} %get-tuple-element.22.refs_3_), custom_call_target="tpu_custom_call" | custom-call | flops 268435456 | bytes 1572864 | tf_op jit(solution)/shard_map/accumulate/pallas_call | solution.py:189
  21.5 0.1 collective-permute-done.8.refs_1_
  21.6 0.5 %accumulate.5 = bf16[3,2,2,32,128]{4,3,2,1,0:T(8,128)(2,1)S(1)} custom-call(bf16[2,96,512]{2,1,0:T(8,128)(2,1)S(1)} %collective-permute-done.4.refs_0_, bf16[2,96,512]{2,1,0:T(8,128)(2,1)S(1)} %collective-permute-done.8.refs_1_, bf16[8,2,2,512,128]{4,3,2,1,0:T(8,128)(2,1)S(1)} %get-tuple-element.21.refs_2_.refs_1_, f32[128,512]{1,0:T(8,128)S(1)} %accumulate.3.refs_2_.refs_3_), custom_call_target="tpu_custom_call" | custom-call | flops 201326592 | bytes 1441792 | tf_op jit(solution)/shard_map/accumulate/pallas_call | solution.py:189
  22.1 1.6 %collective-permute-start.10 = (bf16[2,2,32,128]{3,2,1,0:T(8,128)(2,1)S(1)}, bf16[2,2,32,128]{3,2,1,0:T(8,128)(2,1)S(1)}, u32[]{:S(2)}, u32[]{:S(2)}) collective-permute-start(bf16[2,2,32,128]{3,2,1,0:T(8,128)(2,1)S(1)} %get-tuple-element.26), channel_id=1, source_target_pairs={{0,1},{1,2},{2,3},{3,0},{4,5},{5,6},{6,7},{7,4},{8,9},{9,10},{10,1... | collective-permute-start | bytes 98312 | tf_op jit(solution)/shard_map/ppermute | solution.py:326
  23.7 2.6 %collective-permute-start.11 = (bf16[2,2,32,128]{3,2,1,0:T(8,128)(2,1)S(1)}, bf16[2,2,32,128]{3,2,1,0:T(8,128)(2,1)S(1)}, u32[]{:S(2)}, u32[]{:S(2)}) collective-permute-start(bf16[2,2,32,128]{3,2,1,0:T(8,128)(2,1)S(1)} %get-tuple-element.25), channel_id=1, source_target_pairs={{0,2},{1,3},{2,0},{3,1},{4,6},{5,7},{6,4},{7,5},{8,10},{9,11},{10,... | collective-permute-start | bytes 98312 | tf_op jit(solution)/shard_map/ppermute | solution.py:326
  26.2 1.4 %collective-permute-start.9 = (bf16[2,2,32,128]{3,2,1,0:T(8,128)(2,1)S(1)}, bf16[2,2,32,128]{3,2,1,0:T(8,128)(2,1)S(1)}, u32[]{:S(2)}, u32[]{:S(2)}) collective-permute-start(bf16[2,2,32,128]{3,2,1,0:T(8,128)(2,1)S(1)} %get-tuple-element.27), channel_id=1, source_target_pairs={{0,3},{1,0},{2,1},{3,2},{4,7},{5,4},{6,5},{7,6},{8,11},{9,8},{10,9... | collective-permute-start | bytes 98312 | tf_op jit(solution)/shard_map/ppermute | solution.py:326
  27.6 0.4 %accumulate.4 = bf16[1,2,2,32,128]{4,3,2,1,0:T(8,128)(2,1)S(1)} custom-call(bf16[4,32,512]{2,1,0:T(8,128)(2,1)S(1)} %collective-permute-done.5.refs_0_, bf16[8,2,2,512,128]{4,3,2,1,0:T(8,128)(2,1)S(1)} %get-tuple-element.21.refs_2_.refs_1_, f32[128,512]{1,0:T(8,128)S(1)} %accumulate.3.refs_2_.refs_3_), custom_call_target="tpu_custom_call" | custom-call | flops 67108864 | bytes 1179648 | tf_op jit(solution)/shard_map/accumulate/pallas_call | solution.py:189
  28.1 0.6 %collective-permute-done.11.refs_3_ = bf16[2,2,32,128]{3,2,1,0:T(8,128)(2,1)S(1)} collective-permute-done((bf16[2,2,32,128]{3,2,1,0:T(8,128)(2,1)S(1)}, bf16[2,2,32,128]{3,2,1,0:T(8,128)(2,1)S(1)}, u32[]{:S(2)}, u32[]{:S(2)}) %collective-permute-start.11) | collective-permute-done | bytes 32800 | tf_op jit(solution)/shard_map/ppermute | solution.py:326
  28.7 1.5 %collective-permute-done.9.refs_1_ = bf16[2,2,32,128]{3,2,1,0:T(8,128)(2,1)S(1)} collective-permute-done((bf16[2,2,32,128]{3,2,1,0:T(8,128)(2,1)S(1)}, bf16[2,2,32,128]{3,2,1,0:T(8,128)(2,1)S(1)}, u32[]{:S(2)}, u32[]{:S(2)}) %collective-permute-start.9) | collective-permute-done | bytes 32800 | tf_op jit(solution)/shard_map/ppermute | solution.py:326
  30.2 0.1 collective-permute-start.12
  30.3 1.7 %transform.2.refs_0_ = bf16[4,16,128,256]{3,2,1,0:T(8,128)(2,1)} custom-call(bf16[256,256]{1,0:T(8,128)(2,1)S(1)} %get-tuple-element.17.table_ref, bf16[4,2,32,128]{3,2,1,0:T(8,128)(2,1)S(1)} %get-tuple-element.24.given), custom_call_target="tpu_custom_call" | custom-call | tf_op jit(solution)/shard_map/transform/pallas_call | solution.py:271
  31.9 1.7 %transform.3 = bf16[4,16,128,256]{3,2,1,0:T(8,128)(2,1)} custom-call(bf16[256,256]{1,0:T(8,128)(2,1)S(1)} %get-tuple-element.17.table_ref, bf16[4,2,32,128]{3,2,1,0:T(8,128)(2,1)S(1)} %collective-permute-done.12.given, bf16[4,16,128,256]{3,2,1,0:T(8,128)(2,1)} %transform.2.refs_0_), custom_call_target="tpu_custom_call", output_to_operand_aliasing={{}: (2, {})} | custom-call | tf_op jit(solution)/shard_map/transform/pallas_call | solution.py:271
  (14 shorter events, 0.1 us)
Async XLA Ops:
  0.0 18.0 %collective-permute-start = (bf16[1,2,4096,128]{3,2,1,0:T(8,128)(2,1)}, bf16[1,2,4096,128]{3,2,1,0:T(8,128)(2,1)S(1)}, u32[]{:S(2)}, u32[]{:S(2)}) collective-permute-start(bf16[1,2,4096,128]{3,2,1,0:T(8,128)(2,1)} %data_ref.1), channel_id=1, source_target_pairs={{0,4},{4,0},{8,12},{12,8},{16,20},{20,16},{24,28},{28,24},{1,5},{5... | collective-permute-start | bytes 6291464 | tf_op jit(solution)/shard_map/ppermute | solution.py:290
  1.8 3.1 %collective-permute-start.1 = (bf16[2,128,512]{2,1,0:T(8,128)(2,1)S(1)}, bf16[2,128,512]{2,1,0:T(8,128)(2,1)S(1)}, u32[]{:S(2)}, u32[]{:S(2)}) collective-permute-start(bf16[2,128,512]{2,1,0:T(8,128)(2,1)S(1)} %get-tuple-element.16), channel_id=1, source_target_pairs={{0,4},{4,0},{8,12},{12,8},{16,20},{20,16},{24,28},{28,24},{1,5},{5... | collective-permute-start | bytes 786440 | tf_op jit(solution)/shard_map/ppermute | solution.py:290
  2.0 7.6 %collective-permute-start.2 = (bf16[2,128,512]{2,1,0:T(8,128)(2,1)S(1)}, bf16[2,128,512]{2,1,0:T(8,128)(2,1)S(1)}, u32[]{:S(2)}, u32[]{:S(2)}) collective-permute-start(bf16[2,128,512]{2,1,0:T(8,128)(2,1)S(1)} %get-tuple-element.15.refs_0_), channel_id=1, source_target_pairs={{0,16},{4,12},{8,24},{12,4},{16,0},{20,28},{24,8},{28,20},{1,17},{... | collective-permute-start | bytes 786440 | tf_op jit(solution)/shard_map/ppermute | solution.py:290
  4.9 9.3 %collective-permute-start.3 = (bf16[2,128,512]{2,1,0:T(8,128)(2,1)S(1)}, bf16[2,128,512]{2,1,0:T(8,128)(2,1)S(1)}, u32[]{:S(2)}, u32[]{:S(2)}) collective-permute-start(bf16[2,128,512]{2,1,0:T(8,128)(2,1)S(1)} %collective-permute-done.1.refs_1_), channel_id=1, source_target_pairs={{0,16},{4,12},{8,24},{12,4},{16,0},{20,28},{24,8},{28,20},{1,17},{... | collective-permute-start | bytes 786440 | tf_op jit(solution)/shard_map/ppermute | solution.py:290
  7.5 13.5 %collective-permute-start.6 = (bf16[2,128,512]{2,1,0:T(8,128)(2,1)S(1)}, bf16[2,128,512]{2,1,0:T(8,128)(2,1)S(1)}, u32[]{:S(2)}, u32[]{:S(2)}) collective-permute-start(bf16[2,128,512]{2,1,0:T(8,128)(2,1)S(1)} %get-tuple-element.15.refs_0_), channel_id=1, source_target_pairs={{0,8},{4,20},{8,0},{12,28},{16,24},{20,4},{24,16},{28,12},{1,9},{5... | collective-permute-start | bytes 786440 | tf_op jit(solution)/shard_map/ppermute | solution.py:290
  9.0 12.0 %collective-permute-start.7 = (bf16[2,128,512]{2,1,0:T(8,128)(2,1)S(1)}, bf16[2,128,512]{2,1,0:T(8,128)(2,1)S(1)}, u32[]{:S(2)}, u32[]{:S(2)}) collective-permute-start(bf16[2,128,512]{2,1,0:T(8,128)(2,1)S(1)} %collective-permute-done.1.refs_1_), channel_id=1, source_target_pairs={{0,8},{4,20},{8,0},{12,28},{16,24},{20,4},{24,16},{28,12},{1,9},{5... | collective-permute-start | bytes 786440 | tf_op jit(solution)/shard_map/ppermute | solution.py:290
  9.6 11.1 %collective-permute-start.4 = (bf16[2,96,512]{2,1,0:T(8,128)(2,1)S(1)}, bf16[2,96,512]{2,1,0:T(8,128)(2,1)S(1)}, u32[]{:S(2)}, u32[]{:S(2)}) collective-permute-start(bf16[2,96,512]{2,1,0:T(8,128)(2,1)S(1)} %slice.20), channel_id=1, source_target_pairs={{0,8},{4,20},{8,0},{12,28},{16,24},{20,4},{24,16},{28,12},{1,9},{5... | collective-permute-start | bytes 589832 | tf_op jit(solution)/shard_map/ppermute | solution.py:290
  14.3 7.4 %collective-permute-start.8 = (bf16[2,96,512]{2,1,0:T(8,128)(2,1)S(1)}, bf16[2,96,512]{2,1,0:T(8,128)(2,1)S(1)}, u32[]{:S(2)}, u32[]{:S(2)}) collective-permute-start(bf16[2,96,512]{2,1,0:T(8,128)(2,1)S(1)} %slice.21), channel_id=1, source_target_pairs={{0,8},{4,20},{8,0},{12,28},{16,24},{20,4},{24,16},{28,12},{1,9},{5... | collective-permute-start | bytes 589832 | tf_op jit(solution)/shard_map/ppermute | solution.py:290
  20.7 6.9 %collective-permute-start.5 = (bf16[4,32,512]{2,1,0:T(8,128)(2,1)S(1)}, bf16[4,32,512]{2,1,0:T(8,128)(2,1)S(1)}, u32[]{:S(2)}, u32[]{:S(2)}) collective-permute-start(bf16[4,32,512]{2,1,0:T(8,128)(2,1)S(1)} %last_rows.1), channel_id=1, source_target_pairs={{0,8},{4,20},{8,0},{12,28},{16,24},{20,4},{24,16},{28,12},{1,9},{5... | collective-permute-start | bytes 393224 | tf_op jit(solution)/shard_map/ppermute | solution.py:290
  22.1 6.0 %collective-permute-start.10 = (bf16[2,2,32,128]{3,2,1,0:T(8,128)(2,1)S(1)}, bf16[2,2,32,128]{3,2,1,0:T(8,128)(2,1)S(1)}, u32[]{:S(2)}, u32[]{:S(2)}) collective-permute-start(bf16[2,2,32,128]{3,2,1,0:T(8,128)(2,1)S(1)} %get-tuple-element.26), channel_id=1, source_target_pairs={{0,1},{1,2},{2,3},{3,0},{4,5},{5,6},{6,7},{7,4},{8,9},{9,10},{10,1... | collective-permute-start | bytes 98312 | tf_op jit(solution)/shard_map/ppermute | solution.py:326
  23.7 5.0 %collective-permute-start.11 = (bf16[2,2,32,128]{3,2,1,0:T(8,128)(2,1)S(1)}, bf16[2,2,32,128]{3,2,1,0:T(8,128)(2,1)S(1)}, u32[]{:S(2)}, u32[]{:S(2)}) collective-permute-start(bf16[2,2,32,128]{3,2,1,0:T(8,128)(2,1)S(1)} %get-tuple-element.25), channel_id=1, source_target_pairs={{0,2},{1,3},{2,0},{3,1},{4,6},{5,7},{6,4},{7,5},{8,10},{9,11},{10,... | collective-permute-start | bytes 98312 | tf_op jit(solution)/shard_map/ppermute | solution.py:326
  26.2 3.9 %collective-permute-start.9 = (bf16[2,2,32,128]{3,2,1,0:T(8,128)(2,1)S(1)}, bf16[2,2,32,128]{3,2,1,0:T(8,128)(2,1)S(1)}, u32[]{:S(2)}, u32[]{:S(2)}) collective-permute-start(bf16[2,2,32,128]{3,2,1,0:T(8,128)(2,1)S(1)} %get-tuple-element.27), channel_id=1, source_target_pairs={{0,3},{1,0},{2,1},{3,2},{4,7},{5,4},{6,5},{7,6},{8,11},{9,8},{10,9... | collective-permute-start | bytes 98312 | tf_op jit(solution)/shard_map/ppermute | solution.py:326
  30.2 1.8 %collective-permute-start.12 = (bf16[4,2,32,128]{3,2,1,0:T(8,128)(2,1)S(1)}, bf16[4,2,32,128]{3,2,1,0:T(8,128)(2,1)S(1)}, u32[]{:S(2)}, u32[]{:S(2)}) collective-permute-start(bf16[4,2,32,128]{3,2,1,0:T(8,128)(2,1)S(1)} %get-tuple-element.23), channel_id=1, source_target_pairs={{0,4},{4,0},{8,12},{12,8},{16,20},{20,16},{24,28},{28,24},{1,5},{5... | collective-permute-start | bytes 196616 | tf_op jit(solution)/shard_map/ppermute | solution.py:290

commit v5 on v4

--- a/solution.py
+++ b/solution.py
@@ -11,13 +11,14 @@
 
 NT = 256
 UNIT = 16
+EACH = 4
 VMEM = pl.BlockSpec(memory_space=pltpu.VMEM)
 ANY = pl.BlockSpec(memory_space=pl.ANY)
 PARAMS = pltpu.CompilerParams(vmem_limit_bytes=16 * 2**20)
 
 
 def shifts_of(nf):
-    return (nf - 1, *range(1, nf - 1))
+    return tuple(reversed(range(1, nf)))
 
 
 def order_rows(receivers, receiver_order, nf):
@@ -65,21 +66,21 @@
     )(receiver_order, receivers)
 
 
-def last_rows(arrays, lo):
+def join_rows(arrays, lo, hi):
     n = len(arrays)
-    planes, rows, width = arrays[0].shape
+    planes, _, width = arrays[0].shape
 
     def kernel(*refs):
         for i, ref in enumerate(refs[:n]):
-            refs[n][i * planes : (i + 1) * planes] = ref[:, lo:, :]
-
-    return pl.pallas_call(
-        kernel,
-        out_shape=jax.ShapeDtypeStruct((n * planes, rows - lo, width), jnp.bfloat16),
+            refs[n][i * planes : (i + 1) * planes] = ref[:, lo:hi, :]
+
+    return pl.pallas_call(
+        kernel,
+        out_shape=jax.ShapeDtypeStruct((n * planes, hi - lo, width), jnp.bfloat16),
         in_specs=[VMEM] * n,
         out_specs=VMEM,
         compiler_params=PARAMS,
-        name="last_rows",
+        name="join_rows",
     )(*arrays)
 
 
@@ -100,13 +101,11 @@
     )
 
 
-def accumulate_first(pieces, slots, block_of_slot, data, theirs, tables):
-    n, ns = len(pieces), len(slots)
-    two, rows, width = pieces[0].shape
-    cols = data.shape[3]
-
-    def kernel(block_ref, data_ref, theirs_ref, tables_ref, *refs):
-        given, (out, blocks, table, block, sems, more) = refs[:n], refs[n:]
+def pick_blocks(slots, block_of_slot, data, theirs, tables, width):
+    ns = len(slots)
+    two, _, cols = data.shape[1:]
+
+    def kernel(block_ref, data_ref, theirs_ref, tables_ref, blocks, table, block, sems, more):
         me = lax.axis_index("src")
         chip, core = me // 2, lax.rem(me, 2)
         first = pltpu.make_async_copy(block_ref, block, more.at[0])
@@ -114,47 +113,34 @@
         last = pltpu.make_async_copy(tables_ref.at[lax.axis_index("freq")], table, more.at[1])
         last.start()
         first.wait()
-        copies = []
+        copies = [last]
         for i, (even, odd, other) in enumerate(slots):
             slot = jnp.bitwise_xor(chip, jnp.where(core == 0, even, odd)) * 2 + (1 - core if other else core)
             at = pl.multiple_of(block[slot] * width, width)
-            copies.append(
-                [
-                    pltpu.make_async_copy(ref.at[0, :, pl.ds(at, width), :], blocks.at[i, side], sems.at[i, side])
-                    for side, ref in enumerate((data_ref, theirs_ref))
-                ]
-            )
-            for copy in copies[-1]:
+            for side, ref in enumerate((data_ref, theirs_ref)):
+                copy = pltpu.make_async_copy(ref.at[0, :, pl.ds(at, width), :], blocks.at[i, side], sems.at[i, side])
                 copy.start()
-        total = None
-        for i, piece in enumerate(given):
-            for copy in copies[i]:
-                copy.wait()
-            total = products(total, piece, 0, slice(None), [(blocks[i, side, 0], blocks[i, side, 1]) for side in range(2)])
-        out[...] = total
-        for pair in copies[n:]:
-            for copy in pair:
-                copy.wait()
-        last.wait()
+                copies.append(copy)
+        for copy in copies:
+            copy.wait()
 
     return pl.pallas_call(
         kernel,
         out_shape=[
-            jax.ShapeDtypeStruct((rows, 4 * cols), jnp.float32),
             jax.ShapeDtypeStruct((ns, 2, two, width, cols), jnp.bfloat16),
             jax.ShapeDtypeStruct(tables.shape[1:], jnp.bfloat16),
         ],
-        in_specs=[ANY] * 4 + [VMEM] * n,
-        out_specs=[VMEM] * 3,
+        in_specs=[ANY] * 4,
+        out_specs=[VMEM] * 2,
         scratch_shapes=[
             pltpu.SMEM((ns,), jnp.int32),
             pltpu.SemaphoreType.DMA((ns, 2)),
             pltpu.SemaphoreType.DMA((2,)),
         ],
         compiler_params=PARAMS,
-        cost_estimate=cost_of(n, rows, width, cols),
-        name="accumulate_first",
-    )(block_of_slot, data, theirs, tables, *pieces)
+        cost_estimate=pl.CostEstimate(flops=0, bytes_accessed=0, transcendentals=0),
+        name="pick_blocks",
+    )(block_of_slot, data, theirs, tables)
 
 
 def accumulate(pieces, blocks, old, rows, steps=0):
@@ -167,12 +153,12 @@
     n = len(arrays)
     width = arrays[0].shape[2]
     two, _, cols = blocks.shape[2:]
-    before, at = old
+    before, at = old or (None, 0)
     size = rows // steps if steps else rows
 
     def kernel(*refs):
-        given, (block_ref, old_ref, out) = refs[:n], refs[n:]
-        total = old_ref[at : at + rows, :]
+        given, block_ref, more, out = refs[:n], refs[n], refs[n + 1 : -1], refs[-1]
+        total = more[0][at : at + rows, :] if more else None
         for i, which, plane, lo in plan:
             sides = [(block_ref[i, side, 0], block_ref[i, side, 1]) for side in range(2)]
             total = products(total, given[which], plane, slice(lo, lo + rows), sides)
@@ -191,12 +177,12 @@
         out_shape=jax.ShapeDtypeStruct((steps, 2, two, size, cols), jnp.bfloat16)
         if steps
         else jax.ShapeDtypeStruct((rows, 4 * cols), jnp.float32),
-        in_specs=[VMEM] * (n + 2),
+        in_specs=[VMEM] * (n + 1 + (old is not None)),
         out_specs=VMEM,
         compiler_params=PARAMS,
         cost_estimate=cost_of(len(plan), rows, width, cols),
         name="accumulate",
-    )(*arrays, blocks, before)
+    )(*arrays, blocks, *(() if old is None else (before,)))
 
 
 def tables_of(nf):
@@ -231,36 +217,90 @@
     )(*spectra)
 
 
-def transform(table, spectra, other, quarter, out):
+def trace_rows(table_ref, given):
+    nf, two, count, cols = given.shape
+    groups = count // UNIT
+    wide = NT // 2
+    lhs = []
+    for g in range(groups):
+        x = jnp.concatenate([given[i, part, g * UNIT : (g + 1) * UNIT, :] for i in range(nf) for part in range(two)], axis=0)
+        x = x.T
+        lhs.append(jnp.concatenate([x, x], axis=1))
+    lhs = jnp.concatenate(lhs, axis=0)
+    full = table_ref[:, :wide]
+    row = lax.rem(lax.broadcasted_iota(jnp.int32, full.shape, 0), UNIT)
+    zero = jnp.zeros_like(full)
+
+    def some(rows, held, at):
+        for i in range(0, len(rows), 2):
+            rhs = jnp.concatenate([jnp.where(row == r, full, zero) for r in rows[i : i + 2]], axis=1)
+            res = jnp.dot(lhs, rhs, preferred_element_type=jnp.float32).astype(jnp.bfloat16)
+            for j in range(2):
+                part = res[:, j * wide : (j + 1) * wide].reshape(groups, cols, wide)
+                held[:, at + i + j, :, :wide] = part
+                held[:, at + i + j, :, wide:] = part
+
+    return some
+
+
+def transform_first(table, spectra, quarter):
     nf, _, count, cols = spectra.shape
     groups = count // UNIT
-    depth = table.shape[0]
-    each = 4
-    steps = UNIT // each
-    first = out is None
-
-    def kernel(table_ref, given, *refs):
-        out_ref, held, sems = refs[-3:]
+    early = UNIT // 2
+
+    def kernel(table_ref, given, out_ref, rest, held, sems):
         core = lax.rem(lax.axis_index("src"), 2)
-        half = 1 - core if other else core
-        lhs = []
-        for g in range(groups):
-            rows = pl.ds(g * UNIT, UNIT)
-            x = jnp.concatenate([given[i, part, rows, :] for i in range(nf) for part in range(2)], axis=0)
-            x = x.T
-            lhs.append(jnp.concatenate([x, x], axis=1))
-        lhs = jnp.concatenate(lhs, axis=0)
-        row = lax.rem(lax.broadcasted_iota(jnp.int32, (depth, NT), 0), UNIT)
-        full = table_ref[...]
+        some = trace_rows(table_ref, given)
         copies = []
-        for step in range(steps):
-            for r in range(step * each, (step + 1) * each):
-                rhs = jnp.where(row == r, full, jnp.zeros_like(full))
-                res = jnp.dot(lhs, rhs, preferred_element_type=jnp.float32).astype(jnp.bfloat16)
-                held[:, r] = res.reshape(groups, cols, NT)
+        for step in range(early // EACH):
+            some(range(step * EACH, (step + 1) * EACH), held, step * EACH)
             copy = pltpu.make_async_copy(
-                held.at[:, pl.ds(step * each, each)],
-                out_ref.at[pl.ds(half * groups, groups), pl.ds(step * each, each)],
+                held.at[:, pl.ds(step * EACH, EACH)],
+                out_ref.at[pl.ds(core * groups, groups), pl.ds(step * EACH, EACH)],
+                sems.at[step],
+            )
+            copy.start()
+            copies.append(copy)
+        some(range(early, UNIT), rest, 0)
+        for copy in copies:
+            copy.wait()
+
+    return pl.pallas_call(
+        kernel,
+        out_shape=[
+            jax.ShapeDtypeStruct((quarter // UNIT, UNIT, cols, NT), jnp.bfloat16),
+            jax.ShapeDtypeStruct((groups, UNIT - early, cols, NT), jnp.bfloat16),
+        ],
+        in_specs=[VMEM] * 2,
+        out_specs=[ANY, VMEM],
+        scratch_shapes=[
+            pltpu.VMEM((groups, early, cols, NT), jnp.bfloat16),
+            pltpu.SemaphoreType.DMA((early // EACH,)),
+        ],
+        compiler_params=PARAMS,
+        name="transform_first",
+    )(table, spectra)
+
+
+def transform_rest(table, spectra, out, rest):
+    nf, _, count, cols = spectra.shape
+    groups = count // UNIT
+    late = rest.shape[1]
+
+    def kernel(table_ref, given, rest_ref, _, out_ref, held, sems):
+        core = lax.rem(lax.axis_index("src"), 2)
+        copies = [
+            pltpu.make_async_copy(
+                rest_ref, out_ref.at[pl.ds(core * groups, groups), pl.ds(UNIT - late, late)], sems.at[UNIT // EACH]
+            )
+        ]
+        copies[0].start()
+        some = trace_rows(table_ref, given)
+        for step in range(UNIT // EACH):
+            some(range(step * EACH, (step + 1) * EACH), held, step * EACH)
+            copy = pltpu.make_async_copy(
+                held.at[:, pl.ds(step * EACH, EACH)],
+                out_ref.at[pl.ds((1 - core) * groups, groups), pl.ds(step * EACH, EACH)],
                 sems.at[step],
             )
             copy.start()
@@ -270,14 +310,17 @@
 
     return pl.pallas_call(
         kernel,
-        out_shape=jax.ShapeDtypeStruct((quarter // UNIT, UNIT, cols, NT), jnp.bfloat16),
-        in_specs=[VMEM] * 2 + ([] if first else [ANY]),
+        out_shape=jax.ShapeDtypeStruct(out.shape, jnp.bfloat16),
+        in_specs=[VMEM] * 3 + [ANY],
         out_specs=ANY,
-        scratch_shapes=[pltpu.VMEM((groups, UNIT, cols, NT), jnp.bfloat16), pltpu.SemaphoreType.DMA((steps,))],
-        input_output_aliases={} if first else {2: 0},
-        compiler_params=PARAMS,
-        name="transform",
-    )(table, spectra, *([] if first else [out]))
+        scratch_shapes=[
+            pltpu.VMEM((groups, UNIT, cols, NT), jnp.bfloat16),
+            pltpu.SemaphoreType.DMA((UNIT // EACH + 1,)),
+        ],
+        input_output_aliases={3: 0},
+        compiler_params=PARAMS,
+        name="transform_rest",
+    )(table, spectra, rest, out)
 
 
 def body(ns, nf, receivers, data, block_of_slot, receiver_order):
@@ -299,37 +342,38 @@
     theirs = over(data, 1)
     taken = over(give, 1)
     y_then_x, x_then_y = (4, 2), (2, 4)
-    pairs = [(keep, taken)]
-    pairs += [tuple(over(value, *flips) for value in pairs[0]) for flips in (y_then_x, x_then_y)]
-    relays = [over(value[:, :lo], *x_then_y) for value in pairs[1]]
+    p1 = [over(value, *y_then_x) for value in (keep, taken)]
+    p2 = over(join_rows([keep, taken], 0, lo), *x_then_y)
     slots = [(even, odd, other) for even, odd in ((0, 0), (2, 1), (1, 2), (3, 3)) for other in range(2)]
-    whole = [value for pair in pairs for value in pair]
     while len(slots) < ns:
         step = len(slots) // 2
         slots += [(step + even, step + odd, other) for even, odd, other in slots]
-    sums, blocks, table = accumulate_first(
-        whole[:4], slots, in_hbm(block_of_slot), in_hbm(data), theirs, in_hbm(jnp.asarray(tables_of(nf)))
-    )
-    tied = lax.optimization_barrier((*pairs[1], sums, relays[0]))
-    sums = tied[2]
-    c_near = over(last_rows(tied[:2], lo), *x_then_y)
+    tied = lax.optimization_barrier((in_hbm(block_of_slot), p1[0]))[0]
+    blocks, table = pick_blocks(slots, tied, in_hbm(data), theirs, in_hbm(jnp.asarray(tables_of(nf))), width)
+    late = lax.optimization_barrier((p1[1], blocks))[0]
+    relays = [over(value[:, :lo], *x_then_y) for value in (p1[0], late)]
+    whole = [keep, taken, *p1]
+    sums = accumulate([(i, value, 0, 0) for i, value in enumerate(whole)], blocks, None, half)
+    tied = lax.optimization_barrier((*whole, sums))
+    sums = tied[4]
+    near = over(join_rows(tied[:4], lo, half), *x_then_y)
     places = [((array, 0, 0), (array, 0, lo)) for array in whole]
-    places += [((array, 0, 0), (c_near, 2 * other, 0)) for other, array in enumerate(relays)]
+    places += [((array, at, 0), (near, 2 * i, 0)) for i, (array, at) in enumerate(((p2, 0), (p2, 2), (relays[0], 0), (relays[1], 0)))]
     while len(places) < ns:
         step = len(places) // 2
         moved = {id(entry[0]): over(entry[0], 2 * step) for place in places for entry in place}
         places += [tuple((moved[id(array)], plane, at) for array, plane, at in place) for place in places]
-    sums = accumulate([(i, *places[i][0]) for i in (4, 5)], blocks, (sums, 0), half)
-    ready = accumulate([(i, *places[i][0]) for i in range(6, ns)], blocks, (sums, 0), lo, nf - 1)
-    own = accumulate([(i, *places[i][1]) for i in range(6, ns)], blocks, (sums, lo), size, 1)
+    second = accumulate([(i, *places[i][0]) for i in (4, 5)], blocks, (sums, 0), lo)
+    ready = accumulate([(i, *places[i][0]) for i in range(6, ns)], blocks, (second, 0), lo, nf - 1)
+    own = accumulate([(i, *places[i][1]) for i in range(4, ns)], blocks, (sums, lo), size, 1)
     got = [
         lax.ppermute(ready[step], "freq", [(i, (i + shift) % nf) for i in range(nf)])
         for step, shift in enumerate(shifts_of(nf))
     ]
     mine, other = settle([own[0], *got])
     crossed = over(other, 1)
-    out = transform(table, mine, False, quarter, None)
-    out = transform(table, crossed, True, quarter, out)
+    out, rest = transform_first(table, mine, quarter)
+    out = transform_rest(table, crossed, out, rest)
     return out.reshape(quarter, *out.shape[2:])
 
 

time: 33.8 us -> 33.2 us (0.982)
  starting transfers between devices: 20.5 us -> 19.3 us
  Pallas kernels: 8.83 us -> 9.28 us
    pallas_call x3 -> x4, Pallas kernels: 1.37 us -> 2.48 us  [accumulate(): pl.pallas_call(kernel, out_shape=jax.ShapeDtypeStruct((steps, 2, two, siz...]
    ppermute x10 -> x9, starting transfers between devices: 15 us -> 13.9 us  [over(): lax.ppermute(value, 'src', [(i, i ^ flips[i % 2]) for i in range(ns)])]
    pallas_call x4 -> x5, Pallas kernels: 6.07 us -> 5.4 us  [the longest x1 2.38 us: pick_blocks(): pl.pallas_call(kernel, out_shape=[jax.ShapeDtypeStruct((ns, 2, two, width...]
    ppermute x10 -> x9, waiting for transfers between devices: 2.07 us -> 2.53 us  [over(): lax.ppermute(value, 'src', [(i, i ^ flips[i % 2]) for i in range(ns)])]
    ppermute x3, waiting for transfers between devices: 2.1 us -> 1.75 us  [body(): lax.ppermute(ready[step], 'freq', [(i, (i + shift) % nf) for i in range(n...]
  transfers between devices with their start and end apart: 13 -> 12, of which waited for: 4 -> 4; matrix products, arithmetic and copies ran while one was open for 0% -> 0% of each run, Pallas kernels for 21% -> 23%
where the time goes in v5:
time: 33.2 us; the launch traced here: 33 us
  starting transfers between devices  19.3 us (58%)
  Pallas kernels  9.28 us (28%)
  waiting for transfers between devices  4.27 us (13%)
    ppermute x9, starting transfers between devices, over(): lax.ppermute(value, 'src', [(i, i ^ flips[i % 2]) for i in range(ns)])  13.9 us
    ppermute x3, starting transfers between devices, body(): lax.ppermute(ready[step], 'freq', [(i, (i + shift) % nf) for i in range(n...  5.34 us
    ppermute x9, waiting for transfers between devices, over(): lax.ppermute(value, 'src', [(i, i ^ flips[i % 2]) for i in range(ns)])  2.53 us
    pallas_call x4, Pallas kernels, accumulate(): pl.pallas_call(kernel, out_shape=jax.ShapeDtypeStruct((steps, 2, two, siz...  2.48 us
    pallas_call x1, Pallas kernels, pick_blocks(): pl.pallas_call(kernel, out_shape=[jax.ShapeDtypeStruct((ns, 2, two, width...  2.38 us
    ppermute x3, waiting for transfers between devices, body(): lax.ppermute(ready[step], 'freq', [(i, (i + shift) % nf) for i in range(n...  1.75 us
    pallas_call x1, Pallas kernels, transform_rest(): pl.pallas_call(kernel, out_shape=jax.ShapeDtypeStruct(out.shape, jnp.bflo...  1.72 us
    pallas_call x1, Pallas kernels, order_rows(): pl.pallas_call(kernel, out_shape=[shape, shape], in_specs=[ANY, ANY], out...  1.38 us
  transfers between devices with their start and end apart: 12, of which 4 were waited for; matrix products, arithmetic and copies ran while one was open for 0% of the time, Pallas kernels for 23%

profile of v5, /device:TPU:0, one launch (start us, length us, event | category | flops | bytes accessed | tf_op | source)
XLA Modules:
  0.0 33.0 jit_solution(5607629323687653466)
XLA Ops:
  0.0 0.5 %collective-permute-start.1 = (bf16[1,2,4096,128]{3,2,1,0:T(8,128)(2,1)}, bf16[1,2,4096,128]{3,2,1,0:T(8,128)(2,1)S(1)}, u32[]{:S(2)}, u32[]{:S(2)}) collective-permute-start(bf16[1,2,4096,128]{3,2,1,0:T(8,128)(2,1)} %data_ref.1), channel_id=1, source_target_pairs={{0,4},{4,0},{8,12},{12,8},{16,20},{20,16},{24,28},{28,24},{1,5},{5... | collective-permute-start | bytes 6291464 | tf_op jit(solution)/shard_map/ppermute | solution.py:333
  0.5 1.4 %order_rows.1 = (bf16[2,128,512]{2,1,0:T(8,128)(2,1)S(1)}, bf16[2,128,512]{2,1,0:T(8,128)(2,1)S(1)}) custom-call(s32[1,256]{1,0:T(1,128)} %bitcast.10, bf16[1,1,2,256,512]{4,3,2,1,0:T(8,128)(2,1)} %g_ref.1), custom_call_target="tpu_custom_call" | custom-call | tf_op jit(solution)/shard_map/order_rows/pallas_call | solution.py:53
  1.8 0.1 collective-permute-start.2
  2.0 3.0 %collective-permute-start = (bf16[2,128,512]{2,1,0:T(8,128)(2,1)S(1)}, bf16[2,128,512]{2,1,0:T(8,128)(2,1)S(1)}, u32[]{:S(2)}, u32[]{:S(2)}) collective-permute-start(bf16[2,128,512]{2,1,0:T(8,128)(2,1)S(1)} %get-tuple-element.25.refs_0_), channel_id=1, source_target_pairs={{0,16},{4,12},{8,24},{12,4},{16,0},{20,28},{24,8},{28,20},{1,17},{... | collective-permute-start | bytes 786440 | tf_op jit(solution)/shard_map/ppermute | solution.py:333
  4.9 2.6 %collective-permute-start.3 = (bf16[2,128,512]{2,1,0:T(8,128)(2,1)S(1)}, bf16[2,128,512]{2,1,0:T(8,128)(2,1)S(1)}, u32[]{:S(2)}, u32[]{:S(2)}) collective-permute-start(bf16[2,128,512]{2,1,0:T(8,128)(2,1)S(1)} %collective-permute-done.2.refs_1_), channel_id=1, source_target_pairs={{0,16},{4,12},{8,24},{12,4},{16,0},{20,28},{24,8},{28,20},{1,17},{... | collective-permute-start | bytes 786440 | tf_op jit(solution)/shard_map/ppermute | solution.py:333
  7.5 1.6 %collective-permute-start.7 = (bf16[4,96,512]{2,1,0:T(8,128)(2,1)S(1)}, bf16[4,96,512]{2,1,0:T(8,128)(2,1)S(1)}, u32[]{:S(2)}, u32[]{:S(2)}) collective-permute-start(bf16[4,96,512]{2,1,0:T(8,128)(2,1)S(1)} %join_rows.3), channel_id=1, source_target_pairs={{0,8},{4,20},{8,0},{12,28},{16,24},{20,4},{24,16},{28,12},{1,9},{5... | collective-permute-start | bytes 1179656 | tf_op jit(solution)/shard_map/ppermute | solution.py:333
  9.1 0.2 collective-permute-done.refs_2_
  9.3 2.9 %collective-permute-start.5 = (bf16[2,96,512]{2,1,0:T(8,128)(2,1)S(1)}, bf16[2,96,512]{2,1,0:T(8,128)(2,1)S(1)}, u32[]{:S(2)}, u32[]{:S(2)}) collective-permute-start(bf16[2,96,512]{2,1,0:T(8,128)(2,1)S(1)} %slice.20), channel_id=1, source_target_pairs={{0,8},{4,20},{8,0},{12,28},{16,24},{20,4},{24,16},{28,12},{1,9},{5... | collective-permute-start | bytes 589832 | tf_op jit(solution)/shard_map/ppermute | solution.py:333
  12.2 2.4 %pick_blocks.1 = (bf16[8,2,2,512,128]{4,3,2,1,0:T(8,128)(2,1)S(1)}, bf16[256,256]{1,0:T(8,128)(2,1)S(1)}) custom-call(s32[8]{0:T(128)} %block_ref, bf16[1,2,4096,128]{3,2,1,0:T(8,128)(2,1)} %data_ref.1, bf16[1,2,4096,128]{3,2,1,0:T(8,128)(2,1)S(1)} %collective-permute-done.1.theirs_ref, bf16[4,256,256]{2,1,0:T(8,128)(2,1)} %constant.2.clone.tables_ref), custom_call_target="tpu_custom_call" | custom-call | tf_op jit(solution)/shard_map/pick_blocks/pallas_call | solution.py:127
  14.7 3.2 %collective-permute-start.6 = (bf16[2,96,512]{2,1,0:T(8,128)(2,1)S(1)}, bf16[2,96,512]{2,1,0:T(8,128)(2,1)S(1)}, u32[]{:S(2)}, u32[]{:S(2)}) collective-permute-start(bf16[2,96,512]{2,1,0:T(8,128)(2,1)S(1)} %slice.16), channel_id=1, source_target_pairs={{0,8},{4,20},{8,0},{12,28},{16,24},{20,4},{24,16},{28,12},{1,9},{5... | collective-permute-start | bytes 589832 | tf_op jit(solution)/shard_map/ppermute | solution.py:333
  17.9 0.7 %accumulate.4.refs_2_ = f32[128,512]{1,0:T(8,128)S(1)} custom-call(bf16[2,128,512]{2,1,0:T(8,128)(2,1)S(1)} %get-tuple-element.25.refs_0_, bf16[2,128,512]{2,1,0:T(8,128)(2,1)S(1)} %collective-permute-done.2.refs_1_, bf16[2,128,512]{2,1,0:T(8,128)(2,1)S(1)} %collective-permute-done.refs_2_, bf16[2,128,512]{2,1,0:T(8,128)(2,1)S(1)} %collective-permute-done.3.refs_3_, ...), custom_call_target="tpu_custom_call" | custom-call | flops 536870912 | bytes 3145728 | tf_op jit(solution)/shard_map/accumulate/pallas_call | solution.py:175
  18.6 0.1 collective-permute-start.4
  18.7 0.5 %accumulate.6.refs_3_ = f32[96,512]{1,0:T(8,128)S(1)} custom-call(bf16[4,96,512]{2,1,0:T(8,128)(2,1)S(1)} %collective-permute-done.7.refs_0_, bf16[8,2,2,512,128]{4,3,2,1,0:T(8,128)(2,1)S(1)} %get-tuple-element.24.refs_4_.refs_1_.refs_2_, f32[128,512]{1,0:T(8,128)S(1)} %accumulate.4.refs_2_), custom_call_target="tpu_custom_call" | custom-call | flops 201326592 | bytes 1441792 | tf_op jit(solution)/shard_map/accumulate/pallas_call | solution.py:175
  19.2 2.3 %collective-permute-done.6.refs_1_ = bf16[2,96,512]{2,1,0:T(8,128)(2,1)S(1)} collective-permute-done((bf16[2,96,512]{2,1,0:T(8,128)(2,1)S(1)}, bf16[2,96,512]{2,1,0:T(8,128)(2,1)S(1)}, u32[]{:S(2)}, u32[]{:S(2)}) %collective-permute-start.6) | collective-permute-done | bytes 196640 | tf_op jit(solution)/shard_map/ppermute | solution.py:333
  21.5 0.5 %accumulate.7 = bf16[3,2,2,32,128]{4,3,2,1,0:T(8,128)(2,1)S(1)} custom-call(bf16[2,96,512]{2,1,0:T(8,128)(2,1)S(1)} %collective-permute-done.5.refs_0_, bf16[2,96,512]{2,1,0:T(8,128)(2,1)S(1)} %collective-permute-done.6.refs_1_, bf16[8,2,2,512,128]{4,3,2,1,0:T(8,128)(2,1)S(1)} %get-tuple-element.24.refs_4_.refs_1_.refs_2_, f32[96,512]{1,0:T(8,128)S(1)} %accumulate.6.refs_3_), custom_call_target="tpu_custom_call" | custom-call | flops 201326592 | bytes 1441792 | tf_op jit(solution)/shard_map/accumulate/pallas_call | solution.py:175
  22.0 1.4 %collective-permute-start.10 = (bf16[2,2,32,128]{3,2,1,0:T(8,128)(2,1)S(1)}, bf16[2,2,32,128]{3,2,1,0:T(8,128)(2,1)S(1)}, u32[]{:S(2)}, u32[]{:S(2)}) collective-permute-start(bf16[2,2,32,128]{3,2,1,0:T(8,128)(2,1)S(1)} %get-tuple-element.35), channel_id=1, source_target_pairs={{0,1},{1,2},{2,3},{3,0},{4,5},{5,6},{6,7},{7,4},{8,9},{9,10},{10,1... | collective-permute-start | bytes 98312 | tf_op jit(solution)/shard_map/ppermute | solution.py:370
  23.4 2.6 %collective-permute-start.9 = (bf16[2,2,32,128]{3,2,1,0:T(8,128)(2,1)S(1)}, bf16[2,2,32,128]{3,2,1,0:T(8,128)(2,1)S(1)}, u32[]{:S(2)}, u32[]{:S(2)}) collective-permute-start(bf16[2,2,32,128]{3,2,1,0:T(8,128)(2,1)S(1)} %get-tuple-element.36), channel_id=1, source_target_pairs={{0,2},{1,3},{2,0},{3,1},{4,6},{5,7},{6,4},{7,5},{8,10},{9,11},{10,... | collective-permute-start | bytes 98312 | tf_op jit(solution)/shard_map/ppermute | solution.py:370
  26.0 1.3 %collective-permute-start.8 = (bf16[2,2,32,128]{3,2,1,0:T(8,128)(2,1)S(1)}, bf16[2,2,32,128]{3,2,1,0:T(8,128)(2,1)S(1)}, u32[]{:S(2)}, u32[]{:S(2)}) collective-permute-start(bf16[2,2,32,128]{3,2,1,0:T(8,128)(2,1)S(1)} %get-tuple-element.37), channel_id=1, source_target_pairs={{0,3},{1,0},{2,1},{3,2},{4,7},{5,4},{6,5},{7,6},{8,11},{9,8},{10,9... | collective-permute-start | bytes 98312 | tf_op jit(solution)/shard_map/ppermute | solution.py:370
  27.3 0.8 %accumulate.5 = bf16[1,2,2,32,128]{4,3,2,1,0:T(8,128)(2,1)S(1)} custom-call(bf16[8,32,512]{2,1,0:T(8,128)(2,1)S(1)} %collective-permute-done.4.refs_0_, bf16[8,2,2,512,128]{4,3,2,1,0:T(8,128)(2,1)S(1)} %get-tuple-element.24.refs_4_.refs_1_.refs_2_, f32[128,512]{1,0:T(8,128)S(1)} %accumulate.4.refs_2_), custom_call_target="tpu_custom_call" | custom-call | flops 134217728 | bytes 2359296 | tf_op jit(solution)/shard_map/accumulate/pallas_call | solution.py:175
  28.2 0.7 %collective-permute-done.9.refs_2_ = bf16[2,2,32,128]{3,2,1,0:T(8,128)(2,1)S(1)} collective-permute-done((bf16[2,2,32,128]{3,2,1,0:T(8,128)(2,1)S(1)}, bf16[2,2,32,128]{3,2,1,0:T(8,128)(2,1)S(1)}, u32[]{:S(2)}, u32[]{:S(2)}) %collective-permute-start.9) | collective-permute-done | bytes 32800 | tf_op jit(solution)/shard_map/ppermute | solution.py:370
  28.8 1.1 %collective-permute-done.8.refs_1_ = bf16[2,2,32,128]{3,2,1,0:T(8,128)(2,1)S(1)} collective-permute-done((bf16[2,2,32,128]{3,2,1,0:T(8,128)(2,1)S(1)}, bf16[2,2,32,128]{3,2,1,0:T(8,128)(2,1)S(1)}, u32[]{:S(2)}, u32[]{:S(2)}) %collective-permute-start.8) | collective-permute-done | bytes 32800 | tf_op jit(solution)/shard_map/ppermute | solution.py:370
  29.9 0.1 collective-permute-start.11
  30.0 1.3 %transform_first.1 = (bf16[4,16,128,256]{3,2,1,0:T(8,128)(2,1)}, bf16[2,8,128,256]{3,2,1,0:T(8,128)(2,1)S(1)}) custom-call(bf16[256,256]{1,0:T(8,128)(2,1)S(1)} %get-tuple-element.22.table_ref, bf16[4,2,32,128]{3,2,1,0:T(8,128)(2,1)S(1)} %get-tuple-element.32.given), custom_call_target="tpu_custom_call" | custom-call | tf_op jit(solution)/shard_map/transform_first/pallas_call | solution.py:268
  31.3 1.7 %transform_rest.1 = bf16[4,16,128,256]{3,2,1,0:T(8,128)(2,1)} custom-call(bf16[256,256]{1,0:T(8,128)(2,1)S(1)} %get-tuple-element.22.table_ref, bf16[4,2,32,128]{3,2,1,0:T(8,128)(2,1)S(1)} %collective-permute-done.11.given, bf16[2,8,128,256]{3,2,1,0:T(8,128)(2,1)S(1)} %get-tuple-element.33.rest_ref, ...), custom_call_target="tpu_custom_call", output_to_operand_aliasing={{}: (3, {})} | custom-call | tf_op jit(solution)/shard_map/transform_rest/pallas_call | solution.py:311
  (14 shorter events, 0.1 us)
Async XLA Ops:
  0.0 12.2 %collective-permute-start.1 = (bf16[1,2,4096,128]{3,2,1,0:T(8,128)(2,1)}, bf16[1,2,4096,128]{3,2,1,0:T(8,128)(2,1)S(1)}, u32[]{:S(2)}, u32[]{:S(2)}) collective-permute-start(bf16[1,2,4096,128]{3,2,1,0:T(8,128)(2,1)} %data_ref.1), channel_id=1, source_target_pairs={{0,4},{4,0},{8,12},{12,8},{16,20},{20,16},{24,28},{28,24},{1,5},{5... | collective-permute-start | bytes 6291464 | tf_op jit(solution)/shard_map/ppermute | solution.py:333
  1.8 3.1 %collective-permute-start.2 = (bf16[2,128,512]{2,1,0:T(8,128)(2,1)S(1)}, bf16[2,128,512]{2,1,0:T(8,128)(2,1)S(1)}, u32[]{:S(2)}, u32[]{:S(2)}) collective-permute-start(bf16[2,128,512]{2,1,0:T(8,128)(2,1)S(1)} %get-tuple-element.23), channel_id=1, source_target_pairs={{0,4},{4,0},{8,12},{12,8},{16,20},{20,16},{24,28},{28,24},{1,5},{5... | collective-permute-start | bytes 786440 | tf_op jit(solution)/shard_map/ppermute | solution.py:333
  2.0 7.3 %collective-permute-start = (bf16[2,128,512]{2,1,0:T(8,128)(2,1)S(1)}, bf16[2,128,512]{2,1,0:T(8,128)(2,1)S(1)}, u32[]{:S(2)}, u32[]{:S(2)}) collective-permute-start(bf16[2,128,512]{2,1,0:T(8,128)(2,1)S(1)} %get-tuple-element.25.refs_0_), channel_id=1, source_target_pairs={{0,16},{4,12},{8,24},{12,4},{16,0},{20,28},{24,8},{28,20},{1,17},{... | collective-permute-start | bytes 786440 | tf_op jit(solution)/shard_map/ppermute | solution.py:333
  4.9 9.7 %collective-permute-start.3 = (bf16[2,128,512]{2,1,0:T(8,128)(2,1)S(1)}, bf16[2,128,512]{2,1,0:T(8,128)(2,1)S(1)}, u32[]{:S(2)}, u32[]{:S(2)}) collective-permute-start(bf16[2,128,512]{2,1,0:T(8,128)(2,1)S(1)} %collective-permute-done.2.refs_1_), channel_id=1, source_target_pairs={{0,16},{4,12},{8,24},{12,4},{16,0},{20,28},{24,8},{28,20},{1,17},{... | collective-permute-start | bytes 786440 | tf_op jit(solution)/shard_map/ppermute | solution.py:333
  7.5 11.2 %collective-permute-start.7 = (bf16[4,96,512]{2,1,0:T(8,128)(2,1)S(1)}, bf16[4,96,512]{2,1,0:T(8,128)(2,1)S(1)}, u32[]{:S(2)}, u32[]{:S(2)}) collective-permute-start(bf16[4,96,512]{2,1,0:T(8,128)(2,1)S(1)} %join_rows.3), channel_id=1, source_target_pairs={{0,8},{4,20},{8,0},{12,28},{16,24},{20,4},{24,16},{28,12},{1,9},{5... | collective-permute-start | bytes 1179656 | tf_op jit(solution)/shard_map/ppermute | solution.py:333
  9.3 9.9 %collective-permute-start.5 = (bf16[2,96,512]{2,1,0:T(8,128)(2,1)S(1)}, bf16[2,96,512]{2,1,0:T(8,128)(2,1)S(1)}, u32[]{:S(2)}, u32[]{:S(2)}) collective-permute-start(bf16[2,96,512]{2,1,0:T(8,128)(2,1)S(1)} %slice.20), channel_id=1, source_target_pairs={{0,8},{4,20},{8,0},{12,28},{16,24},{20,4},{24,16},{28,12},{1,9},{5... | collective-permute-start | bytes 589832 | tf_op jit(solution)/shard_map/ppermute | solution.py:333
  14.7 6.8 %collective-permute-start.6 = (bf16[2,96,512]{2,1,0:T(8,128)(2,1)S(1)}, bf16[2,96,512]{2,1,0:T(8,128)(2,1)S(1)}, u32[]{:S(2)}, u32[]{:S(2)}) collective-permute-start(bf16[2,96,512]{2,1,0:T(8,128)(2,1)S(1)} %slice.16), channel_id=1, source_target_pairs={{0,8},{4,20},{8,0},{12,28},{16,24},{20,4},{24,16},{28,12},{1,9},{5... | collective-permute-start | bytes 589832 | tf_op jit(solution)/shard_map/ppermute | solution.py:333
  18.6 8.7 %collective-permute-start.4 = (bf16[8,32,512]{2,1,0:T(8,128)(2,1)S(1)}, bf16[8,32,512]{2,1,0:T(8,128)(2,1)S(1)}, u32[]{:S(2)}, u32[]{:S(2)}) collective-permute-start(bf16[8,32,512]{2,1,0:T(8,128)(2,1)S(1)} %join_rows.2), channel_id=1, source_target_pairs={{0,8},{4,20},{8,0},{12,28},{16,24},{20,4},{24,16},{28,12},{1,9},{5... | collective-permute-start | bytes 786440 | tf_op jit(solution)/shard_map/ppermute | solution.py:333
  22.0 6.2 %collective-permute-start.10 = (bf16[2,2,32,128]{3,2,1,0:T(8,128)(2,1)S(1)}, bf16[2,2,32,128]{3,2,1,0:T(8,128)(2,1)S(1)}, u32[]{:S(2)}, u32[]{:S(2)}) collective-permute-start(bf16[2,2,32,128]{3,2,1,0:T(8,128)(2,1)S(1)} %get-tuple-element.35), channel_id=1, source_target_pairs={{0,1},{1,2},{2,3},{3,0},{4,5},{5,6},{6,7},{7,4},{8,9},{9,10},{10,1... | collective-permute-start | bytes 98312 | tf_op jit(solution)/shard_map/ppermute | solution.py:370
  23.4 5.4 %collective-permute-start.9 = (bf16[2,2,32,128]{3,2,1,0:T(8,128)(2,1)S(1)}, bf16[2,2,32,128]{3,2,1,0:T(8,128)(2,1)S(1)}, u32[]{:S(2)}, u32[]{:S(2)}) collective-permute-start(bf16[2,2,32,128]{3,2,1,0:T(8,128)(2,1)S(1)} %get-tuple-element.36), channel_id=1, source_target_pairs={{0,2},{1,3},{2,0},{3,1},{4,6},{5,7},{6,4},{7,5},{8,10},{9,11},{10,... | collective-permute-start | bytes 98312 | tf_op jit(solution)/shard_map/ppermute | solution.py:370
  26.0 3.9 %collective-permute-start.8 = (bf16[2,2,32,128]{3,2,1,0:T(8,128)(2,1)S(1)}, bf16[2,2,32,128]{3,2,1,0:T(8,128)(2,1)S(1)}, u32[]{:S(2)}, u32[]{:S(2)}) collective-permute-start(bf16[2,2,32,128]{3,2,1,0:T(8,128)(2,1)S(1)} %get-tuple-element.37), channel_id=1, source_target_pairs={{0,3},{1,0},{2,1},{3,2},{4,7},{5,4},{6,5},{7,6},{8,11},{9,8},{10,9... | collective-permute-start | bytes 98312 | tf_op jit(solution)/shard_map/ppermute | solution.py:370
  29.9 1.3 %collective-permute-start.11 = (bf16[4,2,32,128]{3,2,1,0:T(8,128)(2,1)S(1)}, bf16[4,2,32,128]{3,2,1,0:T(8,128)(2,1)S(1)}, u32[]{:S(2)}, u32[]{:S(2)}) collective-permute-start(bf16[4,2,32,128]{3,2,1,0:T(8,128)(2,1)S(1)} %get-tuple-element.31), channel_id=1, source_target_pairs={{0,4},{4,0},{8,12},{12,8},{16,20},{20,16},{24,28},{28,24},{1,5},{5... | collective-permute-start | bytes 196616 | tf_op jit(solution)/shard_map/ppermute | solution.py:333

commit v6 on v5

--- a/solution.py
+++ b/solution.py
@@ -12,13 +12,14 @@
 NT = 256
 UNIT = 16
 EACH = 4
+FIRST = 1
 VMEM = pl.BlockSpec(memory_space=pltpu.VMEM)
 ANY = pl.BlockSpec(memory_space=pl.ANY)
 PARAMS = pltpu.CompilerParams(vmem_limit_bytes=16 * 2**20)
 
 
 def shifts_of(nf):
-    return tuple(reversed(range(1, nf)))
+    return (*range(2, nf), 1)
 
 
 def order_rows(receivers, receiver_order, nf):
@@ -101,46 +102,74 @@
     )
 
 
-def pick_blocks(slots, block_of_slot, data, theirs, tables, width):
+def pick_blocks(slots, block_of_slot, data, width, picked=None, theirs=None, tables=None):
     ns = len(slots)
     two, _, cols = data.shape[1:]
-
-    def kernel(block_ref, data_ref, theirs_ref, tables_ref, blocks, table, block, sems, more):
+    last = picked is not None
+
+    def kernel(block_ref, data_ref, *refs):
+        block, sems, more = refs[-3:]
         me = lax.axis_index("src")
         chip, core = me // 2, lax.rem(me, 2)
-        first = pltpu.make_async_copy(block_ref, block, more.at[0])
-        first.start()
-        last = pltpu.make_async_copy(tables_ref.at[lax.axis_index("freq")], table, more.at[1])
-        last.start()
-        first.wait()
-        copies = [last]
-        for i, (even, odd, other) in enumerate(slots):
-            slot = jnp.bitwise_xor(chip, jnp.where(core == 0, even, odd)) * 2 + (1 - core if other else core)
-            at = pl.multiple_of(block[slot] * width, width)
-            for side, ref in enumerate((data_ref, theirs_ref)):
-                copy = pltpu.make_async_copy(ref.at[0, :, pl.ds(at, width), :], blocks.at[i, side], sems.at[i, side])
+
+        def scalars():
+            copy = pltpu.make_async_copy(block_ref, block, more.at[0])
+            copy.start()
+            copy.wait()
+
+        def copies(ref, out, side):
+            found = []
+            for i, (even, odd, other) in enumerate(slots):
+                slot = jnp.bitwise_xor(chip, jnp.where(core == 0, even, odd)) * 2 + (1 - core if other else core)
+                at = pl.multiple_of(block[slot] * width, width)
+                found.append(pltpu.make_async_copy(ref.at[0, :, pl.ds(at, width), :], out.at[i], sems.at[side, i]))
+            return found
+
+        def run(list_of):
+            for copy in list_of:
                 copy.start()
-                copies.append(copy)
-        for copy in copies:
-            copy.wait()
-
-    return pl.pallas_call(
-        kernel,
-        out_shape=[
-            jax.ShapeDtypeStruct((ns, 2, two, width, cols), jnp.bfloat16),
-            jax.ShapeDtypeStruct(tables.shape[1:], jnp.bfloat16),
-        ],
-        in_specs=[ANY] * 4,
-        out_specs=[VMEM] * 2,
+            for copy in list_of:
+                copy.wait()
+
+        if not last:
+
+            @pl.when(core == FIRST)
+            def _():
+                scalars()
+                run(copies(data_ref, refs[0], 0))
+
+            return
+        theirs_ref, tables_ref, _, out, out_theirs, table = refs[:6]
+        given = pltpu.make_async_copy(tables_ref.at[lax.axis_index("freq")], table, more.at[1])
+        given.start()
+        scalars()
+
+        @pl.when(core != FIRST)
+        def _():
+            run(copies(data_ref, out, 0) + copies(theirs_ref, out_theirs, 1))
+
+        @pl.when(core == FIRST)
+        def _():
+            run(copies(theirs_ref, out_theirs, 1))
+
+        given.wait()
+
+    shape = jax.ShapeDtypeStruct((ns, two, width, cols), jnp.bfloat16)
+    return pl.pallas_call(
+        kernel,
+        out_shape=[shape, shape, jax.ShapeDtypeStruct(tables.shape[1:], jnp.bfloat16)] if last else shape,
+        in_specs=[ANY] * 4 + [VMEM] if last else [ANY] * 2,
+        out_specs=[VMEM] * 3 if last else VMEM,
+        input_output_aliases={4: 0} if last else {},
         scratch_shapes=[
             pltpu.SMEM((ns,), jnp.int32),
-            pltpu.SemaphoreType.DMA((ns, 2)),
+            pltpu.SemaphoreType.DMA((2, ns)),
             pltpu.SemaphoreType.DMA((2,)),
         ],
         compiler_params=PARAMS,
         cost_estimate=pl.CostEstimate(flops=0, bytes_accessed=0, transcendentals=0),
         name="pick_blocks",
-    )(block_of_slot, data, theirs, tables)
+    )(block_of_slot, data, *((theirs, tables, picked) if last else ()))
 
 
 def accumulate(pieces, blocks, old, rows, steps=0):
@@ -152,15 +181,15 @@
         plan.append((slot, next(i for i, held in enumerate(arrays) if held is array), plane, lo))
     n = len(arrays)
     width = arrays[0].shape[2]
-    two, _, cols = blocks.shape[2:]
+    _, two, _, cols = blocks[0].shape
     before, at = old or (None, 0)
     size = rows // steps if steps else rows
 
     def kernel(*refs):
-        given, block_ref, more, out = refs[:n], refs[n], refs[n + 1 : -1], refs[-1]
+        given, picked, more, out = refs[:n], refs[n : n + 2], refs[n + 2 : -1], refs[-1]
         total = more[0][at : at + rows, :] if more else None
         for i, which, plane, lo in plan:
-            sides = [(block_ref[i, side, 0], block_ref[i, side, 1]) for side in range(2)]
+            sides = [(ref[i, 0], ref[i, 1]) for ref in picked]
             total = products(total, given[which], plane, slice(lo, lo + rows), sides)
         if not steps:
             out[...] = total
@@ -177,12 +206,12 @@
         out_shape=jax.ShapeDtypeStruct((steps, 2, two, size, cols), jnp.bfloat16)
         if steps
         else jax.ShapeDtypeStruct((rows, 4 * cols), jnp.float32),
-        in_specs=[VMEM] * (n + 1 + (old is not None)),
+        in_specs=[VMEM] * (n + 2 + (old is not None)),
         out_specs=VMEM,
         compiler_params=PARAMS,
         cost_estimate=cost_of(len(plan), rows, width, cols),
         name="accumulate",
-    )(*arrays, blocks, *(() if old is None else (before,)))
+    )(*arrays, *blocks, *(() if old is None else (before,)))
 
 
 def tables_of(nf):
@@ -343,15 +372,17 @@
     taken = over(give, 1)
     y_then_x, x_then_y = (4, 2), (2, 4)
     p1 = [over(value, *y_then_x) for value in (keep, taken)]
-    p2 = over(join_rows([keep, taken], 0, lo), *x_then_y)
     slots = [(even, odd, other) for even, odd in ((0, 0), (2, 1), (1, 2), (3, 3)) for other in range(2)]
     while len(slots) < ns:
         step = len(slots) // 2
         slots += [(step + even, step + odd, other) for even, odd, other in slots]
-    tied = lax.optimization_barrier((in_hbm(block_of_slot), p1[0]))[0]
-    blocks, table = pick_blocks(slots, tied, in_hbm(data), theirs, in_hbm(jnp.asarray(tables_of(nf))), width)
-    late = lax.optimization_barrier((p1[1], blocks))[0]
-    relays = [over(value[:, :lo], *x_then_y) for value in (p1[0], late)]
+    tied = lax.optimization_barrier((in_hbm(block_of_slot), taken))[0]
+    picked = pick_blocks(slots, tied, in_hbm(data), width)
+    later = lax.optimization_barrier((keep, taken, picked))[:2]
+    p2 = over(join_rows(later, 0, lo), *x_then_y)
+    relays = [over(value[:, :lo], *x_then_y) for value in p1]
+    tied = lax.optimization_barrier((in_hbm(block_of_slot), p1[1]))[0]
+    *blocks, table = pick_blocks(slots, tied, in_hbm(data), width, picked, theirs, in_hbm(jnp.asarray(tables_of(nf))))
     whole = [keep, taken, *p1]
     sums = accumulate([(i, value, 0, 0) for i, value in enumerate(whole)], blocks, None, half)
     tied = lax.optimization_barrier((*whole, sums))

time: 33.2 us -> 32.1 us (0.967)
  waiting for transfers between devices: 4.27 us -> 3.02 us
    ppermute x9, waiting for transfers between devices: 2.53 us -> 1.28 us  [over(): lax.ppermute(value, 'src', [(i, i ^ flips[i % 2]) for i in range(ns)])]
    ppermute x9, starting transfers between devices: 13.9 us -> 13.3 us  [over(): lax.ppermute(value, 'src', [(i, i ^ flips[i % 2]) for i in range(ns)])]
    ppermute x3, starting transfers between devices: 5.34 us -> 5.82 us  [body(): lax.ppermute(ready[step], 'freq', [(i, (i + shift) % nf) for i in range(n...]
    pallas_call x1 -> x2, Pallas kernels: 2.38 us -> 2.65 us  [pick_blocks(): pl.pallas_call(kernel, out_shape=[shape, shape, jax.ShapeDtypeStruct(tabl...]
  transfers between devices with their start and end apart: 12 -> 12, of which waited for: 4 -> 4; matrix products, arithmetic and copies ran while one was open for 0% -> 0% of each run, Pallas kernels for 23% -> 25%
where the time goes in v6:
time: 32.1 us; the launch traced here: 31.8 us
  starting transfers between devices  19.1 us (60%)
  Pallas kernels  9.55 us (30%)
  waiting for transfers between devices  3.02 us (9%)
    ppermute x9, starting transfers between devices, over(): lax.ppermute(value, 'src', [(i, i ^ flips[i % 2]) for i in range(ns)])  13.3 us
    ppermute x3, starting transfers between devices, body(): lax.ppermute(ready[step], 'freq', [(i, (i + shift) % nf) for i in range(n...  5.82 us
    pallas_call x2, Pallas kernels, pick_blocks(): pl.pallas_call(kernel, out_shape=[shape, shape, jax.ShapeDtypeStruct(tabl...  2.65 us
    pallas_call x4, Pallas kernels, accumulate(): pl.pallas_call(kernel, out_shape=jax.ShapeDtypeStruct((steps, 2, two, siz...  2.48 us
    ppermute x3, waiting for transfers between devices, body(): lax.ppermute(ready[step], 'freq', [(i, (i + shift) % nf) for i in range(n...  1.74 us
    pallas_call x1, Pallas kernels, transform_rest(): pl.pallas_call(kernel, out_shape=jax.ShapeDtypeStruct(out.shape, jnp.bflo...  1.72 us
    pallas_call x1, Pallas kernels, order_rows(): pl.pallas_call(kernel, out_shape=[shape, shape], in_specs=[ANY, ANY], out...  1.38 us
    ppermute x9, waiting for transfers between devices, over(): lax.ppermute(value, 'src', [(i, i ^ flips[i % 2]) for i in range(ns)])  1.28 us
  transfers between devices with their start and end apart: 12, of which 4 were waited for; matrix products, arithmetic and copies ran while one was open for 0% of the time, Pallas kernels for 25%

profile of v6, /device:TPU:0, one launch (start us, length us, event | category | flops | bytes accessed | tf_op | source)
XLA Modules:
  0.0 31.8 jit_solution(13386074333484424913)
XLA Ops:
  0.0 0.5 %collective-permute-start.2 = (bf16[1,2,4096,128]{3,2,1,0:T(8,128)(2,1)}, bf16[1,2,4096,128]{3,2,1,0:T(8,128)(2,1)S(1)}, u32[]{:S(2)}, u32[]{:S(2)}) collective-permute-start(bf16[1,2,4096,128]{3,2,1,0:T(8,128)(2,1)} %data_ref.3), channel_id=1, source_target_pairs={{0,4},{4,0},{8,12},{12,8},{16,20},{20,16},{24,28},{28,24},{1,5},{5... | collective-permute-start | bytes 6291464 | tf_op jit(solution)/shard_map/ppermute | solution.py:362
  0.5 1.4 %order_rows.1 = (bf16[2,128,512]{2,1,0:T(8,128)(2,1)S(1)}, bf16[2,128,512]{2,1,0:T(8,128)(2,1)S(1)}) custom-call(s32[1,256]{1,0:T(1,128)} %bitcast.10, bf16[1,1,2,256,512]{4,3,2,1,0:T(8,128)(2,1)} %g_ref.1), custom_call_target="tpu_custom_call" | custom-call | tf_op jit(solution)/shard_map/order_rows/pallas_call | solution.py:54
  1.8 0.1 collective-permute-start
  2.0 3.0 %collective-permute-start.3 = (bf16[2,128,512]{2,1,0:T(8,128)(2,1)S(1)}, bf16[2,128,512]{2,1,0:T(8,128)(2,1)S(1)}, u32[]{:S(2)}, u32[]{:S(2)}) collective-permute-start(bf16[2,128,512]{2,1,0:T(8,128)(2,1)S(1)} %get-tuple-element.35.refs_0_), channel_id=1, source_target_pairs={{0,16},{4,12},{8,24},{12,4},{16,0},{20,28},{24,8},{28,20},{1,17},{... | collective-permute-start | bytes 786440 | tf_op jit(solution)/shard_map/ppermute | solution.py:362
  4.9 2.6 %collective-permute-start.1 = (bf16[2,128,512]{2,1,0:T(8,128)(2,1)S(1)}, bf16[2,128,512]{2,1,0:T(8,128)(2,1)S(1)}, u32[]{:S(2)}, u32[]{:S(2)}) collective-permute-start(bf16[2,128,512]{2,1,0:T(8,128)(2,1)S(1)} %collective-permute-done.refs_1_), channel_id=1, source_target_pairs={{0,16},{4,12},{8,24},{12,4},{16,0},{20,28},{24,8},{28,20},{1,17},{... | collective-permute-start | bytes 786440 | tf_op jit(solution)/shard_map/ppermute | solution.py:362
  7.5 0.2 pick_blocks.2.refs_2_
  7.7 1.6 %collective-permute-start.7 = (bf16[4,96,512]{2,1,0:T(8,128)(2,1)S(1)}, bf16[4,96,512]{2,1,0:T(8,128)(2,1)S(1)}, u32[]{:S(2)}, u32[]{:S(2)}) collective-permute-start(bf16[4,96,512]{2,1,0:T(8,128)(2,1)S(1)} %join_rows.3), channel_id=1, source_target_pairs={{0,8},{4,20},{8,0},{12,28},{16,24},{20,4},{24,16},{28,12},{1,9},{5... | collective-permute-start | bytes 1179656 | tf_op jit(solution)/shard_map/ppermute | solution.py:362
  9.3 2.1 %collective-permute-start.5 = (bf16[2,96,512]{2,1,0:T(8,128)(2,1)S(1)}, bf16[2,96,512]{2,1,0:T(8,128)(2,1)S(1)}, u32[]{:S(2)}, u32[]{:S(2)}) collective-permute-start(bf16[2,96,512]{2,1,0:T(8,128)(2,1)S(1)} %slice.20), channel_id=1, source_target_pairs={{0,8},{4,20},{8,0},{12,28},{16,24},{20,4},{24,16},{28,12},{1,9},{5... | collective-permute-start | bytes 589832 | tf_op jit(solution)/shard_map/ppermute | solution.py:362
  11.4 0.7 %collective-permute-done.1.refs_3_ = bf16[2,128,512]{2,1,0:T(8,128)(2,1)S(1)} collective-permute-done((bf16[2,128,512]{2,1,0:T(8,128)(2,1)S(1)}, bf16[2,128,512]{2,1,0:T(8,128)(2,1)S(1)}, u32[]{:S(2)}, u32[]{:S(2)}) %collective-permute-start.1) | collective-permute-done | bytes 262176 | tf_op jit(solution)/shard_map/ppermute | solution.py:362
  12.1 3.4 %collective-permute-start.6 = (bf16[2,96,512]{2,1,0:T(8,128)(2,1)S(1)}, bf16[2,96,512]{2,1,0:T(8,128)(2,1)S(1)}, u32[]{:S(2)}, u32[]{:S(2)}) collective-permute-start(bf16[2,96,512]{2,1,0:T(8,128)(2,1)S(1)} %slice.21), channel_id=1, source_target_pairs={{0,8},{4,20},{8,0},{12,28},{16,24},{20,4},{24,16},{28,12},{1,9},{5... | collective-permute-start | bytes 589832 | tf_op jit(solution)/shard_map/ppermute | solution.py:362
  15.5 2.5 %pick_blocks.3 = (bf16[8,2,512,128]{3,2,1,0:T(8,128)(2,1)S(1)}, bf16[8,2,512,128]{3,2,1,0:T(8,128)(2,1)S(1)}, bf16[256,256]{1,0:T(8,128)(2,1)S(1)}) custom-call(s32[8]{0:T(128)} %block_ref.1, bf16[1,2,4096,128]{3,2,1,0:T(8,128)(2,1)} %data_ref.3, bf16[1,2,4096,128]{3,2,1,0:T(8,128)(2,1)S(1)} %collective-permute-done.2.refs_0_, ...), custom_call_target="tpu_custom_call", output_to_operand_aliasing={{0}: (4, {})} | custom-call | tf_op jit(solution)/shard_map/pick_blocks/pallas_call | solution.py:158
  18.0 0.7 %accumulate.4.refs_3_ = f32[128,512]{1,0:T(8,128)S(1)} custom-call(bf16[2,128,512]{2,1,0:T(8,128)(2,1)S(1)} %get-tuple-element.35.refs_0_, bf16[2,128,512]{2,1,0:T(8,128)(2,1)S(1)} %collective-permute-done.refs_1_, bf16[2,128,512]{2,1,0:T(8,128)(2,1)S(1)} %collective-permute-done.3.refs_2_, bf16[2,128,512]{2,1,0:T(8,128)(2,1)S(1)} %collective-permute-done.1.refs_3_, ...), custom_call_target="tpu_custom_call" | custom-call | flops 536870912 | bytes 3145728 | tf_op jit(solution)/shard_map/accumulate/pallas_call | solution.py:204
  18.8 0.1 collective-permute-start.4
  18.9 0.5 %accumulate.6.refs_4_ = f32[96,512]{1,0:T(8,128)S(1)} custom-call(bf16[4,96,512]{2,1,0:T(8,128)(2,1)S(1)} %collective-permute-done.7.refs_0_, bf16[8,2,512,128]{3,2,1,0:T(8,128)(2,1)S(1)} %get-tuple-element.28.refs_4_.refs_1_.refs_2_, bf16[8,2,512,128]{3,2,1,0:T(8,128)(2,1)S(1)} %get-tuple-element.29.refs_5_.refs_2_.refs_3_, f32[128,512]{1,0:T(8,128)S(1)} %accumulate.4.refs_3_), custom_call_target="tpu_custom_call" | custom-call | flops 201326592 | bytes 1441792 | tf_op jit(solution)/shard_map/accumulate/pallas_call | solution.py:204
  19.4 0.5 %collective-permute-done.6.refs_1_ = bf16[2,96,512]{2,1,0:T(8,128)(2,1)S(1)} collective-permute-done((bf16[2,96,512]{2,1,0:T(8,128)(2,1)S(1)}, bf16[2,96,512]{2,1,0:T(8,128)(2,1)S(1)}, u32[]{:S(2)}, u32[]{:S(2)}) %collective-permute-start.6) | collective-permute-done | bytes 196640 | tf_op jit(solution)/shard_map/ppermute | solution.py:362
  19.9 0.5 %accumulate.7 = bf16[3,2,2,32,128]{4,3,2,1,0:T(8,128)(2,1)S(1)} custom-call(bf16[2,96,512]{2,1,0:T(8,128)(2,1)S(1)} %collective-permute-done.5.refs_0_, bf16[2,96,512]{2,1,0:T(8,128)(2,1)S(1)} %collective-permute-done.6.refs_1_, bf16[8,2,512,128]{3,2,1,0:T(8,128)(2,1)S(1)} %get-tuple-element.28.refs_4_.refs_1_.refs_2_, ...), custom_call_target="tpu_custom_call" | custom-call | flops 201326592 | bytes 1441792 | tf_op jit(solution)/shard_map/accumulate/pallas_call | solution.py:204
  20.4 1.9 %collective-permute-start.10 = (bf16[2,2,32,128]{3,2,1,0:T(8,128)(2,1)S(1)}, bf16[2,2,32,128]{3,2,1,0:T(8,128)(2,1)S(1)}, u32[]{:S(2)}, u32[]{:S(2)}) collective-permute-start(bf16[2,2,32,128]{3,2,1,0:T(8,128)(2,1)S(1)} %get-tuple-element.41), channel_id=1, source_target_pairs={{0,1},{1,2},{2,3},{3,0},{4,5},{5,6},{6,7},{7,4},{8,9},{9,10},{10,1... | collective-permute-start | bytes 98312 | tf_op jit(solution)/shard_map/ppermute | solution.py:401
  22.3 2.6 %collective-permute-start.8 = (bf16[2,2,32,128]{3,2,1,0:T(8,128)(2,1)S(1)}, bf16[2,2,32,128]{3,2,1,0:T(8,128)(2,1)S(1)}, u32[]{:S(2)}, u32[]{:S(2)}) collective-permute-start(bf16[2,2,32,128]{3,2,1,0:T(8,128)(2,1)S(1)} %get-tuple-element.43), channel_id=1, source_target_pairs={{0,2},{1,3},{2,0},{3,1},{4,6},{5,7},{6,4},{7,5},{8,10},{9,11},{10,... | collective-permute-start | bytes 98312 | tf_op jit(solution)/shard_map/ppermute | solution.py:401
  24.8 1.4 %collective-permute-start.9 = (bf16[2,2,32,128]{3,2,1,0:T(8,128)(2,1)S(1)}, bf16[2,2,32,128]{3,2,1,0:T(8,128)(2,1)S(1)}, u32[]{:S(2)}, u32[]{:S(2)}) collective-permute-start(bf16[2,2,32,128]{3,2,1,0:T(8,128)(2,1)S(1)} %get-tuple-element.42), channel_id=1, source_target_pairs={{0,3},{1,0},{2,1},{3,2},{4,7},{5,4},{6,5},{7,6},{8,11},{9,8},{10,9... | collective-permute-start | bytes 98312 | tf_op jit(solution)/shard_map/ppermute | solution.py:401
  26.2 0.8 %accumulate.5 = bf16[1,2,2,32,128]{4,3,2,1,0:T(8,128)(2,1)S(1)} custom-call(bf16[8,32,512]{2,1,0:T(8,128)(2,1)S(1)} %collective-permute-done.4.refs_0_, bf16[8,2,512,128]{3,2,1,0:T(8,128)(2,1)S(1)} %get-tuple-element.28.refs_4_.refs_1_.refs_2_, bf16[8,2,512,128]{3,2,1,0:T(8,128)(2,1)S(1)} %get-tuple-element.29.refs_5_.refs_2_.refs_3_, ...), custom_call_target="tpu_custom_call" | custom-call | flops 134217728 | bytes 2359296 | tf_op jit(solution)/shard_map/accumulate/pallas_call | solution.py:204
  27.0 0.2 collective-permute-done.8.refs_1_
  27.2 1.5 %collective-permute-done.9.refs_2_ = bf16[2,2,32,128]{3,2,1,0:T(8,128)(2,1)S(1)} collective-permute-done((bf16[2,2,32,128]{3,2,1,0:T(8,128)(2,1)S(1)}, bf16[2,2,32,128]{3,2,1,0:T(8,128)(2,1)S(1)}, u32[]{:S(2)}, u32[]{:S(2)}) %collective-permute-start.9) | collective-permute-done | bytes 32800 | tf_op jit(solution)/shard_map/ppermute | solution.py:401
  28.9 1.3 %transform_first.1 = (bf16[4,16,128,256]{3,2,1,0:T(8,128)(2,1)}, bf16[2,8,128,256]{3,2,1,0:T(8,128)(2,1)S(1)}) custom-call(bf16[256,256]{1,0:T(8,128)(2,1)S(1)} %get-tuple-element.26.table_ref, bf16[4,2,32,128]{3,2,1,0:T(8,128)(2,1)S(1)} %get-tuple-element.38.given), custom_call_target="tpu_custom_call" | custom-call | tf_op jit(solution)/shard_map/transform_first/pallas_call | solution.py:297
  30.1 1.7 %transform_rest.1 = bf16[4,16,128,256]{3,2,1,0:T(8,128)(2,1)} custom-call(bf16[256,256]{1,0:T(8,128)(2,1)S(1)} %get-tuple-element.26.table_ref, bf16[4,2,32,128]{3,2,1,0:T(8,128)(2,1)S(1)} %collective-permute-done.11.given, bf16[2,8,128,256]{3,2,1,0:T(8,128)(2,1)S(1)} %get-tuple-element.39.rest_ref, ...), custom_call_target="tpu_custom_call", output_to_operand_aliasing={{}: (3, {})} | custom-call | tf_op jit(solution)/shard_map/transform_rest/pallas_call | solution.py:340
  (15 shorter events, 0.2 us)
Async XLA Ops:
  0.0 15.5 %collective-permute-start.2 = (bf16[1,2,4096,128]{3,2,1,0:T(8,128)(2,1)}, bf16[1,2,4096,128]{3,2,1,0:T(8,128)(2,1)S(1)}, u32[]{:S(2)}, u32[]{:S(2)}) collective-permute-start(bf16[1,2,4096,128]{3,2,1,0:T(8,128)(2,1)} %data_ref.3), channel_id=1, source_target_pairs={{0,4},{4,0},{8,12},{12,8},{16,20},{20,16},{24,28},{28,24},{1,5},{5... | collective-permute-start | bytes 6291464 | tf_op jit(solution)/shard_map/ppermute | solution.py:362
  1.8 3.1 %collective-permute-start = (bf16[2,128,512]{2,1,0:T(8,128)(2,1)S(1)}, bf16[2,128,512]{2,1,0:T(8,128)(2,1)S(1)}, u32[]{:S(2)}, u32[]{:S(2)}) collective-permute-start(bf16[2,128,512]{2,1,0:T(8,128)(2,1)S(1)} %get-tuple-element.23), channel_id=1, source_target_pairs={{0,4},{4,0},{8,12},{12,8},{16,20},{20,16},{24,28},{28,24},{1,5},{5... | collective-permute-start | bytes 786440 | tf_op jit(solution)/shard_map/ppermute | solution.py:362
  2.0 7.3 %collective-permute-start.3 = (bf16[2,128,512]{2,1,0:T(8,128)(2,1)S(1)}, bf16[2,128,512]{2,1,0:T(8,128)(2,1)S(1)}, u32[]{:S(2)}, u32[]{:S(2)}) collective-permute-start(bf16[2,128,512]{2,1,0:T(8,128)(2,1)S(1)} %get-tuple-element.35.refs_0_), channel_id=1, source_target_pairs={{0,16},{4,12},{8,24},{12,4},{16,0},{20,28},{24,8},{28,20},{1,17},{... | collective-permute-start | bytes 786440 | tf_op jit(solution)/shard_map/ppermute | solution.py:362
  4.9 7.2 %collective-permute-start.1 = (bf16[2,128,512]{2,1,0:T(8,128)(2,1)S(1)}, bf16[2,128,512]{2,1,0:T(8,128)(2,1)S(1)}, u32[]{:S(2)}, u32[]{:S(2)}) collective-permute-start(bf16[2,128,512]{2,1,0:T(8,128)(2,1)S(1)} %collective-permute-done.refs_1_), channel_id=1, source_target_pairs={{0,16},{4,12},{8,24},{12,4},{16,0},{20,28},{24,8},{28,20},{1,17},{... | collective-permute-start | bytes 786440 | tf_op jit(solution)/shard_map/ppermute | solution.py:362
  7.7 11.2 %collective-permute-start.7 = (bf16[4,96,512]{2,1,0:T(8,128)(2,1)S(1)}, bf16[4,96,512]{2,1,0:T(8,128)(2,1)S(1)}, u32[]{:S(2)}, u32[]{:S(2)}) collective-permute-start(bf16[4,96,512]{2,1,0:T(8,128)(2,1)S(1)} %join_rows.3), channel_id=1, source_target_pairs={{0,8},{4,20},{8,0},{12,28},{16,24},{20,4},{24,16},{28,12},{1,9},{5... | collective-permute-start | bytes 1179656 | tf_op jit(solution)/shard_map/ppermute | solution.py:362
  9.3 10.1 %collective-permute-start.5 = (bf16[2,96,512]{2,1,0:T(8,128)(2,1)S(1)}, bf16[2,96,512]{2,1,0:T(8,128)(2,1)S(1)}, u32[]{:S(2)}, u32[]{:S(2)}) collective-permute-start(bf16[2,96,512]{2,1,0:T(8,128)(2,1)S(1)} %slice.20), channel_id=1, source_target_pairs={{0,8},{4,20},{8,0},{12,28},{16,24},{20,4},{24,16},{28,12},{1,9},{5... | collective-permute-start | bytes 589832 | tf_op jit(solution)/shard_map/ppermute | solution.py:362
  12.1 7.8 %collective-permute-start.6 = (bf16[2,96,512]{2,1,0:T(8,128)(2,1)S(1)}, bf16[2,96,512]{2,1,0:T(8,128)(2,1)S(1)}, u32[]{:S(2)}, u32[]{:S(2)}) collective-permute-start(bf16[2,96,512]{2,1,0:T(8,128)(2,1)S(1)} %slice.21), channel_id=1, source_target_pairs={{0,8},{4,20},{8,0},{12,28},{16,24},{20,4},{24,16},{28,12},{1,9},{5... | collective-permute-start | bytes 589832 | tf_op jit(solution)/shard_map/ppermute | solution.py:362
  18.8 7.4 %collective-permute-start.4 = (bf16[8,32,512]{2,1,0:T(8,128)(2,1)S(1)}, bf16[8,32,512]{2,1,0:T(8,128)(2,1)S(1)}, u32[]{:S(2)}, u32[]{:S(2)}) collective-permute-start(bf16[8,32,512]{2,1,0:T(8,128)(2,1)S(1)} %join_rows.2), channel_id=1, source_target_pairs={{0,8},{4,20},{8,0},{12,28},{16,24},{20,4},{24,16},{28,12},{1,9},{5... | collective-permute-start | bytes 786440 | tf_op jit(solution)/shard_map/ppermute | solution.py:362
  20.4 6.6 %collective-permute-start.10 = (bf16[2,2,32,128]{3,2,1,0:T(8,128)(2,1)S(1)}, bf16[2,2,32,128]{3,2,1,0:T(8,128)(2,1)S(1)}, u32[]{:S(2)}, u32[]{:S(2)}) collective-permute-start(bf16[2,2,32,128]{3,2,1,0:T(8,128)(2,1)S(1)} %get-tuple-element.41), channel_id=1, source_target_pairs={{0,1},{1,2},{2,3},{3,0},{4,5},{5,6},{6,7},{7,4},{8,9},{9,10},{10,1... | collective-permute-start | bytes 98312 | tf_op jit(solution)/shard_map/ppermute | solution.py:401
  22.3 5.0 %collective-permute-start.8 = (bf16[2,2,32,128]{3,2,1,0:T(8,128)(2,1)S(1)}, bf16[2,2,32,128]{3,2,1,0:T(8,128)(2,1)S(1)}, u32[]{:S(2)}, u32[]{:S(2)}) collective-permute-start(bf16[2,2,32,128]{3,2,1,0:T(8,128)(2,1)S(1)} %get-tuple-element.43), channel_id=1, source_target_pairs={{0,2},{1,3},{2,0},{3,1},{4,6},{5,7},{6,4},{7,5},{8,10},{9,11},{10,... | collective-permute-start | bytes 98312 | tf_op jit(solution)/shard_map/ppermute | solution.py:401
  24.8 3.9 %collective-permute-start.9 = (bf16[2,2,32,128]{3,2,1,0:T(8,128)(2,1)S(1)}, bf16[2,2,32,128]{3,2,1,0:T(8,128)(2,1)S(1)}, u32[]{:S(2)}, u32[]{:S(2)}) collective-permute-start(bf16[2,2,32,128]{3,2,1,0:T(8,128)(2,1)S(1)} %get-tuple-element.42), channel_id=1, source_target_pairs={{0,3},{1,0},{2,1},{3,2},{4,7},{5,4},{6,5},{7,6},{8,11},{9,8},{10,9... | collective-permute-start | bytes 98312 | tf_op jit(solution)/shard_map/ppermute | solution.py:401
  28.8 1.3 %collective-permute-start.11 = (bf16[4,2,32,128]{3,2,1,0:T(8,128)(2,1)S(1)}, bf16[4,2,32,128]{3,2,1,0:T(8,128)(2,1)S(1)}, u32[]{:S(2)}, u32[]{:S(2)}) collective-permute-start(bf16[4,2,32,128]{3,2,1,0:T(8,128)(2,1)S(1)} %get-tuple-element.37), channel_id=1, source_target_pairs={{0,4},{4,0},{8,12},{12,8},{16,20},{20,16},{24,28},{28,24},{1,5},{5... | collective-permute-start | bytes 196616 | tf_op jit(solution)/shard_map/ppermute | solution.py:362

commit v7 on v6

--- a/solution.py
+++ b/solution.py
@@ -106,6 +106,7 @@
     ns = len(slots)
     two, _, cols = data.shape[1:]
     last = picked is not None
+    early = ns // 2
 
     def kernel(block_ref, data_ref, *refs):
         block, sems, more = refs[-3:]
@@ -117,9 +118,9 @@
             copy.start()
             copy.wait()
 
-        def copies(ref, out, side):
+        def copies(ref, out, side, lo=0, hi=ns):
             found = []
-            for i, (even, odd, other) in enumerate(slots):
+            for i, (even, odd, other) in enumerate(slots[lo:hi], lo):
                 slot = jnp.bitwise_xor(chip, jnp.where(core == 0, even, odd)) * 2 + (1 - core if other else core)
                 at = pl.multiple_of(block[slot] * width, width)
                 found.append(pltpu.make_async_copy(ref.at[0, :, pl.ds(at, width), :], out.at[i], sems.at[side, i]))
@@ -136,7 +137,7 @@
             @pl.when(core == FIRST)
             def _():
                 scalars()
-                run(copies(data_ref, refs[0], 0))
+                run(copies(data_ref, refs[0], 0, 0, early))
 
             return
         theirs_ref, tables_ref, _, out, out_theirs, table = refs[:6]
@@ -150,7 +151,7 @@
 
         @pl.when(core == FIRST)
         def _():
-            run(copies(theirs_ref, out_theirs, 1))
+            run(copies(data_ref, out, 0, early) + copies(theirs_ref, out_theirs, 1))
 
         given.wait()
 

time: 32.1 us -> 32.1 us (level)
  no operation moved by 1% of the time
where the time goes in v7:
time: 32.1 us; the launch traced here: 31.8 us
  starting transfers between devices  19.4 us (60%)
  Pallas kernels  9.55 us (30%)
  waiting for transfers between devices  2.72 us (8%)
    ppermute x9, starting transfers between devices, over(): lax.ppermute(value, 'src', [(i, i ^ flips[i % 2]) for i in range(ns)])  13.6 us
    ppermute x3, starting transfers between devices, body(): lax.ppermute(ready[step], 'freq', [(i, (i + shift) % nf) for i in range(n...  5.82 us
    pallas_call x2, Pallas kernels, pick_blocks(): pl.pallas_call(kernel, out_shape=[shape, shape, jax.ShapeDtypeStruct(tabl...  2.65 us
    pallas_call x4, Pallas kernels, accumulate(): pl.pallas_call(kernel, out_shape=jax.ShapeDtypeStruct((steps, 2, two, siz...  2.48 us
    ppermute x3, waiting for transfers between devices, body(): lax.ppermute(ready[step], 'freq', [(i, (i + shift) % nf) for i in range(n...  1.74 us
    pallas_call x1, Pallas kernels, transform_rest(): pl.pallas_call(kernel, out_shape=jax.ShapeDtypeStruct(out.shape, jnp.bflo...  1.72 us
    pallas_call x1, Pallas kernels, order_rows(): pl.pallas_call(kernel, out_shape=[shape, shape], in_specs=[ANY, ANY], out...  1.38 us
    pallas_call x1, Pallas kernels, transform_first(): pl.pallas_call(kernel, out_shape=[jax.ShapeDtypeStruct((quarter // UNIT,...  1.26 us
  transfers between devices with their start and end apart: 12, of which 4 were waited for; matrix products, arithmetic and copies ran while one was open for 0% of the time, Pallas kernels for 25%

profile of v7, /device:TPU:0, one launch (start us, length us, event | category | flops | bytes accessed | tf_op | source)
XLA Modules:
  0.0 31.8 jit_solution(16319655542034369600)
XLA Ops:
  0.0 0.5 %collective-permute-start.2 = (bf16[1,2,4096,128]{3,2,1,0:T(8,128)(2,1)}, bf16[1,2,4096,128]{3,2,1,0:T(8,128)(2,1)S(1)}, u32[]{:S(2)}, u32[]{:S(2)}) collective-permute-start(bf16[1,2,4096,128]{3,2,1,0:T(8,128)(2,1)} %data_ref.3), channel_id=1, source_target_pairs={{0,4},{4,0},{8,12},{12,8},{16,20},{20,16},{24,28},{28,24},{1,5},{5... | collective-permute-start | bytes 6291464 | tf_op jit(solution)/shard_map/ppermute | solution.py:363
  0.5 1.4 %order_rows.1 = (bf16[2,128,512]{2,1,0:T(8,128)(2,1)S(1)}, bf16[2,128,512]{2,1,0:T(8,128)(2,1)S(1)}) custom-call(s32[1,256]{1,0:T(1,128)} %bitcast.10, bf16[1,1,2,256,512]{4,3,2,1,0:T(8,128)(2,1)} %g_ref.1), custom_call_target="tpu_custom_call" | custom-call | tf_op jit(solution)/shard_map/order_rows/pallas_call | solution.py:54
  1.8 0.1 collective-permute-start
  2.0 3.0 %collective-permute-start.3 = (bf16[2,128,512]{2,1,0:T(8,128)(2,1)S(1)}, bf16[2,128,512]{2,1,0:T(8,128)(2,1)S(1)}, u32[]{:S(2)}, u32[]{:S(2)}) collective-permute-start(bf16[2,128,512]{2,1,0:T(8,128)(2,1)S(1)} %get-tuple-element.35.refs_0_), channel_id=1, source_target_pairs={{0,16},{4,12},{8,24},{12,4},{16,0},{20,28},{24,8},{28,20},{1,17},{... | collective-permute-start | bytes 786440 | tf_op jit(solution)/shard_map/ppermute | solution.py:363
  4.9 2.6 %collective-permute-start.1 = (bf16[2,128,512]{2,1,0:T(8,128)(2,1)S(1)}, bf16[2,128,512]{2,1,0:T(8,128)(2,1)S(1)}, u32[]{:S(2)}, u32[]{:S(2)}) collective-permute-start(bf16[2,128,512]{2,1,0:T(8,128)(2,1)S(1)} %collective-permute-done.refs_1_), channel_id=1, source_target_pairs={{0,16},{4,12},{8,24},{12,4},{16,0},{20,28},{24,8},{28,20},{1,17},{... | collective-permute-start | bytes 786440 | tf_op jit(solution)/shard_map/ppermute | solution.py:363
  7.5 0.2 pick_blocks.2.refs_2_
  7.7 1.6 %collective-permute-start.7 = (bf16[4,96,512]{2,1,0:T(8,128)(2,1)S(1)}, bf16[4,96,512]{2,1,0:T(8,128)(2,1)S(1)}, u32[]{:S(2)}, u32[]{:S(2)}) collective-permute-start(bf16[4,96,512]{2,1,0:T(8,128)(2,1)S(1)} %join_rows.3), channel_id=1, source_target_pairs={{0,8},{4,20},{8,0},{12,28},{16,24},{20,4},{24,16},{28,12},{1,9},{5... | collective-permute-start | bytes 1179656 | tf_op jit(solution)/shard_map/ppermute | solution.py:363
  9.3 2.1 %collective-permute-start.5 = (bf16[2,96,512]{2,1,0:T(8,128)(2,1)S(1)}, bf16[2,96,512]{2,1,0:T(8,128)(2,1)S(1)}, u32[]{:S(2)}, u32[]{:S(2)}) collective-permute-start(bf16[2,96,512]{2,1,0:T(8,128)(2,1)S(1)} %slice.20), channel_id=1, source_target_pairs={{0,8},{4,20},{8,0},{12,28},{16,24},{20,4},{24,16},{28,12},{1,9},{5... | collective-permute-start | bytes 589832 | tf_op jit(solution)/shard_map/ppermute | solution.py:363
  11.4 0.8 %collective-permute-done.1.refs_3_ = bf16[2,128,512]{2,1,0:T(8,128)(2,1)S(1)} collective-permute-done((bf16[2,128,512]{2,1,0:T(8,128)(2,1)S(1)}, bf16[2,128,512]{2,1,0:T(8,128)(2,1)S(1)}, u32[]{:S(2)}, u32[]{:S(2)}) %collective-permute-start.1) | collective-permute-done | bytes 262176 | tf_op jit(solution)/shard_map/ppermute | solution.py:363
  12.1 3.7 %collective-permute-start.6 = (bf16[2,96,512]{2,1,0:T(8,128)(2,1)S(1)}, bf16[2,96,512]{2,1,0:T(8,128)(2,1)S(1)}, u32[]{:S(2)}, u32[]{:S(2)}) collective-permute-start(bf16[2,96,512]{2,1,0:T(8,128)(2,1)S(1)} %slice.21), channel_id=1, source_target_pairs={{0,8},{4,20},{8,0},{12,28},{16,24},{20,4},{24,16},{28,12},{1,9},{5... | collective-permute-start | bytes 589832 | tf_op jit(solution)/shard_map/ppermute | solution.py:363
  15.8 2.5 %pick_blocks.3 = (bf16[8,2,512,128]{3,2,1,0:T(8,128)(2,1)S(1)}, bf16[8,2,512,128]{3,2,1,0:T(8,128)(2,1)S(1)}, bf16[256,256]{1,0:T(8,128)(2,1)S(1)}) custom-call(s32[8]{0:T(128)} %block_ref.1, bf16[1,2,4096,128]{3,2,1,0:T(8,128)(2,1)} %data_ref.3, bf16[1,2,4096,128]{3,2,1,0:T(8,128)(2,1)S(1)} %collective-permute-done.2.refs_0_, ...), custom_call_target="tpu_custom_call", output_to_operand_aliasing={{0}: (4, {})} | custom-call | tf_op jit(solution)/shard_map/pick_blocks/pallas_call | solution.py:159
  18.3 0.7 %accumulate.4.refs_3_ = f32[128,512]{1,0:T(8,128)S(1)} custom-call(bf16[2,128,512]{2,1,0:T(8,128)(2,1)S(1)} %get-tuple-element.35.refs_0_, bf16[2,128,512]{2,1,0:T(8,128)(2,1)S(1)} %collective-permute-done.refs_1_, bf16[2,128,512]{2,1,0:T(8,128)(2,1)S(1)} %collective-permute-done.3.refs_2_, bf16[2,128,512]{2,1,0:T(8,128)(2,1)S(1)} %collective-permute-done.1.refs_3_, ...), custom_call_target="tpu_custom_call" | custom-call | flops 536870912 | bytes 3145728 | tf_op jit(solution)/shard_map/accumulate/pallas_call | solution.py:205
  19.1 0.1 collective-permute-start.4
  19.2 0.5 %accumulate.6.refs_4_ = f32[96,512]{1,0:T(8,128)S(1)} custom-call(bf16[4,96,512]{2,1,0:T(8,128)(2,1)S(1)} %collective-permute-done.7.refs_0_, bf16[8,2,512,128]{3,2,1,0:T(8,128)(2,1)S(1)} %get-tuple-element.28.refs_4_.refs_1_.refs_2_, bf16[8,2,512,128]{3,2,1,0:T(8,128)(2,1)S(1)} %get-tuple-element.29.refs_5_.refs_2_.refs_3_, f32[128,512]{1,0:T(8,128)S(1)} %accumulate.4.refs_3_), custom_call_target="tpu_custom_call" | custom-call | flops 201326592 | bytes 1441792 | tf_op jit(solution)/shard_map/accumulate/pallas_call | solution.py:205
  19.7 0.2 collective-permute-done.6.refs_1_
  19.9 0.5 %accumulate.7 = bf16[3,2,2,32,128]{4,3,2,1,0:T(8,128)(2,1)S(1)} custom-call(bf16[2,96,512]{2,1,0:T(8,128)(2,1)S(1)} %collective-permute-done.5.refs_0_, bf16[2,96,512]{2,1,0:T(8,128)(2,1)S(1)} %collective-permute-done.6.refs_1_, bf16[8,2,512,128]{3,2,1,0:T(8,128)(2,1)S(1)} %get-tuple-element.28.refs_4_.refs_1_.refs_2_, ...), custom_call_target="tpu_custom_call" | custom-call | flops 201326592 | bytes 1441792 | tf_op jit(solution)/shard_map/accumulate/pallas_call | solution.py:205
  20.4 1.9 %collective-permute-start.10 = (bf16[2,2,32,128]{3,2,1,0:T(8,128)(2,1)S(1)}, bf16[2,2,32,128]{3,2,1,0:T(8,128)(2,1)S(1)}, u32[]{:S(2)}, u32[]{:S(2)}) collective-permute-start(bf16[2,2,32,128]{3,2,1,0:T(8,128)(2,1)S(1)} %get-tuple-element.41), channel_id=1, source_target_pairs={{0,1},{1,2},{2,3},{3,0},{4,5},{5,6},{6,7},{7,4},{8,9},{9,10},{10,1... | collective-permute-start | bytes 98312 | tf_op jit(solution)/shard_map/ppermute | solution.py:402
  22.3 2.6 %collective-permute-start.8 = (bf16[2,2,32,128]{3,2,1,0:T(8,128)(2,1)S(1)}, bf16[2,2,32,128]{3,2,1,0:T(8,128)(2,1)S(1)}, u32[]{:S(2)}, u32[]{:S(2)}) collective-permute-start(bf16[2,2,32,128]{3,2,1,0:T(8,128)(2,1)S(1)} %get-tuple-element.43), channel_id=1, source_target_pairs={{0,2},{1,3},{2,0},{3,1},{4,6},{5,7},{6,4},{7,5},{8,10},{9,11},{10,... | collective-permute-start | bytes 98312 | tf_op jit(solution)/shard_map/ppermute | solution.py:402
  24.8 1.4 %collective-permute-start.9 = (bf16[2,2,32,128]{3,2,1,0:T(8,128)(2,1)S(1)}, bf16[2,2,32,128]{3,2,1,0:T(8,128)(2,1)S(1)}, u32[]{:S(2)}, u32[]{:S(2)}) collective-permute-start(bf16[2,2,32,128]{3,2,1,0:T(8,128)(2,1)S(1)} %get-tuple-element.42), channel_id=1, source_target_pairs={{0,3},{1,0},{2,1},{3,2},{4,7},{5,4},{6,5},{7,6},{8,11},{9,8},{10,9... | collective-permute-start | bytes 98312 | tf_op jit(solution)/shard_map/ppermute | solution.py:402
  26.2 0.8 %accumulate.5 = bf16[1,2,2,32,128]{4,3,2,1,0:T(8,128)(2,1)S(1)} custom-call(bf16[8,32,512]{2,1,0:T(8,128)(2,1)S(1)} %collective-permute-done.4.refs_0_, bf16[8,2,512,128]{3,2,1,0:T(8,128)(2,1)S(1)} %get-tuple-element.28.refs_4_.refs_1_.refs_2_, bf16[8,2,512,128]{3,2,1,0:T(8,128)(2,1)S(1)} %get-tuple-element.29.refs_5_.refs_2_.refs_3_, ...), custom_call_target="tpu_custom_call" | custom-call | flops 134217728 | bytes 2359296 | tf_op jit(solution)/shard_map/accumulate/pallas_call | solution.py:205
  27.0 0.2 collective-permute-done.8.refs_1_
  27.2 1.5 %collective-permute-done.9.refs_2_ = bf16[2,2,32,128]{3,2,1,0:T(8,128)(2,1)S(1)} collective-permute-done((bf16[2,2,32,128]{3,2,1,0:T(8,128)(2,1)S(1)}, bf16[2,2,32,128]{3,2,1,0:T(8,128)(2,1)S(1)}, u32[]{:S(2)}, u32[]{:S(2)}) %collective-permute-start.9) | collective-permute-done | bytes 32800 | tf_op jit(solution)/shard_map/ppermute | solution.py:402
  28.9 1.3 %transform_first.1 = (bf16[4,16,128,256]{3,2,1,0:T(8,128)(2,1)}, bf16[2,8,128,256]{3,2,1,0:T(8,128)(2,1)S(1)}) custom-call(bf16[256,256]{1,0:T(8,128)(2,1)S(1)} %get-tuple-element.26.table_ref, bf16[4,2,32,128]{3,2,1,0:T(8,128)(2,1)S(1)} %get-tuple-element.38.given), custom_call_target="tpu_custom_call" | custom-call | tf_op jit(solution)/shard_map/transform_first/pallas_call | solution.py:298
  30.1 1.7 %transform_rest.1 = bf16[4,16,128,256]{3,2,1,0:T(8,128)(2,1)} custom-call(bf16[256,256]{1,0:T(8,128)(2,1)S(1)} %get-tuple-element.26.table_ref, bf16[4,2,32,128]{3,2,1,0:T(8,128)(2,1)S(1)} %collective-permute-done.11.given, bf16[2,8,128,256]{3,2,1,0:T(8,128)(2,1)S(1)} %get-tuple-element.39.rest_ref, ...), custom_call_target="tpu_custom_call", output_to_operand_aliasing={{}: (3, {})} | custom-call | tf_op jit(solution)/shard_map/transform_rest/pallas_call | solution.py:341
  (15 shorter events, 0.2 us)
Async XLA Ops:
  0.0 15.8 %collective-permute-start.2 = (bf16[1,2,4096,128]{3,2,1,0:T(8,128)(2,1)}, bf16[1,2,4096,128]{3,2,1,0:T(8,128)(2,1)S(1)}, u32[]{:S(2)}, u32[]{:S(2)}) collective-permute-start(bf16[1,2,4096,128]{3,2,1,0:T(8,128)(2,1)} %data_ref.3), channel_id=1, source_target_pairs={{0,4},{4,0},{8,12},{12,8},{16,20},{20,16},{24,28},{28,24},{1,5},{5... | collective-permute-start | bytes 6291464 | tf_op jit(solution)/shard_map/ppermute | solution.py:363
  1.8 3.1 %collective-permute-start = (bf16[2,128,512]{2,1,0:T(8,128)(2,1)S(1)}, bf16[2,128,512]{2,1,0:T(8,128)(2,1)S(1)}, u32[]{:S(2)}, u32[]{:S(2)}) collective-permute-start(bf16[2,128,512]{2,1,0:T(8,128)(2,1)S(1)} %get-tuple-element.23), channel_id=1, source_target_pairs={{0,4},{4,0},{8,12},{12,8},{16,20},{20,16},{24,28},{28,24},{1,5},{5... | collective-permute-start | bytes 786440 | tf_op jit(solution)/shard_map/ppermute | solution.py:363
  2.0 7.3 %collective-permute-start.3 = (bf16[2,128,512]{2,1,0:T(8,128)(2,1)S(1)}, bf16[2,128,512]{2,1,0:T(8,128)(2,1)S(1)}, u32[]{:S(2)}, u32[]{:S(2)}) collective-permute-start(bf16[2,128,512]{2,1,0:T(8,128)(2,1)S(1)} %get-tuple-element.35.refs_0_), channel_id=1, source_target_pairs={{0,16},{4,12},{8,24},{12,4},{16,0},{20,28},{24,8},{28,20},{1,17},{... | collective-permute-start | bytes 786440 | tf_op jit(solution)/shard_map/ppermute | solution.py:363
  4.9 7.2 %collective-permute-start.1 = (bf16[2,128,512]{2,1,0:T(8,128)(2,1)S(1)}, bf16[2,128,512]{2,1,0:T(8,128)(2,1)S(1)}, u32[]{:S(2)}, u32[]{:S(2)}) collective-permute-start(bf16[2,128,512]{2,1,0:T(8,128)(2,1)S(1)} %collective-permute-done.refs_1_), channel_id=1, source_target_pairs={{0,16},{4,12},{8,24},{12,4},{16,0},{20,28},{24,8},{28,20},{1,17},{... | collective-permute-start | bytes 786440 | tf_op jit(solution)/shard_map/ppermute | solution.py:363
  7.7 11.5 %collective-permute-start.7 = (bf16[4,96,512]{2,1,0:T(8,128)(2,1)S(1)}, bf16[4,96,512]{2,1,0:T(8,128)(2,1)S(1)}, u32[]{:S(2)}, u32[]{:S(2)}) collective-permute-start(bf16[4,96,512]{2,1,0:T(8,128)(2,1)S(1)} %join_rows.3), channel_id=1, source_target_pairs={{0,8},{4,20},{8,0},{12,28},{16,24},{20,4},{24,16},{28,12},{1,9},{5... | collective-permute-start | bytes 1179656 | tf_op jit(solution)/shard_map/ppermute | solution.py:363
  9.3 10.4 %collective-permute-start.5 = (bf16[2,96,512]{2,1,0:T(8,128)(2,1)S(1)}, bf16[2,96,512]{2,1,0:T(8,128)(2,1)S(1)}, u32[]{:S(2)}, u32[]{:S(2)}) collective-permute-start(bf16[2,96,512]{2,1,0:T(8,128)(2,1)S(1)} %slice.20), channel_id=1, source_target_pairs={{0,8},{4,20},{8,0},{12,28},{16,24},{20,4},{24,16},{28,12},{1,9},{5... | collective-permute-start | bytes 589832 | tf_op jit(solution)/shard_map/ppermute | solution.py:363
  12.1 7.8 %collective-permute-start.6 = (bf16[2,96,512]{2,1,0:T(8,128)(2,1)S(1)}, bf16[2,96,512]{2,1,0:T(8,128)(2,1)S(1)}, u32[]{:S(2)}, u32[]{:S(2)}) collective-permute-start(bf16[2,96,512]{2,1,0:T(8,128)(2,1)S(1)} %slice.21), channel_id=1, source_target_pairs={{0,8},{4,20},{8,0},{12,28},{16,24},{20,4},{24,16},{28,12},{1,9},{5... | collective-permute-start | bytes 589832 | tf_op jit(solution)/shard_map/ppermute | solution.py:363
  19.1 7.1 %collective-permute-start.4 = (bf16[8,32,512]{2,1,0:T(8,128)(2,1)S(1)}, bf16[8,32,512]{2,1,0:T(8,128)(2,1)S(1)}, u32[]{:S(2)}, u32[]{:S(2)}) collective-permute-start(bf16[8,32,512]{2,1,0:T(8,128)(2,1)S(1)} %join_rows.2), channel_id=1, source_target_pairs={{0,8},{4,20},{8,0},{12,28},{16,24},{20,4},{24,16},{28,12},{1,9},{5... | collective-permute-start | bytes 786440 | tf_op jit(solution)/shard_map/ppermute | solution.py:363
  20.4 6.6 %collective-permute-start.10 = (bf16[2,2,32,128]{3,2,1,0:T(8,128)(2,1)S(1)}, bf16[2,2,32,128]{3,2,1,0:T(8,128)(2,1)S(1)}, u32[]{:S(2)}, u32[]{:S(2)}) collective-permute-start(bf16[2,2,32,128]{3,2,1,0:T(8,128)(2,1)S(1)} %get-tuple-element.41), channel_id=1, source_target_pairs={{0,1},{1,2},{2,3},{3,0},{4,5},{5,6},{6,7},{7,4},{8,9},{9,10},{10,1... | collective-permute-start | bytes 98312 | tf_op jit(solution)/shard_map/ppermute | solution.py:402
  22.3 5.0 %collective-permute-start.8 = (bf16[2,2,32,128]{3,2,1,0:T(8,128)(2,1)S(1)}, bf16[2,2,32,128]{3,2,1,0:T(8,128)(2,1)S(1)}, u32[]{:S(2)}, u32[]{:S(2)}) collective-permute-start(bf16[2,2,32,128]{3,2,1,0:T(8,128)(2,1)S(1)} %get-tuple-element.43), channel_id=1, source_target_pairs={{0,2},{1,3},{2,0},{3,1},{4,6},{5,7},{6,4},{7,5},{8,10},{9,11},{10,... | collective-permute-start | bytes 98312 | tf_op jit(solution)/shard_map/ppermute | solution.py:402
  24.8 3.9 %collective-permute-start.9 = (bf16[2,2,32,128]{3,2,1,0:T(8,128)(2,1)S(1)}, bf16[2,2,32,128]{3,2,1,0:T(8,128)(2,1)S(1)}, u32[]{:S(2)}, u32[]{:S(2)}) collective-permute-start(bf16[2,2,32,128]{3,2,1,0:T(8,128)(2,1)S(1)} %get-tuple-element.42), channel_id=1, source_target_pairs={{0,3},{1,0},{2,1},{3,2},{4,7},{5,4},{6,5},{7,6},{8,11},{9,8},{10,9... | collective-permute-start | bytes 98312 | tf_op jit(solution)/shard_map/ppermute | solution.py:402
  28.8 1.3 %collective-permute-start.11 = (bf16[4,2,32,128]{3,2,1,0:T(8,128)(2,1)S(1)}, bf16[4,2,32,128]{3,2,1,0:T(8,128)(2,1)S(1)}, u32[]{:S(2)}, u32[]{:S(2)}) collective-permute-start(bf16[4,2,32,128]{3,2,1,0:T(8,128)(2,1)S(1)} %get-tuple-element.37), channel_id=1, source_target_pairs={{0,4},{4,0},{8,12},{12,8},{16,20},{20,16},{24,28},{28,24},{1,5},{5... | collective-permute-start | bytes 196616 | tf_op jit(solution)/shard_map/ppermute | solution.py:363

commit v8 on v7

--- a/solution.py
+++ b/solution.py
@@ -37,8 +37,8 @@
         core = lax.rem(lax.axis_index("src"), 2)
         z = lax.axis_index("freq")
         copies[0].wait()
-        wanted = jnp.broadcast_to(order[...], (rows, rows)).T
-        lane = lax.broadcasted_iota(jnp.int32, (rows, rows), 1)
+        wanted = jnp.broadcast_to(order[...].astype(jnp.float32), (8, rows)).T[:, :1]
+        lane = lax.broadcasted_iota(jnp.int32, (rows, rows), 1).astype(jnp.float32)
         hot[...] = jnp.where(wanted == lane, 1.0, 0.0).astype(jnp.bfloat16)
         copies[1].wait()
         for half, out in ((core, keep), (1 - core, give)):
@@ -102,7 +102,27 @@
     )
 
 
-def pick_blocks(slots, block_of_slot, data, width, picked=None, theirs=None, tables=None):
+def load_rows(data, count):
+    def kernel(ref, out, sem):
+        @pl.when(lax.rem(lax.axis_index("src"), 2) != FIRST)
+        def _():
+            copy = pltpu.make_async_copy(ref.at[0, :, pl.ds(0, count), :], out, sem.at[0])
+            copy.start()
+            copy.wait()
+
+    return pl.pallas_call(
+        kernel,
+        out_shape=jax.ShapeDtypeStruct((data.shape[1], count, data.shape[3]), jnp.bfloat16),
+        in_specs=[ANY],
+        out_specs=VMEM,
+        scratch_shapes=[pltpu.SemaphoreType.DMA((1,))],
+        compiler_params=PARAMS,
+        cost_estimate=pl.CostEstimate(flops=0, bytes_accessed=0, transcendentals=0),
+        name="load_rows",
+    )(data)
+
+
+def pick_blocks(slots, block_of_slot, data, width, picked=None, theirs=None, tables=None, loaded=None):
     ns = len(slots)
     two, _, cols = data.shape[1:]
     last = picked is not None
@@ -140,14 +160,29 @@
                 run(copies(data_ref, refs[0], 0, 0, early))
 
             return
-        theirs_ref, tables_ref, _, out, out_theirs, table = refs[:6]
+        theirs_ref, tables_ref, _, loaded_ref, out, out_theirs, table = refs[:7]
         given = pltpu.make_async_copy(tables_ref.at[lax.axis_index("freq")], table, more.at[1])
         given.start()
         scalars()
 
         @pl.when(core != FIRST)
         def _():
-            run(copies(data_ref, out, 0) + copies(theirs_ref, out_theirs, 1))
+            rest = copies(theirs_ref, out_theirs, 1)
+            for copy in rest:
+                copy.start()
+            near, here = [], []
+            for i, (even, odd, other) in enumerate(slots):
+                slot = jnp.bitwise_xor(chip, jnp.where(core == 0, even, odd)) * 2 + (1 - core if other else core)
+                near.append(block[slot] < loaded.shape[1] // width)
+                at = pl.multiple_of(jnp.where(near[i], block[slot], 0) * width, width)
+                here.append(pltpu.make_async_copy(loaded_ref.at[:, pl.ds(at, width), :], out.at[i], sems.at[0, i]))
+            there = copies(data_ref, out, 0)
+            for act in ("start", "wait"):
+                for i in range(ns):
+                    pl.when(near[i])(getattr(here[i], act))
+                    pl.when(jnp.logical_not(near[i]))(getattr(there[i], act))
+            for copy in rest:
+                copy.wait()
 
         @pl.when(core == FIRST)
         def _():
@@ -159,7 +194,7 @@
     return pl.pallas_call(
         kernel,
         out_shape=[shape, shape, jax.ShapeDtypeStruct(tables.shape[1:], jnp.bfloat16)] if last else shape,
-        in_specs=[ANY] * 4 + [VMEM] if last else [ANY] * 2,
+        in_specs=[ANY] * 4 + [VMEM] * 2 if last else [ANY] * 2,
         out_specs=[VMEM] * 3 if last else VMEM,
         input_output_aliases={4: 0} if last else {},
         scratch_shapes=[
@@ -170,7 +205,7 @@
         compiler_params=PARAMS,
         cost_estimate=pl.CostEstimate(flops=0, bytes_accessed=0, transcendentals=0),
         name="pick_blocks",
-    )(block_of_slot, data, *((theirs, tables, picked) if last else ()))
+    )(block_of_slot, data, *((theirs, tables, picked, loaded) if last else ()))
 
 
 def accumulate(pieces, blocks, old, rows, steps=0):
@@ -372,6 +407,8 @@
     theirs = over(data, 1)
     taken = over(give, 1)
     y_then_x, x_then_y = (4, 2), (2, 4)
+    loaded = load_rows(in_hbm(data), (ns // 4) * width)
+    taken, loaded = lax.optimization_barrier((taken, loaded))
     p1 = [over(value, *y_then_x) for value in (keep, taken)]
     slots = [(even, odd, other) for even, odd in ((0, 0), (2, 1), (1, 2), (3, 3)) for other in range(2)]
     while len(slots) < ns:
@@ -383,11 +420,11 @@
     p2 = over(join_rows(later, 0, lo), *x_then_y)
     relays = [over(value[:, :lo], *x_then_y) for value in p1]
     tied = lax.optimization_barrier((in_hbm(block_of_slot), p1[1]))[0]
-    *blocks, table = pick_blocks(slots, tied, in_hbm(data), width, picked, theirs, in_hbm(jnp.asarray(tables_of(nf))))
+    *blocks, table = pick_blocks(slots, tied, in_hbm(data), width, picked, theirs, in_hbm(jnp.asarray(tables_of(nf))), loaded)
     whole = [keep, taken, *p1]
     sums = accumulate([(i, value, 0, 0) for i, value in enumerate(whole)], blocks, None, half)
-    tied = lax.optimization_barrier((*whole, sums))
-    sums = tied[4]
+    tied = lax.optimization_barrier((*whole, sums, p2))
+    sums, p2 = tied[4:]
     near = over(join_rows(tied[:4], lo, half), *x_then_y)
     places = [((array, 0, 0), (array, 0, lo)) for array in whole]
     places += [((array, at, 0), (near, 2 * i, 0)) for i, (array, at) in enumerate(((p2, 0), (p2, 2), (relays[0], 0), (relays[1], 0)))]

time: 32.1 us -> 32.1 us (level)
  starting transfers between devices: 19.4 us -> 17.7 us
  Pallas kernels: 9.55 us -> 10.6 us
  waiting for transfers between devices: 2.72 us -> 3.35 us
    ppermute x9, starting transfers between devices: 13.6 us -> 11.9 us  [over(): lax.ppermute(value, 'src', [(i, i ^ flips[i % 2]) for i in range(ns)])]
    pallas_call x0 -> x1, Pallas kernels: none -> 1.05 us  [load_rows(): pl.pallas_call(kernel, out_shape=jax.ShapeDtypeStruct((data.shape[1], cou...]
    ppermute x9, waiting for transfers between devices: 0.99 us -> 1.61 us  [over(): lax.ppermute(value, 'src', [(i, i ^ flips[i % 2]) for i in range(ns)])]
  transfers between devices with their start and end apart: 12 -> 12, of which waited for: 4 -> 4; matrix products, arithmetic and copies ran while one was open for 0% -> 0% of each run, Pallas kernels for 25% -> 28%
where the time goes in v8:
time: 32.1 us; the launch traced here: 31.8 us
  starting transfers between devices  17.7 us (55%)
  Pallas kernels  10.6 us (33%)
  waiting for transfers between devices  3.35 us (10%)
    ppermute x9, starting transfers between devices, over(): lax.ppermute(value, 'src', [(i, i ^ flips[i % 2]) for i in range(ns)])  11.9 us
    ppermute x3, starting transfers between devices, body(): lax.ppermute(ready[step], 'freq', [(i, (i + shift) % nf) for i in range(n...  5.82 us
    pallas_call x2, Pallas kernels, pick_blocks(): pl.pallas_call(kernel, out_shape=[shape, shape, jax.ShapeDtypeStruct(tabl...  2.68 us
    pallas_call x4, Pallas kernels, accumulate(): pl.pallas_call(kernel, out_shape=jax.ShapeDtypeStruct((steps, 2, two, siz...  2.48 us
    ppermute x3, waiting for transfers between devices, body(): lax.ppermute(ready[step], 'freq', [(i, (i + shift) % nf) for i in range(n...  1.74 us
    pallas_call x1, Pallas kernels, transform_rest(): pl.pallas_call(kernel, out_shape=jax.ShapeDtypeStruct(out.shape, jnp.bflo...  1.72 us
    ppermute x9, waiting for transfers between devices, over(): lax.ppermute(value, 'src', [(i, i ^ flips[i % 2]) for i in range(ns)])  1.61 us
    pallas_call x1, Pallas kernels, order_rows(): pl.pallas_call(kernel, out_shape=[shape, shape], in_specs=[ANY, ANY], out...  1.38 us
  transfers between devices with their start and end apart: 12, of which 4 were waited for; matrix products, arithmetic and copies ran while one was open for 0% of the time, Pallas kernels for 28%

profile of v8, /device:TPU:0, one launch (start us, length us, event | category | flops | bytes accessed | tf_op | source)
XLA Modules:
  0.0 31.8 jit_solution(14451602582372764224)
XLA Ops:
  0.0 0.5 %collective-permute-start.2 = (bf16[1,2,4096,128]{3,2,1,0:T(8,128)(2,1)}, bf16[1,2,4096,128]{3,2,1,0:T(8,128)(2,1)S(1)}, u32[]{:S(2)}, u32[]{:S(2)}) collective-permute-start(bf16[1,2,4096,128]{3,2,1,0:T(8,128)(2,1)} %data_ref.3), channel_id=1, source_target_pairs={{0,4},{4,0},{8,12},{12,8},{16,20},{20,16},{24,28},{28,24},{1,5},{5... | collective-permute-start | bytes 6291464 | tf_op jit(solution)/shard_map/ppermute | solution.py:398
  0.5 1.4 %order_rows.1 = (bf16[2,128,512]{2,1,0:T(8,128)(2,1)S(1)}, bf16[2,128,512]{2,1,0:T(8,128)(2,1)S(1)}) custom-call(s32[1,256]{1,0:T(1,128)} %bitcast.10, bf16[1,1,2,256,512]{4,3,2,1,0:T(8,128)(2,1)} %g_ref.1), custom_call_target="tpu_custom_call" | custom-call | tf_op jit(solution)/shard_map/order_rows/pallas_call | solution.py:54
  1.8 0.1 collective-permute-start
  2.0 3.0 %collective-permute-start.3 = (bf16[2,128,512]{2,1,0:T(8,128)(2,1)S(1)}, bf16[2,128,512]{2,1,0:T(8,128)(2,1)S(1)}, u32[]{:S(2)}, u32[]{:S(2)}) collective-permute-start(bf16[2,128,512]{2,1,0:T(8,128)(2,1)S(1)} %get-tuple-element.37.refs_0_), channel_id=1, source_target_pairs={{0,16},{4,12},{8,24},{12,4},{16,0},{20,28},{24,8},{28,20},{1,17},{... | collective-permute-start | bytes 786440 | tf_op jit(solution)/shard_map/ppermute | solution.py:398
  4.9 1.0 %load_rows.1.refs_3_ = bf16[2,1024,128]{2,1,0:T(8,128)(2,1)S(1)} custom-call(bf16[1,2,4096,128]{3,2,1,0:T(8,128)(2,1)} %data_ref.3), custom_call_target="tpu_custom_call" | custom-call | tf_op jit(solution)/shard_map/load_rows/pallas_call | solution.py:113
  6.0 1.5 %collective-permute-start.1 = (bf16[2,128,512]{2,1,0:T(8,128)(2,1)S(1)}, bf16[2,128,512]{2,1,0:T(8,128)(2,1)S(1)}, u32[]{:S(2)}, u32[]{:S(2)}) collective-permute-start(bf16[2,128,512]{2,1,0:T(8,128)(2,1)S(1)} %collective-permute-done.refs_1_), channel_id=1, source_target_pairs={{0,16},{4,12},{8,24},{12,4},{16,0},{20,28},{24,8},{28,20},{1,17},{... | collective-permute-start | bytes 786440 | tf_op jit(solution)/shard_map/ppermute | solution.py:398
  7.5 0.2 pick_blocks.2.refs_2_
  7.7 1.6 %collective-permute-start.4 = (bf16[4,96,512]{2,1,0:T(8,128)(2,1)S(1)}, bf16[4,96,512]{2,1,0:T(8,128)(2,1)S(1)}, u32[]{:S(2)}, u32[]{:S(2)}) collective-permute-start(bf16[4,96,512]{2,1,0:T(8,128)(2,1)S(1)} %join_rows.2), channel_id=1, source_target_pairs={{0,8},{4,20},{8,0},{12,28},{16,24},{20,4},{24,16},{28,12},{1,9},{5... | collective-permute-start | bytes 1179656 | tf_op jit(solution)/shard_map/ppermute | solution.py:398
  9.3 2.1 %collective-permute-start.6 = (bf16[2,96,512]{2,1,0:T(8,128)(2,1)S(1)}, bf16[2,96,512]{2,1,0:T(8,128)(2,1)S(1)}, u32[]{:S(2)}, u32[]{:S(2)}) collective-permute-start(bf16[2,96,512]{2,1,0:T(8,128)(2,1)S(1)} %slice.20), channel_id=1, source_target_pairs={{0,8},{4,20},{8,0},{12,28},{16,24},{20,4},{24,16},{28,12},{1,9},{5... | collective-permute-start | bytes 589832 | tf_op jit(solution)/shard_map/ppermute | solution.py:398
  11.4 1.4 %collective-permute-done.1.refs_3_ = bf16[2,128,512]{2,1,0:T(8,128)(2,1)S(1)} collective-permute-done((bf16[2,128,512]{2,1,0:T(8,128)(2,1)S(1)}, bf16[2,128,512]{2,1,0:T(8,128)(2,1)S(1)}, u32[]{:S(2)}, u32[]{:S(2)}) %collective-permute-start.1) | collective-permute-done | bytes 262176 | tf_op jit(solution)/shard_map/ppermute | solution.py:398
  12.8 3.0 %collective-permute-start.7 = (bf16[2,96,512]{2,1,0:T(8,128)(2,1)S(1)}, bf16[2,96,512]{2,1,0:T(8,128)(2,1)S(1)}, u32[]{:S(2)}, u32[]{:S(2)}) collective-permute-start(bf16[2,96,512]{2,1,0:T(8,128)(2,1)S(1)} %slice.21), channel_id=1, source_target_pairs={{0,8},{4,20},{8,0},{12,28},{16,24},{20,4},{24,16},{28,12},{1,9},{5... | collective-permute-start | bytes 589832 | tf_op jit(solution)/shard_map/ppermute | solution.py:398
  15.8 2.5 %pick_blocks.3 = (bf16[8,2,512,128]{3,2,1,0:T(8,128)(2,1)S(1)}, bf16[8,2,512,128]{3,2,1,0:T(8,128)(2,1)S(1)}, bf16[256,256]{1,0:T(8,128)(2,1)S(1)}) custom-call(s32[8]{0:T(128)} %block_ref.1, bf16[1,2,4096,128]{3,2,1,0:T(8,128)(2,1)} %data_ref.3, bf16[1,2,4096,128]{3,2,1,0:T(8,128)(2,1)S(1)} %collective-permute-done.2.refs_0_, ...), custom_call_target="tpu_custom_call", output_to_operand_aliasing={{0}: (4, {})} | custom-call | tf_op jit(solution)/shard_map/pick_blocks/pallas_call | solution.py:194
  18.4 0.7 %accumulate.4.refs_3_ = f32[128,512]{1,0:T(8,128)S(1)} custom-call(bf16[2,128,512]{2,1,0:T(8,128)(2,1)S(1)} %get-tuple-element.37.refs_0_, bf16[2,128,512]{2,1,0:T(8,128)(2,1)S(1)} %collective-permute-done.refs_1_, bf16[2,128,512]{2,1,0:T(8,128)(2,1)S(1)} %collective-permute-done.3.refs_2_, bf16[2,128,512]{2,1,0:T(8,128)(2,1)S(1)} %collective-permute-done.1.refs_3_, ...), custom_call_target="tpu_custom_call" | custom-call | flops 536870912 | bytes 3145728 | tf_op jit(solution)/shard_map/accumulate/pallas_call | solution.py:240
  19.2 0.5 %accumulate.6.refs_4_ = f32[96,512]{1,0:T(8,128)S(1)} custom-call(bf16[4,96,512]{2,1,0:T(8,128)(2,1)S(1)} %collective-permute-done.4.refs_0_, bf16[8,2,512,128]{3,2,1,0:T(8,128)(2,1)S(1)} %get-tuple-element.33.refs_4_.refs_1_.refs_2_, bf16[8,2,512,128]{3,2,1,0:T(8,128)(2,1)S(1)} %get-tuple-element.34.refs_5_.refs_2_.refs_3_, f32[128,512]{1,0:T(8,128)S(1)} %accumulate.4.refs_3_), custom_call_target="tpu_custom_call" | custom-call | flops 201326592 | bytes 1441792 | tf_op jit(solution)/shard_map/accumulate/pallas_call | solution.py:240
  19.7 0.2 collective-permute-done.7.refs_1_
  19.9 0.5 %accumulate.7 = bf16[3,2,2,32,128]{4,3,2,1,0:T(8,128)(2,1)S(1)} custom-call(bf16[2,96,512]{2,1,0:T(8,128)(2,1)S(1)} %collective-permute-done.6.refs_0_, bf16[2,96,512]{2,1,0:T(8,128)(2,1)S(1)} %collective-permute-done.7.refs_1_, bf16[8,2,512,128]{3,2,1,0:T(8,128)(2,1)S(1)} %get-tuple-element.33.refs_4_.refs_1_.refs_2_, ...), custom_call_target="tpu_custom_call" | custom-call | flops 201326592 | bytes 1441792 | tf_op jit(solution)/shard_map/accumulate/pallas_call | solution.py:240
  20.4 1.9 %collective-permute-start.10 = (bf16[2,2,32,128]{3,2,1,0:T(8,128)(2,1)S(1)}, bf16[2,2,32,128]{3,2,1,0:T(8,128)(2,1)S(1)}, u32[]{:S(2)}, u32[]{:S(2)}) collective-permute-start(bf16[2,2,32,128]{3,2,1,0:T(8,128)(2,1)S(1)} %get-tuple-element.47), channel_id=1, source_target_pairs={{0,1},{1,2},{2,3},{3,0},{4,5},{5,6},{6,7},{7,4},{8,9},{9,10},{10,1... | collective-permute-start | bytes 98312 | tf_op jit(solution)/shard_map/ppermute | solution.py:439
  22.3 2.6 %collective-permute-start.8 = (bf16[2,2,32,128]{3,2,1,0:T(8,128)(2,1)S(1)}, bf16[2,2,32,128]{3,2,1,0:T(8,128)(2,1)S(1)}, u32[]{:S(2)}, u32[]{:S(2)}) collective-permute-start(bf16[2,2,32,128]{3,2,1,0:T(8,128)(2,1)S(1)} %get-tuple-element.49), channel_id=1, source_target_pairs={{0,2},{1,3},{2,0},{3,1},{4,6},{5,7},{6,4},{7,5},{8,10},{9,11},{10,... | collective-permute-start | bytes 98312 | tf_op jit(solution)/shard_map/ppermute | solution.py:439
  24.8 1.4 %collective-permute-start.9 = (bf16[2,2,32,128]{3,2,1,0:T(8,128)(2,1)S(1)}, bf16[2,2,32,128]{3,2,1,0:T(8,128)(2,1)S(1)}, u32[]{:S(2)}, u32[]{:S(2)}) collective-permute-start(bf16[2,2,32,128]{3,2,1,0:T(8,128)(2,1)S(1)} %get-tuple-element.48), channel_id=1, source_target_pairs={{0,3},{1,0},{2,1},{3,2},{4,7},{5,4},{6,5},{7,6},{8,11},{9,8},{10,9... | collective-permute-start | bytes 98312 | tf_op jit(solution)/shard_map/ppermute | solution.py:439
  26.2 0.8 %accumulate.5 = bf16[1,2,2,32,128]{4,3,2,1,0:T(8,128)(2,1)S(1)} custom-call(bf16[8,32,512]{2,1,0:T(8,128)(2,1)S(1)} %collective-permute-done.5.refs_0_, bf16[8,2,512,128]{3,2,1,0:T(8,128)(2,1)S(1)} %get-tuple-element.33.refs_4_.refs_1_.refs_2_, bf16[8,2,512,128]{3,2,1,0:T(8,128)(2,1)S(1)} %get-tuple-element.34.refs_5_.refs_2_.refs_3_, ...), custom_call_target="tpu_custom_call" | custom-call | flops 134217728 | bytes 2359296 | tf_op jit(solution)/shard_map/accumulate/pallas_call | solution.py:240
  27.0 0.2 collective-permute-done.8.refs_1_
  27.2 1.5 %collective-permute-done.9.refs_2_ = bf16[2,2,32,128]{3,2,1,0:T(8,128)(2,1)S(1)} collective-permute-done((bf16[2,2,32,128]{3,2,1,0:T(8,128)(2,1)S(1)}, bf16[2,2,32,128]{3,2,1,0:T(8,128)(2,1)S(1)}, u32[]{:S(2)}, u32[]{:S(2)}) %collective-permute-start.9) | collective-permute-done | bytes 32800 | tf_op jit(solution)/shard_map/ppermute | solution.py:439
  28.9 1.3 %transform_first.1 = (bf16[4,16,128,256]{3,2,1,0:T(8,128)(2,1)}, bf16[2,8,128,256]{3,2,1,0:T(8,128)(2,1)S(1)}) custom-call(bf16[256,256]{1,0:T(8,128)(2,1)S(1)} %get-tuple-element.31.table_ref, bf16[4,2,32,128]{3,2,1,0:T(8,128)(2,1)S(1)} %get-tuple-element.44.given), custom_call_target="tpu_custom_call" | custom-call | tf_op jit(solution)/shard_map/transform_first/pallas_call | solution.py:333
  30.1 1.7 %transform_rest.1 = bf16[4,16,128,256]{3,2,1,0:T(8,128)(2,1)} custom-call(bf16[256,256]{1,0:T(8,128)(2,1)S(1)} %get-tuple-element.31.table_ref, bf16[4,2,32,128]{3,2,1,0:T(8,128)(2,1)S(1)} %collective-permute-done.11.given, bf16[2,8,128,256]{3,2,1,0:T(8,128)(2,1)S(1)} %get-tuple-element.45.rest_ref, ...), custom_call_target="tpu_custom_call", output_to_operand_aliasing={{}: (3, {})} | custom-call | tf_op jit(solution)/shard_map/transform_rest/pallas_call | solution.py:376
  (16 shorter events, 0.3 us)
Async XLA Ops:
  0.0 15.8 %collective-permute-start.2 = (bf16[1,2,4096,128]{3,2,1,0:T(8,128)(2,1)}, bf16[1,2,4096,128]{3,2,1,0:T(8,128)(2,1)S(1)}, u32[]{:S(2)}, u32[]{:S(2)}) collective-permute-start(bf16[1,2,4096,128]{3,2,1,0:T(8,128)(2,1)} %data_ref.3), channel_id=1, source_target_pairs={{0,4},{4,0},{8,12},{12,8},{16,20},{20,16},{24,28},{28,24},{1,5},{5... | collective-permute-start | bytes 6291464 | tf_op jit(solution)/shard_map/ppermute | solution.py:398
  1.8 4.2 %collective-permute-start = (bf16[2,128,512]{2,1,0:T(8,128)(2,1)S(1)}, bf16[2,128,512]{2,1,0:T(8,128)(2,1)S(1)}, u32[]{:S(2)}, u32[]{:S(2)}) collective-permute-start(bf16[2,128,512]{2,1,0:T(8,128)(2,1)S(1)} %get-tuple-element.26), channel_id=1, source_target_pairs={{0,4},{4,0},{8,12},{12,8},{16,20},{20,16},{24,28},{28,24},{1,5},{5... | collective-permute-start | bytes 786440 | tf_op jit(solution)/shard_map/ppermute | solution.py:398
  2.0 7.3 %collective-permute-start.3 = (bf16[2,128,512]{2,1,0:T(8,128)(2,1)S(1)}, bf16[2,128,512]{2,1,0:T(8,128)(2,1)S(1)}, u32[]{:S(2)}, u32[]{:S(2)}) collective-permute-start(bf16[2,128,512]{2,1,0:T(8,128)(2,1)S(1)} %get-tuple-element.37.refs_0_), channel_id=1, source_target_pairs={{0,16},{4,12},{8,24},{12,4},{16,0},{20,28},{24,8},{28,20},{1,17},{... | collective-permute-start | bytes 786440 | tf_op jit(solution)/shard_map/ppermute | solution.py:398
  6.0 6.8 %collective-permute-start.1 = (bf16[2,128,512]{2,1,0:T(8,128)(2,1)S(1)}, bf16[2,128,512]{2,1,0:T(8,128)(2,1)S(1)}, u32[]{:S(2)}, u32[]{:S(2)}) collective-permute-start(bf16[2,128,512]{2,1,0:T(8,128)(2,1)S(1)} %collective-permute-done.refs_1_), channel_id=1, source_target_pairs={{0,16},{4,12},{8,24},{12,4},{16,0},{20,28},{24,8},{28,20},{1,17},{... | collective-permute-start | bytes 786440 | tf_op jit(solution)/shard_map/ppermute | solution.py:398
  7.7 11.4 %collective-permute-start.4 = (bf16[4,96,512]{2,1,0:T(8,128)(2,1)S(1)}, bf16[4,96,512]{2,1,0:T(8,128)(2,1)S(1)}, u32[]{:S(2)}, u32[]{:S(2)}) collective-permute-start(bf16[4,96,512]{2,1,0:T(8,128)(2,1)S(1)} %join_rows.2), channel_id=1, source_target_pairs={{0,8},{4,20},{8,0},{12,28},{16,24},{20,4},{24,16},{28,12},{1,9},{5... | collective-permute-start | bytes 1179656 | tf_op jit(solution)/shard_map/ppermute | solution.py:398
  9.3 10.4 %collective-permute-start.6 = (bf16[2,96,512]{2,1,0:T(8,128)(2,1)S(1)}, bf16[2,96,512]{2,1,0:T(8,128)(2,1)S(1)}, u32[]{:S(2)}, u32[]{:S(2)}) collective-permute-start(bf16[2,96,512]{2,1,0:T(8,128)(2,1)S(1)} %slice.20), channel_id=1, source_target_pairs={{0,8},{4,20},{8,0},{12,28},{16,24},{20,4},{24,16},{28,12},{1,9},{5... | collective-permute-start | bytes 589832 | tf_op jit(solution)/shard_map/ppermute | solution.py:398
  12.8 7.1 %collective-permute-start.7 = (bf16[2,96,512]{2,1,0:T(8,128)(2,1)S(1)}, bf16[2,96,512]{2,1,0:T(8,128)(2,1)S(1)}, u32[]{:S(2)}, u32[]{:S(2)}) collective-permute-start(bf16[2,96,512]{2,1,0:T(8,128)(2,1)S(1)} %slice.21), channel_id=1, source_target_pairs={{0,8},{4,20},{8,0},{12,28},{16,24},{20,4},{24,16},{28,12},{1,9},{5... | collective-permute-start | bytes 589832 | tf_op jit(solution)/shard_map/ppermute | solution.py:398
  19.1 7.1 %collective-permute-start.5 = (bf16[8,32,512]{2,1,0:T(8,128)(2,1)S(1)}, bf16[8,32,512]{2,1,0:T(8,128)(2,1)S(1)}, u32[]{:S(2)}, u32[]{:S(2)}) collective-permute-start(bf16[8,32,512]{2,1,0:T(8,128)(2,1)S(1)} %join_rows.3), channel_id=1, source_target_pairs={{0,8},{4,20},{8,0},{12,28},{16,24},{20,4},{24,16},{28,12},{1,9},{5... | collective-permute-start | bytes 786440 | tf_op jit(solution)/shard_map/ppermute | solution.py:398
  20.4 6.6 %collective-permute-start.10 = (bf16[2,2,32,128]{3,2,1,0:T(8,128)(2,1)S(1)}, bf16[2,2,32,128]{3,2,1,0:T(8,128)(2,1)S(1)}, u32[]{:S(2)}, u32[]{:S(2)}) collective-permute-start(bf16[2,2,32,128]{3,2,1,0:T(8,128)(2,1)S(1)} %get-tuple-element.47), channel_id=1, source_target_pairs={{0,1},{1,2},{2,3},{3,0},{4,5},{5,6},{6,7},{7,4},{8,9},{9,10},{10,1... | collective-permute-start | bytes 98312 | tf_op jit(solution)/shard_map/ppermute | solution.py:439
  22.3 5.0 %collective-permute-start.8 = (bf16[2,2,32,128]{3,2,1,0:T(8,128)(2,1)S(1)}, bf16[2,2,32,128]{3,2,1,0:T(8,128)(2,1)S(1)}, u32[]{:S(2)}, u32[]{:S(2)}) collective-permute-start(bf16[2,2,32,128]{3,2,1,0:T(8,128)(2,1)S(1)} %get-tuple-element.49), channel_id=1, source_target_pairs={{0,2},{1,3},{2,0},{3,1},{4,6},{5,7},{6,4},{7,5},{8,10},{9,11},{10,... | collective-permute-start | bytes 98312 | tf_op jit(solution)/shard_map/ppermute | solution.py:439
  24.8 3.9 %collective-permute-start.9 = (bf16[2,2,32,128]{3,2,1,0:T(8,128)(2,1)S(1)}, bf16[2,2,32,128]{3,2,1,0:T(8,128)(2,1)S(1)}, u32[]{:S(2)}, u32[]{:S(2)}) collective-permute-start(bf16[2,2,32,128]{3,2,1,0:T(8,128)(2,1)S(1)} %get-tuple-element.48), channel_id=1, source_target_pairs={{0,3},{1,0},{2,1},{3,2},{4,7},{5,4},{6,5},{7,6},{8,11},{9,8},{10,9... | collective-permute-start | bytes 98312 | tf_op jit(solution)/shard_map/ppermute | solution.py:439
  28.8 1.3 %collective-permute-start.11 = (bf16[4,2,32,128]{3,2,1,0:T(8,128)(2,1)S(1)}, bf16[4,2,32,128]{3,2,1,0:T(8,128)(2,1)S(1)}, u32[]{:S(2)}, u32[]{:S(2)}) collective-permute-start(bf16[4,2,32,128]{3,2,1,0:T(8,128)(2,1)S(1)} %get-tuple-element.43), channel_id=1, source_target_pairs={{0,4},{4,0},{8,12},{12,8},{16,20},{20,16},{24,28},{28,24},{1,5},{5... | collective-permute-start | bytes 196616 | tf_op jit(solution)/shard_map/ppermute | solution.py:398

commit v9 on v7

--- a/solution.py
+++ b/solution.py
@@ -37,8 +37,8 @@
         core = lax.rem(lax.axis_index("src"), 2)
         z = lax.axis_index("freq")
         copies[0].wait()
-        wanted = jnp.broadcast_to(order[...], (rows, rows)).T
-        lane = lax.broadcasted_iota(jnp.int32, (rows, rows), 1)
+        wanted = jnp.broadcast_to(order[...].astype(jnp.float32), (8, rows)).T[:, :1]
+        lane = lax.broadcasted_iota(jnp.int32, (rows, rows), 1).astype(jnp.float32)
         hot[...] = jnp.where(wanted == lane, 1.0, 0.0).astype(jnp.bfloat16)
         copies[1].wait()
         for half, out in ((core, keep), (1 - core, give)):

time: 32.1 us -> 32.1 us (level)
  no operation moved by 1% of the time
where the time goes in v9:
time: 32.1 us; the launch traced here: 31.8 us
  starting transfers between devices  19.4 us (60%)
  Pallas kernels  9.55 us (30%)
  waiting for transfers between devices  2.72 us (8%)
    ppermute x9, starting transfers between devices, over(): lax.ppermute(value, 'src', [(i, i ^ flips[i % 2]) for i in range(ns)])  13.6 us
    ppermute x3, starting transfers between devices, body(): lax.ppermute(ready[step], 'freq', [(i, (i + shift) % nf) for i in range(n...  5.82 us
    pallas_call x2, Pallas kernels, pick_blocks(): pl.pallas_call(kernel, out_shape=[shape, shape, jax.ShapeDtypeStruct(tabl...  2.65 us
    pallas_call x4, Pallas kernels, accumulate(): pl.pallas_call(kernel, out_shape=jax.ShapeDtypeStruct((steps, 2, two, siz...  2.48 us
    ppermute x3, waiting for transfers between devices, body(): lax.ppermute(ready[step], 'freq', [(i, (i + shift) % nf) for i in range(n...  1.74 us
    pallas_call x1, Pallas kernels, transform_rest(): pl.pallas_call(kernel, out_shape=jax.ShapeDtypeStruct(out.shape, jnp.bflo...  1.72 us
    pallas_call x1, Pallas kernels, order_rows(): pl.pallas_call(kernel, out_shape=[shape, shape], in_specs=[ANY, ANY], out...  1.38 us
    pallas_call x1, Pallas kernels, transform_first(): pl.pallas_call(kernel, out_shape=[jax.ShapeDtypeStruct((quarter // UNIT,...  1.26 us
  transfers between devices with their start and end apart: 12, of which 4 were waited for; matrix products, arithmetic and copies ran while one was open for 0% of the time, Pallas kernels for 25%

profile of v9, /device:TPU:0, one launch (start us, length us, event | category | flops | bytes accessed | tf_op | source)
XLA Modules:
  0.0 31.8 jit_solution(6419608565442284659)
XLA Ops:
  0.0 0.5 %collective-permute-start.2 = (bf16[1,2,4096,128]{3,2,1,0:T(8,128)(2,1)}, bf16[1,2,4096,128]{3,2,1,0:T(8,128)(2,1)S(1)}, u32[]{:S(2)}, u32[]{:S(2)}) collective-permute-start(bf16[1,2,4096,128]{3,2,1,0:T(8,128)(2,1)} %data_ref.3), channel_id=1, source_target_pairs={{0,4},{4,0},{8,12},{12,8},{16,20},{20,16},{24,28},{28,24},{1,5},{5... | collective-permute-start | bytes 6291464 | tf_op jit(solution)/shard_map/ppermute | solution.py:363
  0.5 1.4 %order_rows.1 = (bf16[2,128,512]{2,1,0:T(8,128)(2,1)S(1)}, bf16[2,128,512]{2,1,0:T(8,128)(2,1)S(1)}) custom-call(s32[1,256]{1,0:T(1,128)} %bitcast.10, bf16[1,1,2,256,512]{4,3,2,1,0:T(8,128)(2,1)} %g_ref.1), custom_call_target="tpu_custom_call" | custom-call | tf_op jit(solution)/shard_map/order_rows/pallas_call | solution.py:54
  1.8 0.1 collective-permute-start
  2.0 3.0 %collective-permute-start.3 = (bf16[2,128,512]{2,1,0:T(8,128)(2,1)S(1)}, bf16[2,128,512]{2,1,0:T(8,128)(2,1)S(1)}, u32[]{:S(2)}, u32[]{:S(2)}) collective-permute-start(bf16[2,128,512]{2,1,0:T(8,128)(2,1)S(1)} %get-tuple-element.35.refs_0_), channel_id=1, source_target_pairs={{0,16},{4,12},{8,24},{12,4},{16,0},{20,28},{24,8},{28,20},{1,17},{... | collective-permute-start | bytes 786440 | tf_op jit(solution)/shard_map/ppermute | solution.py:363
  4.9 2.6 %collective-permute-start.1 = (bf16[2,128,512]{2,1,0:T(8,128)(2,1)S(1)}, bf16[2,128,512]{2,1,0:T(8,128)(2,1)S(1)}, u32[]{:S(2)}, u32[]{:S(2)}) collective-permute-start(bf16[2,128,512]{2,1,0:T(8,128)(2,1)S(1)} %collective-permute-done.refs_1_), channel_id=1, source_target_pairs={{0,16},{4,12},{8,24},{12,4},{16,0},{20,28},{24,8},{28,20},{1,17},{... | collective-permute-start | bytes 786440 | tf_op jit(solution)/shard_map/ppermute | solution.py:363
  7.5 0.2 pick_blocks.2.refs_2_
  7.7 1.6 %collective-permute-start.7 = (bf16[4,96,512]{2,1,0:T(8,128)(2,1)S(1)}, bf16[4,96,512]{2,1,0:T(8,128)(2,1)S(1)}, u32[]{:S(2)}, u32[]{:S(2)}) collective-permute-start(bf16[4,96,512]{2,1,0:T(8,128)(2,1)S(1)} %join_rows.3), channel_id=1, source_target_pairs={{0,8},{4,20},{8,0},{12,28},{16,24},{20,4},{24,16},{28,12},{1,9},{5... | collective-permute-start | bytes 1179656 | tf_op jit(solution)/shard_map/ppermute | solution.py:363
  9.3 2.1 %collective-permute-start.5 = (bf16[2,96,512]{2,1,0:T(8,128)(2,1)S(1)}, bf16[2,96,512]{2,1,0:T(8,128)(2,1)S(1)}, u32[]{:S(2)}, u32[]{:S(2)}) collective-permute-start(bf16[2,96,512]{2,1,0:T(8,128)(2,1)S(1)} %slice.20), channel_id=1, source_target_pairs={{0,8},{4,20},{8,0},{12,28},{16,24},{20,4},{24,16},{28,12},{1,9},{5... | collective-permute-start | bytes 589832 | tf_op jit(solution)/shard_map/ppermute | solution.py:363
  11.4 0.8 %collective-permute-done.1.refs_3_ = bf16[2,128,512]{2,1,0:T(8,128)(2,1)S(1)} collective-permute-done((bf16[2,128,512]{2,1,0:T(8,128)(2,1)S(1)}, bf16[2,128,512]{2,1,0:T(8,128)(2,1)S(1)}, u32[]{:S(2)}, u32[]{:S(2)}) %collective-permute-start.1) | collective-permute-done | bytes 262176 | tf_op jit(solution)/shard_map/ppermute | solution.py:363
  12.1 3.7 %collective-permute-start.6 = (bf16[2,96,512]{2,1,0:T(8,128)(2,1)S(1)}, bf16[2,96,512]{2,1,0:T(8,128)(2,1)S(1)}, u32[]{:S(2)}, u32[]{:S(2)}) collective-permute-start(bf16[2,96,512]{2,1,0:T(8,128)(2,1)S(1)} %slice.21), channel_id=1, source_target_pairs={{0,8},{4,20},{8,0},{12,28},{16,24},{20,4},{24,16},{28,12},{1,9},{5... | collective-permute-start | bytes 589832 | tf_op jit(solution)/shard_map/ppermute | solution.py:363
  15.8 2.5 %pick_blocks.3 = (bf16[8,2,512,128]{3,2,1,0:T(8,128)(2,1)S(1)}, bf16[8,2,512,128]{3,2,1,0:T(8,128)(2,1)S(1)}, bf16[256,256]{1,0:T(8,128)(2,1)S(1)}) custom-call(s32[8]{0:T(128)} %block_ref.1, bf16[1,2,4096,128]{3,2,1,0:T(8,128)(2,1)} %data_ref.3, bf16[1,2,4096,128]{3,2,1,0:T(8,128)(2,1)S(1)} %collective-permute-done.2.refs_0_, ...), custom_call_target="tpu_custom_call", output_to_operand_aliasing={{0}: (4, {})} | custom-call | tf_op jit(solution)/shard_map/pick_blocks/pallas_call | solution.py:159
  18.3 0.7 %accumulate.4.refs_3_ = f32[128,512]{1,0:T(8,128)S(1)} custom-call(bf16[2,128,512]{2,1,0:T(8,128)(2,1)S(1)} %get-tuple-element.35.refs_0_, bf16[2,128,512]{2,1,0:T(8,128)(2,1)S(1)} %collective-permute-done.refs_1_, bf16[2,128,512]{2,1,0:T(8,128)(2,1)S(1)} %collective-permute-done.3.refs_2_, bf16[2,128,512]{2,1,0:T(8,128)(2,1)S(1)} %collective-permute-done.1.refs_3_, ...), custom_call_target="tpu_custom_call" | custom-call | flops 536870912 | bytes 3145728 | tf_op jit(solution)/shard_map/accumulate/pallas_call | solution.py:205
  19.1 0.1 collective-permute-start.4
  19.2 0.5 %accumulate.6.refs_4_ = f32[96,512]{1,0:T(8,128)S(1)} custom-call(bf16[4,96,512]{2,1,0:T(8,128)(2,1)S(1)} %collective-permute-done.7.refs_0_, bf16[8,2,512,128]{3,2,1,0:T(8,128)(2,1)S(1)} %get-tuple-element.28.refs_4_.refs_1_.refs_2_, bf16[8,2,512,128]{3,2,1,0:T(8,128)(2,1)S(1)} %get-tuple-element.29.refs_5_.refs_2_.refs_3_, f32[128,512]{1,0:T(8,128)S(1)} %accumulate.4.refs_3_), custom_call_target="tpu_custom_call" | custom-call | flops 201326592 | bytes 1441792 | tf_op jit(solution)/shard_map/accumulate/pallas_call | solution.py:205
  19.7 0.2 collective-permute-done.6.refs_1_
  19.9 0.5 %accumulate.7 = bf16[3,2,2,32,128]{4,3,2,1,0:T(8,128)(2,1)S(1)} custom-call(bf16[2,96,512]{2,1,0:T(8,128)(2,1)S(1)} %collective-permute-done.5.refs_0_, bf16[2,96,512]{2,1,0:T(8,128)(2,1)S(1)} %collective-permute-done.6.refs_1_, bf16[8,2,512,128]{3,2,1,0:T(8,128)(2,1)S(1)} %get-tuple-element.28.refs_4_.refs_1_.refs_2_, ...), custom_call_target="tpu_custom_call" | custom-call | flops 201326592 | bytes 1441792 | tf_op jit(solution)/shard_map/accumulate/pallas_call | solution.py:205
  20.4 1.9 %collective-permute-start.10 = (bf16[2,2,32,128]{3,2,1,0:T(8,128)(2,1)S(1)}, bf16[2,2,32,128]{3,2,1,0:T(8,128)(2,1)S(1)}, u32[]{:S(2)}, u32[]{:S(2)}) collective-permute-start(bf16[2,2,32,128]{3,2,1,0:T(8,128)(2,1)S(1)} %get-tuple-element.41), channel_id=1, source_target_pairs={{0,1},{1,2},{2,3},{3,0},{4,5},{5,6},{6,7},{7,4},{8,9},{9,10},{10,1... | collective-permute-start | bytes 98312 | tf_op jit(solution)/shard_map/ppermute | solution.py:402
  22.3 2.6 %collective-permute-start.8 = (bf16[2,2,32,128]{3,2,1,0:T(8,128)(2,1)S(1)}, bf16[2,2,32,128]{3,2,1,0:T(8,128)(2,1)S(1)}, u32[]{:S(2)}, u32[]{:S(2)}) collective-permute-start(bf16[2,2,32,128]{3,2,1,0:T(8,128)(2,1)S(1)} %get-tuple-element.43), channel_id=1, source_target_pairs={{0,2},{1,3},{2,0},{3,1},{4,6},{5,7},{6,4},{7,5},{8,10},{9,11},{10,... | collective-permute-start | bytes 98312 | tf_op jit(solution)/shard_map/ppermute | solution.py:402
  24.8 1.4 %collective-permute-start.9 = (bf16[2,2,32,128]{3,2,1,0:T(8,128)(2,1)S(1)}, bf16[2,2,32,128]{3,2,1,0:T(8,128)(2,1)S(1)}, u32[]{:S(2)}, u32[]{:S(2)}) collective-permute-start(bf16[2,2,32,128]{3,2,1,0:T(8,128)(2,1)S(1)} %get-tuple-element.42), channel_id=1, source_target_pairs={{0,3},{1,0},{2,1},{3,2},{4,7},{5,4},{6,5},{7,6},{8,11},{9,8},{10,9... | collective-permute-start | bytes 98312 | tf_op jit(solution)/shard_map/ppermute | solution.py:402
  26.2 0.8 %accumulate.5 = bf16[1,2,2,32,128]{4,3,2,1,0:T(8,128)(2,1)S(1)} custom-call(bf16[8,32,512]{2,1,0:T(8,128)(2,1)S(1)} %collective-permute-done.4.refs_0_, bf16[8,2,512,128]{3,2,1,0:T(8,128)(2,1)S(1)} %get-tuple-element.28.refs_4_.refs_1_.refs_2_, bf16[8,2,512,128]{3,2,1,0:T(8,128)(2,1)S(1)} %get-tuple-element.29.refs_5_.refs_2_.refs_3_, ...), custom_call_target="tpu_custom_call" | custom-call | flops 134217728 | bytes 2359296 | tf_op jit(solution)/shard_map/accumulate/pallas_call | solution.py:205
  27.0 0.2 collective-permute-done.8.refs_1_
  27.2 1.5 %collective-permute-done.9.refs_2_ = bf16[2,2,32,128]{3,2,1,0:T(8,128)(2,1)S(1)} collective-permute-done((bf16[2,2,32,128]{3,2,1,0:T(8,128)(2,1)S(1)}, bf16[2,2,32,128]{3,2,1,0:T(8,128)(2,1)S(1)}, u32[]{:S(2)}, u32[]{:S(2)}) %collective-permute-start.9) | collective-permute-done | bytes 32800 | tf_op jit(solution)/shard_map/ppermute | solution.py:402
  28.9 1.3 %transform_first.1 = (bf16[4,16,128,256]{3,2,1,0:T(8,128)(2,1)}, bf16[2,8,128,256]{3,2,1,0:T(8,128)(2,1)S(1)}) custom-call(bf16[256,256]{1,0:T(8,128)(2,1)S(1)} %get-tuple-element.26.table_ref, bf16[4,2,32,128]{3,2,1,0:T(8,128)(2,1)S(1)} %get-tuple-element.38.given), custom_call_target="tpu_custom_call" | custom-call | tf_op jit(solution)/shard_map/transform_first/pallas_call | solution.py:298
  30.1 1.7 %transform_rest.1 = bf16[4,16,128,256]{3,2,1,0:T(8,128)(2,1)} custom-call(bf16[256,256]{1,0:T(8,128)(2,1)S(1)} %get-tuple-element.26.table_ref, bf16[4,2,32,128]{3,2,1,0:T(8,128)(2,1)S(1)} %collective-permute-done.11.given, bf16[2,8,128,256]{3,2,1,0:T(8,128)(2,1)S(1)} %get-tuple-element.39.rest_ref, ...), custom_call_target="tpu_custom_call", output_to_operand_aliasing={{}: (3, {})} | custom-call | tf_op jit(solution)/shard_map/transform_rest/pallas_call | solution.py:341
  (15 shorter events, 0.2 us)
Async XLA Ops:
  0.0 15.8 %collective-permute-start.2 = (bf16[1,2,4096,128]{3,2,1,0:T(8,128)(2,1)}, bf16[1,2,4096,128]{3,2,1,0:T(8,128)(2,1)S(1)}, u32[]{:S(2)}, u32[]{:S(2)}) collective-permute-start(bf16[1,2,4096,128]{3,2,1,0:T(8,128)(2,1)} %data_ref.3), channel_id=1, source_target_pairs={{0,4},{4,0},{8,12},{12,8},{16,20},{20,16},{24,28},{28,24},{1,5},{5... | collective-permute-start | bytes 6291464 | tf_op jit(solution)/shard_map/ppermute | solution.py:363
  1.8 3.1 %collective-permute-start = (bf16[2,128,512]{2,1,0:T(8,128)(2,1)S(1)}, bf16[2,128,512]{2,1,0:T(8,128)(2,1)S(1)}, u32[]{:S(2)}, u32[]{:S(2)}) collective-permute-start(bf16[2,128,512]{2,1,0:T(8,128)(2,1)S(1)} %get-tuple-element.23), channel_id=1, source_target_pairs={{0,4},{4,0},{8,12},{12,8},{16,20},{20,16},{24,28},{28,24},{1,5},{5... | collective-permute-start | bytes 786440 | tf_op jit(solution)/shard_map/ppermute | solution.py:363
  2.0 7.3 %collective-permute-start.3 = (bf16[2,128,512]{2,1,0:T(8,128)(2,1)S(1)}, bf16[2,128,512]{2,1,0:T(8,128)(2,1)S(1)}, u32[]{:S(2)}, u32[]{:S(2)}) collective-permute-start(bf16[2,128,512]{2,1,0:T(8,128)(2,1)S(1)} %get-tuple-element.35.refs_0_), channel_id=1, source_target_pairs={{0,16},{4,12},{8,24},{12,4},{16,0},{20,28},{24,8},{28,20},{1,17},{... | collective-permute-start | bytes 786440 | tf_op jit(solution)/shard_map/ppermute | solution.py:363
  4.9 7.2 %collective-permute-start.1 = (bf16[2,128,512]{2,1,0:T(8,128)(2,1)S(1)}, bf16[2,128,512]{2,1,0:T(8,128)(2,1)S(1)}, u32[]{:S(2)}, u32[]{:S(2)}) collective-permute-start(bf16[2,128,512]{2,1,0:T(8,128)(2,1)S(1)} %collective-permute-done.refs_1_), channel_id=1, source_target_pairs={{0,16},{4,12},{8,24},{12,4},{16,0},{20,28},{24,8},{28,20},{1,17},{... | collective-permute-start | bytes 786440 | tf_op jit(solution)/shard_map/ppermute | solution.py:363
  7.7 11.5 %collective-permute-start.7 = (bf16[4,96,512]{2,1,0:T(8,128)(2,1)S(1)}, bf16[4,96,512]{2,1,0:T(8,128)(2,1)S(1)}, u32[]{:S(2)}, u32[]{:S(2)}) collective-permute-start(bf16[4,96,512]{2,1,0:T(8,128)(2,1)S(1)} %join_rows.3), channel_id=1, source_target_pairs={{0,8},{4,20},{8,0},{12,28},{16,24},{20,4},{24,16},{28,12},{1,9},{5... | collective-permute-start | bytes 1179656 | tf_op jit(solution)/shard_map/ppermute | solution.py:363
  9.3 10.4 %collective-permute-start.5 = (bf16[2,96,512]{2,1,0:T(8,128)(2,1)S(1)}, bf16[2,96,512]{2,1,0:T(8,128)(2,1)S(1)}, u32[]{:S(2)}, u32[]{:S(2)}) collective-permute-start(bf16[2,96,512]{2,1,0:T(8,128)(2,1)S(1)} %slice.20), channel_id=1, source_target_pairs={{0,8},{4,20},{8,0},{12,28},{16,24},{20,4},{24,16},{28,12},{1,9},{5... | collective-permute-start | bytes 589832 | tf_op jit(solution)/shard_map/ppermute | solution.py:363
  12.1 7.8 %collective-permute-start.6 = (bf16[2,96,512]{2,1,0:T(8,128)(2,1)S(1)}, bf16[2,96,512]{2,1,0:T(8,128)(2,1)S(1)}, u32[]{:S(2)}, u32[]{:S(2)}) collective-permute-start(bf16[2,96,512]{2,1,0:T(8,128)(2,1)S(1)} %slice.21), channel_id=1, source_target_pairs={{0,8},{4,20},{8,0},{12,28},{16,24},{20,4},{24,16},{28,12},{1,9},{5... | collective-permute-start | bytes 589832 | tf_op jit(solution)/shard_map/ppermute | solution.py:363
  19.1 7.1 %collective-permute-start.4 = (bf16[8,32,512]{2,1,0:T(8,128)(2,1)S(1)}, bf16[8,32,512]{2,1,0:T(8,128)(2,1)S(1)}, u32[]{:S(2)}, u32[]{:S(2)}) collective-permute-start(bf16[8,32,512]{2,1,0:T(8,128)(2,1)S(1)} %join_rows.2), channel_id=1, source_target_pairs={{0,8},{4,20},{8,0},{12,28},{16,24},{20,4},{24,16},{28,12},{1,9},{5... | collective-permute-start | bytes 786440 | tf_op jit(solution)/shard_map/ppermute | solution.py:363
  20.4 6.6 %collective-permute-start.10 = (bf16[2,2,32,128]{3,2,1,0:T(8,128)(2,1)S(1)}, bf16[2,2,32,128]{3,2,1,0:T(8,128)(2,1)S(1)}, u32[]{:S(2)}, u32[]{:S(2)}) collective-permute-start(bf16[2,2,32,128]{3,2,1,0:T(8,128)(2,1)S(1)} %get-tuple-element.41), channel_id=1, source_target_pairs={{0,1},{1,2},{2,3},{3,0},{4,5},{5,6},{6,7},{7,4},{8,9},{9,10},{10,1... | collective-permute-start | bytes 98312 | tf_op jit(solution)/shard_map/ppermute | solution.py:402
  22.3 5.0 %collective-permute-start.8 = (bf16[2,2,32,128]{3,2,1,0:T(8,128)(2,1)S(1)}, bf16[2,2,32,128]{3,2,1,0:T(8,128)(2,1)S(1)}, u32[]{:S(2)}, u32[]{:S(2)}) collective-permute-start(bf16[2,2,32,128]{3,2,1,0:T(8,128)(2,1)S(1)} %get-tuple-element.43), channel_id=1, source_target_pairs={{0,2},{1,3},{2,0},{3,1},{4,6},{5,7},{6,4},{7,5},{8,10},{9,11},{10,... | collective-permute-start | bytes 98312 | tf_op jit(solution)/shard_map/ppermute | solution.py:402
  24.8 3.9 %collective-permute-start.9 = (bf16[2,2,32,128]{3,2,1,0:T(8,128)(2,1)S(1)}, bf16[2,2,32,128]{3,2,1,0:T(8,128)(2,1)S(1)}, u32[]{:S(2)}, u32[]{:S(2)}) collective-permute-start(bf16[2,2,32,128]{3,2,1,0:T(8,128)(2,1)S(1)} %get-tuple-element.42), channel_id=1, source_target_pairs={{0,3},{1,0},{2,1},{3,2},{4,7},{5,4},{6,5},{7,6},{8,11},{9,8},{10,9... | collective-permute-start | bytes 98312 | tf_op jit(solution)/shard_map/ppermute | solution.py:402
  28.8 1.3 %collective-permute-start.11 = (bf16[4,2,32,128]{3,2,1,0:T(8,128)(2,1)S(1)}, bf16[4,2,32,128]{3,2,1,0:T(8,128)(2,1)S(1)}, u32[]{:S(2)}, u32[]{:S(2)}) collective-permute-start(bf16[4,2,32,128]{3,2,1,0:T(8,128)(2,1)S(1)} %get-tuple-element.37), channel_id=1, source_target_pairs={{0,4},{4,0},{8,12},{12,8},{16,20},{20,16},{24,28},{28,24},{1,5},{5... | collective-permute-start | bytes 196616 | tf_op jit(solution)/shard_map/ppermute | solution.py:363

commit v10 on v9

--- a/solution.py
+++ b/solution.py
@@ -106,7 +106,7 @@
     ns = len(slots)
     two, _, cols = data.shape[1:]
     last = picked is not None
-    early = ns // 2
+    early = 3 * ns // 4
 
     def kernel(block_ref, data_ref, *refs):
         block, sems, more = refs[-3:]

time: 32.1 us -> 32.1 us (level)
  no operation moved by 1% of the time
where the time goes in v10:
time: 32.1 us; the launch traced here: 31.8 us
  starting transfers between devices  19.3 us (60%)
  Pallas kernels  9.55 us (30%)
  waiting for transfers between devices  2.86 us (9%)
    ppermute x9, starting transfers between devices, over(): lax.ppermute(value, 'src', [(i, i ^ flips[i % 2]) for i in range(ns)])  13.5 us
    ppermute x3, starting transfers between devices, body(): lax.ppermute(ready[step], 'freq', [(i, (i + shift) % nf) for i in range(n...  5.82 us
    pallas_call x2, Pallas kernels, pick_blocks(): pl.pallas_call(kernel, out_shape=[shape, shape, jax.ShapeDtypeStruct(tabl...  2.65 us
    pallas_call x4, Pallas kernels, accumulate(): pl.pallas_call(kernel, out_shape=jax.ShapeDtypeStruct((steps, 2, two, siz...  2.49 us
    ppermute x3, waiting for transfers between devices, body(): lax.ppermute(ready[step], 'freq', [(i, (i + shift) % nf) for i in range(n...  1.74 us
    pallas_call x1, Pallas kernels, transform_rest(): pl.pallas_call(kernel, out_shape=jax.ShapeDtypeStruct(out.shape, jnp.bflo...  1.72 us
    pallas_call x1, Pallas kernels, order_rows(): pl.pallas_call(kernel, out_shape=[shape, shape], in_specs=[ANY, ANY], out...  1.38 us
    pallas_call x1, Pallas kernels, transform_first(): pl.pallas_call(kernel, out_shape=[jax.ShapeDtypeStruct((quarter // UNIT,...  1.26 us
  transfers between devices with their start and end apart: 12, of which 4 were waited for; matrix products, arithmetic and copies ran while one was open for 0% of the time, Pallas kernels for 25%

profile of v10, /device:TPU:0, one launch (start us, length us, event | category | flops | bytes accessed | tf_op | source)
XLA Modules:
  0.0 31.8 jit_solution(9629618055649817604)
XLA Ops:
  0.0 0.5 %collective-permute-start.2 = (bf16[1,2,4096,128]{3,2,1,0:T(8,128)(2,1)}, bf16[1,2,4096,128]{3,2,1,0:T(8,128)(2,1)S(1)}, u32[]{:S(2)}, u32[]{:S(2)}) collective-permute-start(bf16[1,2,4096,128]{3,2,1,0:T(8,128)(2,1)} %data_ref.3), channel_id=1, source_target_pairs={{0,4},{4,0},{8,12},{12,8},{16,20},{20,16},{24,28},{28,24},{1,5},{5... | collective-permute-start | bytes 6291464 | tf_op jit(solution)/shard_map/ppermute | solution.py:363
  0.5 1.4 %order_rows.1 = (bf16[2,128,512]{2,1,0:T(8,128)(2,1)S(1)}, bf16[2,128,512]{2,1,0:T(8,128)(2,1)S(1)}) custom-call(s32[1,256]{1,0:T(1,128)} %bitcast.10, bf16[1,1,2,256,512]{4,3,2,1,0:T(8,128)(2,1)} %g_ref.1), custom_call_target="tpu_custom_call" | custom-call | tf_op jit(solution)/shard_map/order_rows/pallas_call | solution.py:54
  1.8 0.1 collective-permute-start
  2.0 3.0 %collective-permute-start.3 = (bf16[2,128,512]{2,1,0:T(8,128)(2,1)S(1)}, bf16[2,128,512]{2,1,0:T(8,128)(2,1)S(1)}, u32[]{:S(2)}, u32[]{:S(2)}) collective-permute-start(bf16[2,128,512]{2,1,0:T(8,128)(2,1)S(1)} %get-tuple-element.35.refs_0_), channel_id=1, source_target_pairs={{0,16},{4,12},{8,24},{12,4},{16,0},{20,28},{24,8},{28,20},{1,17},{... | collective-permute-start | bytes 786440 | tf_op jit(solution)/shard_map/ppermute | solution.py:363
  4.9 2.6 %collective-permute-start.1 = (bf16[2,128,512]{2,1,0:T(8,128)(2,1)S(1)}, bf16[2,128,512]{2,1,0:T(8,128)(2,1)S(1)}, u32[]{:S(2)}, u32[]{:S(2)}) collective-permute-start(bf16[2,128,512]{2,1,0:T(8,128)(2,1)S(1)} %collective-permute-done.refs_1_), channel_id=1, source_target_pairs={{0,16},{4,12},{8,24},{12,4},{16,0},{20,28},{24,8},{28,20},{1,17},{... | collective-permute-start | bytes 786440 | tf_op jit(solution)/shard_map/ppermute | solution.py:363
  7.5 0.2 pick_blocks.2.refs_2_
  7.7 1.6 %collective-permute-start.7 = (bf16[4,96,512]{2,1,0:T(8,128)(2,1)S(1)}, bf16[4,96,512]{2,1,0:T(8,128)(2,1)S(1)}, u32[]{:S(2)}, u32[]{:S(2)}) collective-permute-start(bf16[4,96,512]{2,1,0:T(8,128)(2,1)S(1)} %join_rows.3), channel_id=1, source_target_pairs={{0,8},{4,20},{8,0},{12,28},{16,24},{20,4},{24,16},{28,12},{1,9},{5... | collective-permute-start | bytes 1179656 | tf_op jit(solution)/shard_map/ppermute | solution.py:363
  9.3 2.1 %collective-permute-start.5 = (bf16[2,96,512]{2,1,0:T(8,128)(2,1)S(1)}, bf16[2,96,512]{2,1,0:T(8,128)(2,1)S(1)}, u32[]{:S(2)}, u32[]{:S(2)}) collective-permute-start(bf16[2,96,512]{2,1,0:T(8,128)(2,1)S(1)} %slice.20), channel_id=1, source_target_pairs={{0,8},{4,20},{8,0},{12,28},{16,24},{20,4},{24,16},{28,12},{1,9},{5... | collective-permute-start | bytes 589832 | tf_op jit(solution)/shard_map/ppermute | solution.py:363
  11.4 0.7 %collective-permute-done.1.refs_3_ = bf16[2,128,512]{2,1,0:T(8,128)(2,1)S(1)} collective-permute-done((bf16[2,128,512]{2,1,0:T(8,128)(2,1)S(1)}, bf16[2,128,512]{2,1,0:T(8,128)(2,1)S(1)}, u32[]{:S(2)}, u32[]{:S(2)}) %collective-permute-start.1) | collective-permute-done | bytes 262176 | tf_op jit(solution)/shard_map/ppermute | solution.py:363
  12.1 3.6 %collective-permute-start.6 = (bf16[2,96,512]{2,1,0:T(8,128)(2,1)S(1)}, bf16[2,96,512]{2,1,0:T(8,128)(2,1)S(1)}, u32[]{:S(2)}, u32[]{:S(2)}) collective-permute-start(bf16[2,96,512]{2,1,0:T(8,128)(2,1)S(1)} %slice.21), channel_id=1, source_target_pairs={{0,8},{4,20},{8,0},{12,28},{16,24},{20,4},{24,16},{28,12},{1,9},{5... | collective-permute-start | bytes 589832 | tf_op jit(solution)/shard_map/ppermute | solution.py:363
  15.7 2.5 %pick_blocks.3 = (bf16[8,2,512,128]{3,2,1,0:T(8,128)(2,1)S(1)}, bf16[8,2,512,128]{3,2,1,0:T(8,128)(2,1)S(1)}, bf16[256,256]{1,0:T(8,128)(2,1)S(1)}) custom-call(s32[8]{0:T(128)} %block_ref.1, bf16[1,2,4096,128]{3,2,1,0:T(8,128)(2,1)} %data_ref.3, bf16[1,2,4096,128]{3,2,1,0:T(8,128)(2,1)S(1)} %collective-permute-done.2.refs_0_, ...), custom_call_target="tpu_custom_call", output_to_operand_aliasing={{0}: (4, {})} | custom-call | tf_op jit(solution)/shard_map/pick_blocks/pallas_call | solution.py:159
  18.2 0.7 %accumulate.4.refs_3_ = f32[128,512]{1,0:T(8,128)S(1)} custom-call(bf16[2,128,512]{2,1,0:T(8,128)(2,1)S(1)} %get-tuple-element.35.refs_0_, bf16[2,128,512]{2,1,0:T(8,128)(2,1)S(1)} %collective-permute-done.refs_1_, bf16[2,128,512]{2,1,0:T(8,128)(2,1)S(1)} %collective-permute-done.3.refs_2_, bf16[2,128,512]{2,1,0:T(8,128)(2,1)S(1)} %collective-permute-done.1.refs_3_, ...), custom_call_target="tpu_custom_call" | custom-call | flops 536870912 | bytes 3145728 | tf_op jit(solution)/shard_map/accumulate/pallas_call | solution.py:205
  18.9 0.1 collective-permute-start.4
  19.0 0.5 %accumulate.6.refs_4_ = f32[96,512]{1,0:T(8,128)S(1)} custom-call(bf16[4,96,512]{2,1,0:T(8,128)(2,1)S(1)} %collective-permute-done.7.refs_0_, bf16[8,2,512,128]{3,2,1,0:T(8,128)(2,1)S(1)} %get-tuple-element.28.refs_4_.refs_1_.refs_2_, bf16[8,2,512,128]{3,2,1,0:T(8,128)(2,1)S(1)} %get-tuple-element.29.refs_5_.refs_2_.refs_3_, f32[128,512]{1,0:T(8,128)S(1)} %accumulate.4.refs_3_), custom_call_target="tpu_custom_call" | custom-call | flops 201326592 | bytes 1441792 | tf_op jit(solution)/shard_map/accumulate/pallas_call | solution.py:205
  19.5 0.4 %collective-permute-done.6.refs_1_ = bf16[2,96,512]{2,1,0:T(8,128)(2,1)S(1)} collective-permute-done((bf16[2,96,512]{2,1,0:T(8,128)(2,1)S(1)}, bf16[2,96,512]{2,1,0:T(8,128)(2,1)S(1)}, u32[]{:S(2)}, u32[]{:S(2)}) %collective-permute-start.6) | collective-permute-done | bytes 196640 | tf_op jit(solution)/shard_map/ppermute | solution.py:363
  19.9 0.5 %accumulate.7 = bf16[3,2,2,32,128]{4,3,2,1,0:T(8,128)(2,1)S(1)} custom-call(bf16[2,96,512]{2,1,0:T(8,128)(2,1)S(1)} %collective-permute-done.5.refs_0_, bf16[2,96,512]{2,1,0:T(8,128)(2,1)S(1)} %collective-permute-done.6.refs_1_, bf16[8,2,512,128]{3,2,1,0:T(8,128)(2,1)S(1)} %get-tuple-element.28.refs_4_.refs_1_.refs_2_, ...), custom_call_target="tpu_custom_call" | custom-call | flops 201326592 | bytes 1441792 | tf_op jit(solution)/shard_map/accumulate/pallas_call | solution.py:205
  20.4 1.9 %collective-permute-start.10 = (bf16[2,2,32,128]{3,2,1,0:T(8,128)(2,1)S(1)}, bf16[2,2,32,128]{3,2,1,0:T(8,128)(2,1)S(1)}, u32[]{:S(2)}, u32[]{:S(2)}) collective-permute-start(bf16[2,2,32,128]{3,2,1,0:T(8,128)(2,1)S(1)} %get-tuple-element.41), channel_id=1, source_target_pairs={{0,1},{1,2},{2,3},{3,0},{4,5},{5,6},{6,7},{7,4},{8,9},{9,10},{10,1... | collective-permute-start | bytes 98312 | tf_op jit(solution)/shard_map/ppermute | solution.py:402
  22.3 2.6 %collective-permute-start.8 = (bf16[2,2,32,128]{3,2,1,0:T(8,128)(2,1)S(1)}, bf16[2,2,32,128]{3,2,1,0:T(8,128)(2,1)S(1)}, u32[]{:S(2)}, u32[]{:S(2)}) collective-permute-start(bf16[2,2,32,128]{3,2,1,0:T(8,128)(2,1)S(1)} %get-tuple-element.43), channel_id=1, source_target_pairs={{0,2},{1,3},{2,0},{3,1},{4,6},{5,7},{6,4},{7,5},{8,10},{9,11},{10,... | collective-permute-start | bytes 98312 | tf_op jit(solution)/shard_map/ppermute | solution.py:402
  24.8 1.4 %collective-permute-start.9 = (bf16[2,2,32,128]{3,2,1,0:T(8,128)(2,1)S(1)}, bf16[2,2,32,128]{3,2,1,0:T(8,128)(2,1)S(1)}, u32[]{:S(2)}, u32[]{:S(2)}) collective-permute-start(bf16[2,2,32,128]{3,2,1,0:T(8,128)(2,1)S(1)} %get-tuple-element.42), channel_id=1, source_target_pairs={{0,3},{1,0},{2,1},{3,2},{4,7},{5,4},{6,5},{7,6},{8,11},{9,8},{10,9... | collective-permute-start | bytes 98312 | tf_op jit(solution)/shard_map/ppermute | solution.py:402
  26.2 0.8 %accumulate.5 = bf16[1,2,2,32,128]{4,3,2,1,0:T(8,128)(2,1)S(1)} custom-call(bf16[8,32,512]{2,1,0:T(8,128)(2,1)S(1)} %collective-permute-done.4.refs_0_, bf16[8,2,512,128]{3,2,1,0:T(8,128)(2,1)S(1)} %get-tuple-element.28.refs_4_.refs_1_.refs_2_, bf16[8,2,512,128]{3,2,1,0:T(8,128)(2,1)S(1)} %get-tuple-element.29.refs_5_.refs_2_.refs_3_, ...), custom_call_target="tpu_custom_call" | custom-call | flops 134217728 | bytes 2359296 | tf_op jit(solution)/shard_map/accumulate/pallas_call | solution.py:205
  27.0 0.2 collective-permute-done.8.refs_1_
  27.2 1.5 %collective-permute-done.9.refs_2_ = bf16[2,2,32,128]{3,2,1,0:T(8,128)(2,1)S(1)} collective-permute-done((bf16[2,2,32,128]{3,2,1,0:T(8,128)(2,1)S(1)}, bf16[2,2,32,128]{3,2,1,0:T(8,128)(2,1)S(1)}, u32[]{:S(2)}, u32[]{:S(2)}) %collective-permute-start.9) | collective-permute-done | bytes 32800 | tf_op jit(solution)/shard_map/ppermute | solution.py:402
  28.9 1.3 %transform_first.1 = (bf16[4,16,128,256]{3,2,1,0:T(8,128)(2,1)}, bf16[2,8,128,256]{3,2,1,0:T(8,128)(2,1)S(1)}) custom-call(bf16[256,256]{1,0:T(8,128)(2,1)S(1)} %get-tuple-element.26.table_ref, bf16[4,2,32,128]{3,2,1,0:T(8,128)(2,1)S(1)} %get-tuple-element.38.given), custom_call_target="tpu_custom_call" | custom-call | tf_op jit(solution)/shard_map/transform_first/pallas_call | solution.py:298
  30.1 1.7 %transform_rest.1 = bf16[4,16,128,256]{3,2,1,0:T(8,128)(2,1)} custom-call(bf16[256,256]{1,0:T(8,128)(2,1)S(1)} %get-tuple-element.26.table_ref, bf16[4,2,32,128]{3,2,1,0:T(8,128)(2,1)S(1)} %collective-permute-done.11.given, bf16[2,8,128,256]{3,2,1,0:T(8,128)(2,1)S(1)} %get-tuple-element.39.rest_ref, ...), custom_call_target="tpu_custom_call", output_to_operand_aliasing={{}: (3, {})} | custom-call | tf_op jit(solution)/shard_map/transform_rest/pallas_call | solution.py:341
  (15 shorter events, 0.2 us)
Async XLA Ops:
  0.0 15.7 %collective-permute-start.2 = (bf16[1,2,4096,128]{3,2,1,0:T(8,128)(2,1)}, bf16[1,2,4096,128]{3,2,1,0:T(8,128)(2,1)S(1)}, u32[]{:S(2)}, u32[]{:S(2)}) collective-permute-start(bf16[1,2,4096,128]{3,2,1,0:T(8,128)(2,1)} %data_ref.3), channel_id=1, source_target_pairs={{0,4},{4,0},{8,12},{12,8},{16,20},{20,16},{24,28},{28,24},{1,5},{5... | collective-permute-start | bytes 6291464 | tf_op jit(solution)/shard_map/ppermute | solution.py:363
  1.8 3.1 %collective-permute-start = (bf16[2,128,512]{2,1,0:T(8,128)(2,1)S(1)}, bf16[2,128,512]{2,1,0:T(8,128)(2,1)S(1)}, u32[]{:S(2)}, u32[]{:S(2)}) collective-permute-start(bf16[2,128,512]{2,1,0:T(8,128)(2,1)S(1)} %get-tuple-element.23), channel_id=1, source_target_pairs={{0,4},{4,0},{8,12},{12,8},{16,20},{20,16},{24,28},{28,24},{1,5},{5... | collective-permute-start | bytes 786440 | tf_op jit(solution)/shard_map/ppermute | solution.py:363
  2.0 7.3 %collective-permute-start.3 = (bf16[2,128,512]{2,1,0:T(8,128)(2,1)S(1)}, bf16[2,128,512]{2,1,0:T(8,128)(2,1)S(1)}, u32[]{:S(2)}, u32[]{:S(2)}) collective-permute-start(bf16[2,128,512]{2,1,0:T(8,128)(2,1)S(1)} %get-tuple-element.35.refs_0_), channel_id=1, source_target_pairs={{0,16},{4,12},{8,24},{12,4},{16,0},{20,28},{24,8},{28,20},{1,17},{... | collective-permute-start | bytes 786440 | tf_op jit(solution)/shard_map/ppermute | solution.py:363
  4.9 7.2 %collective-permute-start.1 = (bf16[2,128,512]{2,1,0:T(8,128)(2,1)S(1)}, bf16[2,128,512]{2,1,0:T(8,128)(2,1)S(1)}, u32[]{:S(2)}, u32[]{:S(2)}) collective-permute-start(bf16[2,128,512]{2,1,0:T(8,128)(2,1)S(1)} %collective-permute-done.refs_1_), channel_id=1, source_target_pairs={{0,16},{4,12},{8,24},{12,4},{16,0},{20,28},{24,8},{28,20},{1,17},{... | collective-permute-start | bytes 786440 | tf_op jit(solution)/shard_map/ppermute | solution.py:363
  7.7 11.3 %collective-permute-start.7 = (bf16[4,96,512]{2,1,0:T(8,128)(2,1)S(1)}, bf16[4,96,512]{2,1,0:T(8,128)(2,1)S(1)}, u32[]{:S(2)}, u32[]{:S(2)}) collective-permute-start(bf16[4,96,512]{2,1,0:T(8,128)(2,1)S(1)} %join_rows.3), channel_id=1, source_target_pairs={{0,8},{4,20},{8,0},{12,28},{16,24},{20,4},{24,16},{28,12},{1,9},{5... | collective-permute-start | bytes 1179656 | tf_op jit(solution)/shard_map/ppermute | solution.py:363
  9.3 10.2 %collective-permute-start.5 = (bf16[2,96,512]{2,1,0:T(8,128)(2,1)S(1)}, bf16[2,96,512]{2,1,0:T(8,128)(2,1)S(1)}, u32[]{:S(2)}, u32[]{:S(2)}) collective-permute-start(bf16[2,96,512]{2,1,0:T(8,128)(2,1)S(1)} %slice.20), channel_id=1, source_target_pairs={{0,8},{4,20},{8,0},{12,28},{16,24},{20,4},{24,16},{28,12},{1,9},{5... | collective-permute-start | bytes 589832 | tf_op jit(solution)/shard_map/ppermute | solution.py:363
  12.1 7.8 %collective-permute-start.6 = (bf16[2,96,512]{2,1,0:T(8,128)(2,1)S(1)}, bf16[2,96,512]{2,1,0:T(8,128)(2,1)S(1)}, u32[]{:S(2)}, u32[]{:S(2)}) collective-permute-start(bf16[2,96,512]{2,1,0:T(8,128)(2,1)S(1)} %slice.21), channel_id=1, source_target_pairs={{0,8},{4,20},{8,0},{12,28},{16,24},{20,4},{24,16},{28,12},{1,9},{5... | collective-permute-start | bytes 589832 | tf_op jit(solution)/shard_map/ppermute | solution.py:363
  18.9 7.3 %collective-permute-start.4 = (bf16[8,32,512]{2,1,0:T(8,128)(2,1)S(1)}, bf16[8,32,512]{2,1,0:T(8,128)(2,1)S(1)}, u32[]{:S(2)}, u32[]{:S(2)}) collective-permute-start(bf16[8,32,512]{2,1,0:T(8,128)(2,1)S(1)} %join_rows.2), channel_id=1, source_target_pairs={{0,8},{4,20},{8,0},{12,28},{16,24},{20,4},{24,16},{28,12},{1,9},{5... | collective-permute-start | bytes 786440 | tf_op jit(solution)/shard_map/ppermute | solution.py:363
  20.4 6.6 %collective-permute-start.10 = (bf16[2,2,32,128]{3,2,1,0:T(8,128)(2,1)S(1)}, bf16[2,2,32,128]{3,2,1,0:T(8,128)(2,1)S(1)}, u32[]{:S(2)}, u32[]{:S(2)}) collective-permute-start(bf16[2,2,32,128]{3,2,1,0:T(8,128)(2,1)S(1)} %get-tuple-element.41), channel_id=1, source_target_pairs={{0,1},{1,2},{2,3},{3,0},{4,5},{5,6},{6,7},{7,4},{8,9},{9,10},{10,1... | collective-permute-start | bytes 98312 | tf_op jit(solution)/shard_map/ppermute | solution.py:402
  22.3 5.0 %collective-permute-start.8 = (bf16[2,2,32,128]{3,2,1,0:T(8,128)(2,1)S(1)}, bf16[2,2,32,128]{3,2,1,0:T(8,128)(2,1)S(1)}, u32[]{:S(2)}, u32[]{:S(2)}) collective-permute-start(bf16[2,2,32,128]{3,2,1,0:T(8,128)(2,1)S(1)} %get-tuple-element.43), channel_id=1, source_target_pairs={{0,2},{1,3},{2,0},{3,1},{4,6},{5,7},{6,4},{7,5},{8,10},{9,11},{10,... | collective-permute-start | bytes 98312 | tf_op jit(solution)/shard_map/ppermute | solution.py:402
  24.8 3.9 %collective-permute-start.9 = (bf16[2,2,32,128]{3,2,1,0:T(8,128)(2,1)S(1)}, bf16[2,2,32,128]{3,2,1,0:T(8,128)(2,1)S(1)}, u32[]{:S(2)}, u32[]{:S(2)}) collective-permute-start(bf16[2,2,32,128]{3,2,1,0:T(8,128)(2,1)S(1)} %get-tuple-element.42), channel_id=1, source_target_pairs={{0,3},{1,0},{2,1},{3,2},{4,7},{5,4},{6,5},{7,6},{8,11},{9,8},{10,9... | collective-permute-start | bytes 98312 | tf_op jit(solution)/shard_map/ppermute | solution.py:402
  28.8 1.3 %collective-permute-start.11 = (bf16[4,2,32,128]{3,2,1,0:T(8,128)(2,1)S(1)}, bf16[4,2,32,128]{3,2,1,0:T(8,128)(2,1)S(1)}, u32[]{:S(2)}, u32[]{:S(2)}) collective-permute-start(bf16[4,2,32,128]{3,2,1,0:T(8,128)(2,1)S(1)} %get-tuple-element.37), channel_id=1, source_target_pairs={{0,4},{4,0},{8,12},{12,8},{16,20},{20,16},{24,28},{28,24},{1,5},{5... | collective-permute-start | bytes 196616 | tf_op jit(solution)/shard_map/ppermute | solution.py:363

commit v11 on v9

--- a/solution.py
+++ b/solution.py
@@ -11,7 +11,7 @@
 
 NT = 256
 UNIT = 16
-EACH = 4
+EACH = 2
 FIRST = 1
 VMEM = pl.BlockSpec(memory_space=pltpu.VMEM)
 ANY = pl.BlockSpec(memory_space=pl.ANY)

time: 32.1 us -> 32.1 us (level)
  no operation moved by 1% of the time
where the time goes in v11:
time: 32.1 us; the launch traced here: 31.9 us
  starting transfers between devices  19.4 us (60%)
  Pallas kernels  9.58 us (30%)
  waiting for transfers between devices  2.72 us (8%)
    ppermute x9, starting transfers between devices, over(): lax.ppermute(value, 'src', [(i, i ^ flips[i % 2]) for i in range(ns)])  13.6 us
    ppermute x3, starting transfers between devices, body(): lax.ppermute(ready[step], 'freq', [(i, (i + shift) % nf) for i in range(n...  5.82 us
    pallas_call x2, Pallas kernels, pick_blocks(): pl.pallas_call(kernel, out_shape=[shape, shape, jax.ShapeDtypeStruct(tabl...  2.65 us
    pallas_call x4, Pallas kernels, accumulate(): pl.pallas_call(kernel, out_shape=jax.ShapeDtypeStruct((steps, 2, two, siz...  2.48 us
    pallas_call x1, Pallas kernels, transform_rest(): pl.pallas_call(kernel, out_shape=jax.ShapeDtypeStruct(out.shape, jnp.bflo...  1.75 us
    ppermute x3, waiting for transfers between devices, body(): lax.ppermute(ready[step], 'freq', [(i, (i + shift) % nf) for i in range(n...  1.74 us
    pallas_call x1, Pallas kernels, order_rows(): pl.pallas_call(kernel, out_shape=[shape, shape], in_specs=[ANY, ANY], out...  1.38 us
    pallas_call x1, Pallas kernels, transform_first(): pl.pallas_call(kernel, out_shape=[jax.ShapeDtypeStruct((quarter // UNIT,...  1.25 us
  transfers between devices with their start and end apart: 12, of which 4 were waited for; matrix products, arithmetic and copies ran while one was open for 0% of the time, Pallas kernels for 25%

profile of v11, /device:TPU:0, one launch (start us, length us, event | category | flops | bytes accessed | tf_op | source)
XLA Modules:
  0.0 31.9 jit_solution(3938193462434808953)
XLA Ops:
  0.0 0.5 %collective-permute-start.2 = (bf16[1,2,4096,128]{3,2,1,0:T(8,128)(2,1)}, bf16[1,2,4096,128]{3,2,1,0:T(8,128)(2,1)S(1)}, u32[]{:S(2)}, u32[]{:S(2)}) collective-permute-start(bf16[1,2,4096,128]{3,2,1,0:T(8,128)(2,1)} %data_ref.3), channel_id=1, source_target_pairs={{0,4},{4,0},{8,12},{12,8},{16,20},{20,16},{24,28},{28,24},{1,5},{5... | collective-permute-start | bytes 6291464 | tf_op jit(solution)/shard_map/ppermute | solution.py:363
  0.5 1.4 %order_rows.1 = (bf16[2,128,512]{2,1,0:T(8,128)(2,1)S(1)}, bf16[2,128,512]{2,1,0:T(8,128)(2,1)S(1)}) custom-call(s32[1,256]{1,0:T(1,128)} %bitcast.10, bf16[1,1,2,256,512]{4,3,2,1,0:T(8,128)(2,1)} %g_ref.1), custom_call_target="tpu_custom_call" | custom-call | tf_op jit(solution)/shard_map/order_rows/pallas_call | solution.py:54
  1.8 0.1 collective-permute-start
  2.0 3.0 %collective-permute-start.3 = (bf16[2,128,512]{2,1,0:T(8,128)(2,1)S(1)}, bf16[2,128,512]{2,1,0:T(8,128)(2,1)S(1)}, u32[]{:S(2)}, u32[]{:S(2)}) collective-permute-start(bf16[2,128,512]{2,1,0:T(8,128)(2,1)S(1)} %get-tuple-element.35.refs_0_), channel_id=1, source_target_pairs={{0,16},{4,12},{8,24},{12,4},{16,0},{20,28},{24,8},{28,20},{1,17},{... | collective-permute-start | bytes 786440 | tf_op jit(solution)/shard_map/ppermute | solution.py:363
  4.9 2.6 %collective-permute-start.1 = (bf16[2,128,512]{2,1,0:T(8,128)(2,1)S(1)}, bf16[2,128,512]{2,1,0:T(8,128)(2,1)S(1)}, u32[]{:S(2)}, u32[]{:S(2)}) collective-permute-start(bf16[2,128,512]{2,1,0:T(8,128)(2,1)S(1)} %collective-permute-done.refs_1_), channel_id=1, source_target_pairs={{0,16},{4,12},{8,24},{12,4},{16,0},{20,28},{24,8},{28,20},{1,17},{... | collective-permute-start | bytes 786440 | tf_op jit(solution)/shard_map/ppermute | solution.py:363
  7.5 0.2 pick_blocks.2.refs_2_
  7.7 1.6 %collective-permute-start.7 = (bf16[4,96,512]{2,1,0:T(8,128)(2,1)S(1)}, bf16[4,96,512]{2,1,0:T(8,128)(2,1)S(1)}, u32[]{:S(2)}, u32[]{:S(2)}) collective-permute-start(bf16[4,96,512]{2,1,0:T(8,128)(2,1)S(1)} %join_rows.3), channel_id=1, source_target_pairs={{0,8},{4,20},{8,0},{12,28},{16,24},{20,4},{24,16},{28,12},{1,9},{5... | collective-permute-start | bytes 1179656 | tf_op jit(solution)/shard_map/ppermute | solution.py:363
  9.3 2.1 %collective-permute-start.5 = (bf16[2,96,512]{2,1,0:T(8,128)(2,1)S(1)}, bf16[2,96,512]{2,1,0:T(8,128)(2,1)S(1)}, u32[]{:S(2)}, u32[]{:S(2)}) collective-permute-start(bf16[2,96,512]{2,1,0:T(8,128)(2,1)S(1)} %slice.20), channel_id=1, source_target_pairs={{0,8},{4,20},{8,0},{12,28},{16,24},{20,4},{24,16},{28,12},{1,9},{5... | collective-permute-start | bytes 589832 | tf_op jit(solution)/shard_map/ppermute | solution.py:363
  11.4 0.8 %collective-permute-done.1.refs_3_ = bf16[2,128,512]{2,1,0:T(8,128)(2,1)S(1)} collective-permute-done((bf16[2,128,512]{2,1,0:T(8,128)(2,1)S(1)}, bf16[2,128,512]{2,1,0:T(8,128)(2,1)S(1)}, u32[]{:S(2)}, u32[]{:S(2)}) %collective-permute-start.1) | collective-permute-done | bytes 262176 | tf_op jit(solution)/shard_map/ppermute | solution.py:363
  12.1 3.7 %collective-permute-start.6 = (bf16[2,96,512]{2,1,0:T(8,128)(2,1)S(1)}, bf16[2,96,512]{2,1,0:T(8,128)(2,1)S(1)}, u32[]{:S(2)}, u32[]{:S(2)}) collective-permute-start(bf16[2,96,512]{2,1,0:T(8,128)(2,1)S(1)} %slice.21), channel_id=1, source_target_pairs={{0,8},{4,20},{8,0},{12,28},{16,24},{20,4},{24,16},{28,12},{1,9},{5... | collective-permute-start | bytes 589832 | tf_op jit(solution)/shard_map/ppermute | solution.py:363
  15.8 2.5 %pick_blocks.3 = (bf16[8,2,512,128]{3,2,1,0:T(8,128)(2,1)S(1)}, bf16[8,2,512,128]{3,2,1,0:T(8,128)(2,1)S(1)}, bf16[256,256]{1,0:T(8,128)(2,1)S(1)}) custom-call(s32[8]{0:T(128)} %block_ref.1, bf16[1,2,4096,128]{3,2,1,0:T(8,128)(2,1)} %data_ref.3, bf16[1,2,4096,128]{3,2,1,0:T(8,128)(2,1)S(1)} %collective-permute-done.2.refs_0_, ...), custom_call_target="tpu_custom_call", output_to_operand_aliasing={{0}: (4, {})} | custom-call | tf_op jit(solution)/shard_map/pick_blocks/pallas_call | solution.py:159
  18.3 0.7 %accumulate.4.refs_3_ = f32[128,512]{1,0:T(8,128)S(1)} custom-call(bf16[2,128,512]{2,1,0:T(8,128)(2,1)S(1)} %get-tuple-element.35.refs_0_, bf16[2,128,512]{2,1,0:T(8,128)(2,1)S(1)} %collective-permute-done.refs_1_, bf16[2,128,512]{2,1,0:T(8,128)(2,1)S(1)} %collective-permute-done.3.refs_2_, bf16[2,128,512]{2,1,0:T(8,128)(2,1)S(1)} %collective-permute-done.1.refs_3_, ...), custom_call_target="tpu_custom_call" | custom-call | flops 536870912 | bytes 3145728 | tf_op jit(solution)/shard_map/accumulate/pallas_call | solution.py:205
  19.1 0.1 collective-permute-start.4
  19.2 0.5 %accumulate.6.refs_4_ = f32[96,512]{1,0:T(8,128)S(1)} custom-call(bf16[4,96,512]{2,1,0:T(8,128)(2,1)S(1)} %collective-permute-done.7.refs_0_, bf16[8,2,512,128]{3,2,1,0:T(8,128)(2,1)S(1)} %get-tuple-element.28.refs_4_.refs_1_.refs_2_, bf16[8,2,512,128]{3,2,1,0:T(8,128)(2,1)S(1)} %get-tuple-element.29.refs_5_.refs_2_.refs_3_, f32[128,512]{1,0:T(8,128)S(1)} %accumulate.4.refs_3_), custom_call_target="tpu_custom_call" | custom-call | flops 201326592 | bytes 1441792 | tf_op jit(solution)/shard_map/accumulate/pallas_call | solution.py:205
  19.7 0.2 collective-permute-done.6.refs_1_
  19.9 0.5 %accumulate.7 = bf16[3,2,2,32,128]{4,3,2,1,0:T(8,128)(2,1)S(1)} custom-call(bf16[2,96,512]{2,1,0:T(8,128)(2,1)S(1)} %collective-permute-done.5.refs_0_, bf16[2,96,512]{2,1,0:T(8,128)(2,1)S(1)} %collective-permute-done.6.refs_1_, bf16[8,2,512,128]{3,2,1,0:T(8,128)(2,1)S(1)} %get-tuple-element.28.refs_4_.refs_1_.refs_2_, ...), custom_call_target="tpu_custom_call" | custom-call | flops 201326592 | bytes 1441792 | tf_op jit(solution)/shard_map/accumulate/pallas_call | solution.py:205
  20.4 1.9 %collective-permute-start.10 = (bf16[2,2,32,128]{3,2,1,0:T(8,128)(2,1)S(1)}, bf16[2,2,32,128]{3,2,1,0:T(8,128)(2,1)S(1)}, u32[]{:S(2)}, u32[]{:S(2)}) collective-permute-start(bf16[2,2,32,128]{3,2,1,0:T(8,128)(2,1)S(1)} %get-tuple-element.41), channel_id=1, source_target_pairs={{0,1},{1,2},{2,3},{3,0},{4,5},{5,6},{6,7},{7,4},{8,9},{9,10},{10,1... | collective-permute-start | bytes 98312 | tf_op jit(solution)/shard_map/ppermute | solution.py:402
  22.3 2.6 %collective-permute-start.8 = (bf16[2,2,32,128]{3,2,1,0:T(8,128)(2,1)S(1)}, bf16[2,2,32,128]{3,2,1,0:T(8,128)(2,1)S(1)}, u32[]{:S(2)}, u32[]{:S(2)}) collective-permute-start(bf16[2,2,32,128]{3,2,1,0:T(8,128)(2,1)S(1)} %get-tuple-element.43), channel_id=1, source_target_pairs={{0,2},{1,3},{2,0},{3,1},{4,6},{5,7},{6,4},{7,5},{8,10},{9,11},{10,... | collective-permute-start | bytes 98312 | tf_op jit(solution)/shard_map/ppermute | solution.py:402
  24.8 1.4 %collective-permute-start.9 = (bf16[2,2,32,128]{3,2,1,0:T(8,128)(2,1)S(1)}, bf16[2,2,32,128]{3,2,1,0:T(8,128)(2,1)S(1)}, u32[]{:S(2)}, u32[]{:S(2)}) collective-permute-start(bf16[2,2,32,128]{3,2,1,0:T(8,128)(2,1)S(1)} %get-tuple-element.42), channel_id=1, source_target_pairs={{0,3},{1,0},{2,1},{3,2},{4,7},{5,4},{6,5},{7,6},{8,11},{9,8},{10,9... | collective-permute-start | bytes 98312 | tf_op jit(solution)/shard_map/ppermute | solution.py:402
  26.2 0.8 %accumulate.5 = bf16[1,2,2,32,128]{4,3,2,1,0:T(8,128)(2,1)S(1)} custom-call(bf16[8,32,512]{2,1,0:T(8,128)(2,1)S(1)} %collective-permute-done.4.refs_0_, bf16[8,2,512,128]{3,2,1,0:T(8,128)(2,1)S(1)} %get-tuple-element.28.refs_4_.refs_1_.refs_2_, bf16[8,2,512,128]{3,2,1,0:T(8,128)(2,1)S(1)} %get-tuple-element.29.refs_5_.refs_2_.refs_3_, ...), custom_call_target="tpu_custom_call" | custom-call | flops 134217728 | bytes 2359296 | tf_op jit(solution)/shard_map/accumulate/pallas_call | solution.py:205
  27.0 0.2 collective-permute-done.8.refs_1_
  27.2 1.5 %collective-permute-done.9.refs_2_ = bf16[2,2,32,128]{3,2,1,0:T(8,128)(2,1)S(1)} collective-permute-done((bf16[2,2,32,128]{3,2,1,0:T(8,128)(2,1)S(1)}, bf16[2,2,32,128]{3,2,1,0:T(8,128)(2,1)S(1)}, u32[]{:S(2)}, u32[]{:S(2)}) %collective-permute-start.9) | collective-permute-done | bytes 32800 | tf_op jit(solution)/shard_map/ppermute | solution.py:402
  28.9 1.3 %transform_first.1 = (bf16[4,16,128,256]{3,2,1,0:T(8,128)(2,1)}, bf16[2,8,128,256]{3,2,1,0:T(8,128)(2,1)S(1)}) custom-call(bf16[256,256]{1,0:T(8,128)(2,1)S(1)} %get-tuple-element.26.table_ref, bf16[4,2,32,128]{3,2,1,0:T(8,128)(2,1)S(1)} %get-tuple-element.38.given), custom_call_target="tpu_custom_call" | custom-call | tf_op jit(solution)/shard_map/transform_first/pallas_call | solution.py:298
  30.1 1.7 %transform_rest.1 = bf16[4,16,128,256]{3,2,1,0:T(8,128)(2,1)} custom-call(bf16[256,256]{1,0:T(8,128)(2,1)S(1)} %get-tuple-element.26.table_ref, bf16[4,2,32,128]{3,2,1,0:T(8,128)(2,1)S(1)} %collective-permute-done.11.given, bf16[2,8,128,256]{3,2,1,0:T(8,128)(2,1)S(1)} %get-tuple-element.39.rest_ref, ...), custom_call_target="tpu_custom_call", output_to_operand_aliasing={{}: (3, {})} | custom-call | tf_op jit(solution)/shard_map/transform_rest/pallas_call | solution.py:341
  (15 shorter events, 0.2 us)
Async XLA Ops:
  0.0 15.8 %collective-permute-start.2 = (bf16[1,2,4096,128]{3,2,1,0:T(8,128)(2,1)}, bf16[1,2,4096,128]{3,2,1,0:T(8,128)(2,1)S(1)}, u32[]{:S(2)}, u32[]{:S(2)}) collective-permute-start(bf16[1,2,4096,128]{3,2,1,0:T(8,128)(2,1)} %data_ref.3), channel_id=1, source_target_pairs={{0,4},{4,0},{8,12},{12,8},{16,20},{20,16},{24,28},{28,24},{1,5},{5... | collective-permute-start | bytes 6291464 | tf_op jit(solution)/shard_map/ppermute | solution.py:363
  1.8 3.1 %collective-permute-start = (bf16[2,128,512]{2,1,0:T(8,128)(2,1)S(1)}, bf16[2,128,512]{2,1,0:T(8,128)(2,1)S(1)}, u32[]{:S(2)}, u32[]{:S(2)}) collective-permute-start(bf16[2,128,512]{2,1,0:T(8,128)(2,1)S(1)} %get-tuple-element.23), channel_id=1, source_target_pairs={{0,4},{4,0},{8,12},{12,8},{16,20},{20,16},{24,28},{28,24},{1,5},{5... | collective-permute-start | bytes 786440 | tf_op jit(solution)/shard_map/ppermute | solution.py:363
  2.0 7.3 %collective-permute-start.3 = (bf16[2,128,512]{2,1,0:T(8,128)(2,1)S(1)}, bf16[2,128,512]{2,1,0:T(8,128)(2,1)S(1)}, u32[]{:S(2)}, u32[]{:S(2)}) collective-permute-start(bf16[2,128,512]{2,1,0:T(8,128)(2,1)S(1)} %get-tuple-element.35.refs_0_), channel_id=1, source_target_pairs={{0,16},{4,12},{8,24},{12,4},{16,0},{20,28},{24,8},{28,20},{1,17},{... | collective-permute-start | bytes 786440 | tf_op jit(solution)/shard_map/ppermute | solution.py:363
  4.9 7.2 %collective-permute-start.1 = (bf16[2,128,512]{2,1,0:T(8,128)(2,1)S(1)}, bf16[2,128,512]{2,1,0:T(8,128)(2,1)S(1)}, u32[]{:S(2)}, u32[]{:S(2)}) collective-permute-start(bf16[2,128,512]{2,1,0:T(8,128)(2,1)S(1)} %collective-permute-done.refs_1_), channel_id=1, source_target_pairs={{0,16},{4,12},{8,24},{12,4},{16,0},{20,28},{24,8},{28,20},{1,17},{... | collective-permute-start | bytes 786440 | tf_op jit(solution)/shard_map/ppermute | solution.py:363
  7.7 11.5 %collective-permute-start.7 = (bf16[4,96,512]{2,1,0:T(8,128)(2,1)S(1)}, bf16[4,96,512]{2,1,0:T(8,128)(2,1)S(1)}, u32[]{:S(2)}, u32[]{:S(2)}) collective-permute-start(bf16[4,96,512]{2,1,0:T(8,128)(2,1)S(1)} %join_rows.3), channel_id=1, source_target_pairs={{0,8},{4,20},{8,0},{12,28},{16,24},{20,4},{24,16},{28,12},{1,9},{5... | collective-permute-start | bytes 1179656 | tf_op jit(solution)/shard_map/ppermute | solution.py:363
  9.3 10.4 %collective-permute-start.5 = (bf16[2,96,512]{2,1,0:T(8,128)(2,1)S(1)}, bf16[2,96,512]{2,1,0:T(8,128)(2,1)S(1)}, u32[]{:S(2)}, u32[]{:S(2)}) collective-permute-start(bf16[2,96,512]{2,1,0:T(8,128)(2,1)S(1)} %slice.20), channel_id=1, source_target_pairs={{0,8},{4,20},{8,0},{12,28},{16,24},{20,4},{24,16},{28,12},{1,9},{5... | collective-permute-start | bytes 589832 | tf_op jit(solution)/shard_map/ppermute | solution.py:363
  12.1 7.8 %collective-permute-start.6 = (bf16[2,96,512]{2,1,0:T(8,128)(2,1)S(1)}, bf16[2,96,512]{2,1,0:T(8,128)(2,1)S(1)}, u32[]{:S(2)}, u32[]{:S(2)}) collective-permute-start(bf16[2,96,512]{2,1,0:T(8,128)(2,1)S(1)} %slice.21), channel_id=1, source_target_pairs={{0,8},{4,20},{8,0},{12,28},{16,24},{20,4},{24,16},{28,12},{1,9},{5... | collective-permute-start | bytes 589832 | tf_op jit(solution)/shard_map/ppermute | solution.py:363
  19.1 7.1 %collective-permute-start.4 = (bf16[8,32,512]{2,1,0:T(8,128)(2,1)S(1)}, bf16[8,32,512]{2,1,0:T(8,128)(2,1)S(1)}, u32[]{:S(2)}, u32[]{:S(2)}) collective-permute-start(bf16[8,32,512]{2,1,0:T(8,128)(2,1)S(1)} %join_rows.2), channel_id=1, source_target_pairs={{0,8},{4,20},{8,0},{12,28},{16,24},{20,4},{24,16},{28,12},{1,9},{5... | collective-permute-start | bytes 786440 | tf_op jit(solution)/shard_map/ppermute | solution.py:363
  20.4 6.6 %collective-permute-start.10 = (bf16[2,2,32,128]{3,2,1,0:T(8,128)(2,1)S(1)}, bf16[2,2,32,128]{3,2,1,0:T(8,128)(2,1)S(1)}, u32[]{:S(2)}, u32[]{:S(2)}) collective-permute-start(bf16[2,2,32,128]{3,2,1,0:T(8,128)(2,1)S(1)} %get-tuple-element.41), channel_id=1, source_target_pairs={{0,1},{1,2},{2,3},{3,0},{4,5},{5,6},{6,7},{7,4},{8,9},{9,10},{10,1... | collective-permute-start | bytes 98312 | tf_op jit(solution)/shard_map/ppermute | solution.py:402
  22.3 5.0 %collective-permute-start.8 = (bf16[2,2,32,128]{3,2,1,0:T(8,128)(2,1)S(1)}, bf16[2,2,32,128]{3,2,1,0:T(8,128)(2,1)S(1)}, u32[]{:S(2)}, u32[]{:S(2)}) collective-permute-start(bf16[2,2,32,128]{3,2,1,0:T(8,128)(2,1)S(1)} %get-tuple-element.43), channel_id=1, source_target_pairs={{0,2},{1,3},{2,0},{3,1},{4,6},{5,7},{6,4},{7,5},{8,10},{9,11},{10,... | collective-permute-start | bytes 98312 | tf_op jit(solution)/shard_map/ppermute | solution.py:402
  24.8 3.9 %collective-permute-start.9 = (bf16[2,2,32,128]{3,2,1,0:T(8,128)(2,1)S(1)}, bf16[2,2,32,128]{3,2,1,0:T(8,128)(2,1)S(1)}, u32[]{:S(2)}, u32[]{:S(2)}) collective-permute-start(bf16[2,2,32,128]{3,2,1,0:T(8,128)(2,1)S(1)} %get-tuple-element.42), channel_id=1, source_target_pairs={{0,3},{1,0},{2,1},{3,2},{4,7},{5,4},{6,5},{7,6},{8,11},{9,8},{10,9... | collective-permute-start | bytes 98312 | tf_op jit(solution)/shard_map/ppermute | solution.py:402
  28.8 1.3 %collective-permute-start.11 = (bf16[4,2,32,128]{3,2,1,0:T(8,128)(2,1)S(1)}, bf16[4,2,32,128]{3,2,1,0:T(8,128)(2,1)S(1)}, u32[]{:S(2)}, u32[]{:S(2)}) collective-permute-start(bf16[4,2,32,128]{3,2,1,0:T(8,128)(2,1)S(1)} %get-tuple-element.37), channel_id=1, source_target_pairs={{0,4},{4,0},{8,12},{12,8},{16,20},{20,16},{24,28},{28,24},{1,5},{5... | collective-permute-start | bytes 196616 | tf_op jit(solution)/shard_map/ppermute | solution.py:363
